TPU v7x, 128 devices: a whole 4x4x4 slice. The times are simulated.
128 devices in a mesh: seq: 32 (over z, y, core), tp: 4 (over x).
Axes of the slice: x: 4, y: 4, z: 4, core: 2. Of those that a mesh axis runs over, the one named last changes fastest.
Arguments:
- queries: bfloat16 [1024, 4096], P('seq', 'tp'), may hold values from -40 to 40
- cache_keys: bfloat16 [131072, 512], P('seq', 'tp'), may hold values from -4 to 4
- cache_values: bfloat16 [131072, 512], P('seq', 'tp'), may hold values from -16 to 16
- new_keys: bfloat16 [1024, 512], P('seq', 'tp'), may hold values from -4 to 4
- new_values: bfloat16 [1024, 512], P('seq', 'tp'), may hold values from -16 to 16
- reach: int32 [1024], replicated, may hold values from 65537 to 131072, as said below
- norm_gain: float32 [4096], replicated, may hold values from 0.1 to 1.9
- gate_weights: float32 [1024, 2], P('seq'), may hold values from 0.1 to 1
- expert_ids: int32 [1024, 2], P('seq'), may hold values from 0 to 7, all different within a row; in each aligned block of 32 rows (0 to 31, 32 to 63, ...) at most 16 rows name the same one
- w_up: bfloat16 [32, 4096, 3072], P('seq', None, 'tp'), may hold values from -0.09375 to 0.09375
- w_down: bfloat16 [32, 3072, 4096], P('seq', 'tp'), may hold values from -0.0546875 to 0.0546875
Outputs:
- attended: bfloat16 [1024, 4096], P('seq', 'tp')
- expert_mix: bfloat16 [1024, 4096], P('seq', 'tp')
Inputs may be any that keep to these rules, and one draw needn't show every extreme that they name: `expert_ids`: each row names two different experts. In each aligned block of 32 rows (the rows of one index of seq) no expert is named by more than 16 rows, and in every draw some expert is named by exactly 16 rows of some block. `reach`: the first query token's entry is 131072; the last token's entry is the least allowed.
All inputs are finite; a program needn't handle non-finite values.
Results may differ from a plain program's by a relative error of at most 0.017.
Values may be sent and summed in bfloat16 or wider, within the bound.
No kernel may reach another device: no remote copies, remote signals or barrier semaphores. Data moves between devices by JAX's collectives and lax.ppermute only.
A program may use at most 128 MiB of HBM per device.

v0:
```python
import math

import jax
import jax.numpy as jnp
from jax import lax
from jax.sharding import PartitionSpec as P

HD = 128
E = 8
CAP = 16


EPSILON = 1e-05
MASKED = -1e30


def block_attention(
    query_block, row_start, reach_block, all_keys, all_values, cache_first, window_first, ctx_count
):
    block_tokens = query_block.shape[0]
    kv_local = all_keys.shape[1] // HD
    head_ratio = query_block.shape[1] // (kv_local * HD)
    key_count = all_keys.shape[0]
    token_ids = row_start + jnp.arange(block_tokens, dtype=jnp.int32)
    cache_pos = cache_first + jnp.arange(ctx_count, dtype=jnp.int32)
    window_pos = window_first + jnp.arange(key_count - ctx_count, dtype=jnp.int32)
    visible = jnp.concatenate(
        [cache_pos[None, :] < reach_block[:, None], window_pos[None, :] <= token_ids[:, None]],
        axis=1,
    )
    allowed = visible[:, None, :]
    head_queries = query_block.reshape(block_tokens * head_ratio, HD)
    scores = lax.dot_general(
        head_queries, all_keys, (((1,), (1,)), ((), ())), preferred_element_type=jnp.float32
    )
    scores = scores.reshape(block_tokens, head_ratio, key_count) * HD ** (-0.5)
    masked = jnp.where(allowed, scores, MASKED)
    top_score = jnp.max(masked, axis=-1)
    weights = jnp.where(allowed, jnp.exp(masked - top_score[..., None]), 0.0)
    weight_sum = jnp.sum(weights, axis=-1)
    head_out = jnp.dot(
        weights.astype(jnp.bfloat16).reshape(block_tokens * head_ratio, key_count),
        all_values,
        preferred_element_type=jnp.float32,
    )
    head_out = (
        head_out.reshape(block_tokens, head_ratio, HD) / jnp.maximum(weight_sum, 1.0)[..., None]
    )
    out_list = [head_out.reshape(block_tokens, head_ratio * HD)]
    top_list = [top_score]
    sum_list = [weight_sum]
    return (
        jnp.concatenate(out_list, axis=1),
        jnp.concatenate(top_list, axis=1),
        jnp.concatenate(sum_list, axis=1),
    )


def per_device(
    queries,
    cache_keys,
    cache_values,
    new_keys,
    new_values,
    reach,
    norm_gain,
    gate_weights,
    expert_ids,
    w_up,
    w_down,
):
    seq_count = lax.axis_size("seq")
    seq_index = lax.axis_index("seq")
    tok_count = queries.shape[0]
    ctx_count = cache_keys.shape[0]
    every_query = lax.all_gather(queries, "seq", axis=0, tiled=True)
    all_keys = jnp.concatenate([cache_keys, new_keys], axis=0)
    all_values = jnp.concatenate([cache_values, new_values], axis=0)
    token_total = every_query.shape[0]
    block_size = math.gcd(token_total, 128)
    block_count = token_total // block_size

    def one_block(block_index):
        row_start = block_index * block_size
        query_block = lax.dynamic_slice_in_dim(every_query, row_start, block_size, 0)
        reach_block = lax.dynamic_slice_in_dim(reach, row_start, block_size, 0)
        return block_attention(
            query_block,
            row_start,
            reach_block,
            all_keys,
            all_values,
            seq_index * ctx_count,
            seq_index * tok_count,
            ctx_count,
        )

    block_outs, block_tops, block_sums = lax.map(
        one_block, jnp.arange(block_count, dtype=jnp.int32)
    )
    out_width = block_outs.shape[-1]
    heads_local = block_tops.shape[-1]
    arrived_outs, arrived_tops, arrived_sums = (
        lax.all_to_all(
            block_outs.reshape(token_total, out_width),
            "seq",
            split_axis=0,
            concat_axis=0,
            tiled=True,
        ),
        lax.all_to_all(
            block_tops.reshape(token_total, heads_local),
            "seq",
            split_axis=0,
            concat_axis=0,
            tiled=True,
        ),
        lax.all_to_all(
            block_sums.reshape(token_total, heads_local),
            "seq",
            split_axis=0,
            concat_axis=0,
            tiled=True,
        ),
    )
    from_blocks = arrived_outs.reshape(seq_count, tok_count, heads_local, HD)
    tops_in = arrived_tops.reshape(seq_count, tok_count, heads_local)
    sums_in = arrived_sums.reshape(seq_count, tok_count, heads_local)
    overall = jnp.max(tops_in, axis=0)
    shares = sums_in * jnp.exp(tops_in - overall[None])
    combined = jnp.sum(shares[..., None] * from_blocks, axis=0) / jnp.sum(shares, axis=0)[..., None]
    attended = combined.reshape(tok_count, heads_local * HD).astype(jnp.bfloat16)
    group_size = seq_count // E
    capacity = CAP
    flat_ids = expert_ids.reshape(-1)
    onehot = (flat_ids[:, None] == jnp.arange(E, dtype=jnp.int32)[None, :]).astype(jnp.int32)
    rank_within = jnp.sum((jnp.cumsum(onehot, axis=0) - 1) * onehot, axis=1)
    slot_index = (flat_ids * capacity + rank_within).reshape(tok_count, 2)
    slot_ids = jnp.arange(E * capacity, dtype=jnp.int32)
    placing = (
        (slot_ids[:, None] == slot_index[None, :, 0])
        | (slot_ids[:, None] == slot_index[None, :, 1])
    ).astype(jnp.bfloat16)
    full_rows = lax.all_gather(attended, "tp", axis=1, tiled=True)
    as_float = full_rows.astype(jnp.float32)
    inverse = lax.rsqrt(jnp.mean(as_float * as_float, axis=1) + EPSILON)
    normed = (as_float * inverse[:, None] * norm_gain[None, :]).astype(jnp.bfloat16)
    outgoing = (
        jnp.dot(placing, normed, preferred_element_type=jnp.float32)
        .astype(jnp.bfloat16)
        .reshape(E, capacity, normed.shape[1])
    )
    outgoing = jnp.repeat(outgoing, group_size, axis=0)
    arrived = lax.all_to_all(outgoing, "seq", split_axis=0, concat_axis=0, tiled=True)
    upward = jnp.dot(
        arrived.reshape(-1, arrived.shape[-1]), w_up[0], preferred_element_type=jnp.float32
    )
    hidden = jax.nn.silu(upward).astype(jnp.bfloat16)
    downward = jnp.dot(hidden, w_down[0], preferred_element_type=jnp.float32)
    column_share = lax.psum_scatter(
        downward.astype(jnp.bfloat16), "tp", scatter_dimension=1, tiled=True
    ).astype(jnp.float32)
    returned = lax.all_to_all(
        column_share.reshape(seq_count, capacity, column_share.shape[1]).astype(jnp.bfloat16),
        "seq",
        split_axis=0,
        concat_axis=0,
        tiled=True,
    ).astype(jnp.float32)
    out_cols = returned.shape[-1]
    per_slot = jnp.sum(returned.reshape(E, group_size, capacity, out_cols), axis=1).reshape(
        E * capacity, out_cols
    )
    picked = jnp.take(per_slot, slot_index.reshape(-1), axis=0).reshape(tok_count, 2, out_cols)
    expert_mix = jnp.sum(picked * gate_weights[:, :, None], axis=1).astype(jnp.bfloat16)
    return (attended, expert_mix)


def solution(mesh):
    placed = (
        P("seq", "tp"),
        P("seq", "tp"),
        P("seq", "tp"),
        P("seq", "tp"),
        P("seq", "tp"),
        P(),
        P(),
        P("seq", None),
        P("seq", None),
        P("seq", None, "tp"),
        P("seq", "tp", None),
    )
    return jax.shard_map(
        per_device,
        mesh=mesh,
        in_specs=placed,
        out_specs=(P("seq", "tp"), P("seq", "tp")),
        check_vma=False,
    )
```

profile of v0, /device:TPU:1, one launch (start us, length us, event | category | flops | bytes accessed | tf_op | source)
XLA Modules:
  0.0 444.0 jit_solution(6822602163104977946)
XLA Ops:
  9.7 48.3 %all-gather.2.cloned.1.call-done = bf16[1024,1024]{1,0:T(8,128)(2,1)} async-done(((bf16[32,1024]{1,0:T(8,128)(2,1)}), bf16[1024,1024]{1,0:T(8,128)(2,1)}) %all-gather.2.cloned.1.call-update) | async-done | bytes 2097168 | tf_op jit(solution)/shard_map/all_gather | solution.py:76
  57.9 135.8 %while.16 = (s32[]{:T(128)}, f32[8,128,1024]{2,1,0:T(8,128)}, f32[8,128,8]{1,0,2:T(8,128)S(1)}, f32[8,128,8]{1,0,2:T(8,128)S(1)}, s32[]{:T(128)}, /*index=5*/s32...) while((s32[]{:T(128)}, f32[8,128,1024]{2,1,0:T(8,128)}, ...), condition=%wide.region_3.4_spmd, body=%wide.region_0.3_spmd.sunk | while | flops 2220403712 | bytes 60022240 | solution.py:98
  59.9 1.8 broadcast_compare_fusion.5
  63.1 2.5 fusion.56
  65.6 4.1 fusion.57
  69.7 4.1 fusion.58
  76.9 1.8 broadcast_compare_fusion.5
  80.1 2.5 fusion.56
  82.6 4.1 fusion.57
  86.7 4.1 fusion.58
  94.0 1.8 broadcast_compare_fusion.5
  97.1 2.5 fusion.56
  99.6 4.1 fusion.57
  103.7 4.1 fusion.58
  110.9 1.8 broadcast_compare_fusion.5
  114.1 2.5 fusion.56
  116.6 4.1 fusion.57
  120.6 4.1 fusion.58
  127.9 1.8 broadcast_compare_fusion.5
  131.0 2.5 fusion.56
  133.5 4.1 fusion.57
  137.6 4.1 fusion.58
  144.9 1.8 broadcast_compare_fusion.5
  148.0 2.5 fusion.56
  150.5 4.1 fusion.57
  154.6 4.1 fusion.58
  161.8 1.8 broadcast_compare_fusion.5
  165.0 2.5 fusion.56
  167.5 4.1 fusion.57
  171.5 4.1 fusion.58
  178.8 1.8 broadcast_compare_fusion.5
  181.9 2.5 fusion.56
  184.4 4.1 fusion.57
  188.5 4.1 fusion.58
  194.6 5.2 %all-to-all-start.1 = ((f32[32,1,256]{2,1,0:T(1,128)}), f32[32,1,256]{2,1,0:T(1,128)S(1)}, u32[]{:S(2)}, u32[]{:S(2)}) async-start(f32[32,1,256]{2,1,0:T(1,128)} %reshape.169), calls=%async_computation.1 | async-start | bytes 65536 | tf_op jit(solution)/shard_map/all_to_all | solution.py:111
  200.2 7.0 %all-to-all-done.1 = f32[32,1,256]{2,1,0:T(1,128)S(1)} async-done(((f32[32,1,256]{2,1,0:T(1,128)}), f32[32,1,256]{2,1,0:T(1,128)S(1)}, u32[]{:S(2)}, u32[]{:S(2)}) %all-to-all-start.1) | async-done | bytes 32800 | tf_op jit(solution)/shard_map/all_to_all | solution.py:111
  207.1 10.7 %all_to_all.37 = f32[32,1,256]{2,1,0:T(1,128)S(1)} all-to-all(f32[32,1,256]{2,1,0:T(1,128)S(1)} %reshape.167), channel_id=1, replica_groups=mesh['seq'=32,'tp'=4] {'seq'}, dimensions={0} | all-to-all | bytes 65536 | tf_op jit(solution)/shard_map/all_to_all | solution.py:118
  217.9 5.0 %all-to-all-start.2 = ((f32[32,32,1024]{2,1,0:T(8,128)}), f32[32,32,1024]{2,1,0:T(8,128)}, u32[]{:S(2)}, u32[]{:S(2)}) async-start(f32[32,32,1024]{2,1,0:T(8,128)} %bitcast.95), calls=%async_computation.2 | async-start | bytes 8388608 | tf_op jit(solution)/shard_map/all_to_all | solution.py:104
  226.3 2.6 mul.96
  228.9 4.9 %mul.97 = f32[32,32,1024]{2,1,0:T(8,128)} reshape(f32[32,32,8,128]{3,2,1,0:T(8,128)} %mul.96) | data formatting | bytes 8388608 | tf_op jit(solution)/shard_map/mul | solution.py:131
  233.9 39.3 %all-to-all-done.2 = f32[32,32,1024]{2,1,0:T(8,128)} async-done(((f32[32,32,1024]{2,1,0:T(8,128)}), f32[32,32,1024]{2,1,0:T(8,128)}, u32[]{:S(2)}, u32[]{:S(2)}) %all-to-all-start.2) | async-done | bytes 4194336 | tf_op jit(solution)/shard_map/all_to_all | solution.py:104
  273.2 4.1 multiply_reduce_fusion
  277.5 9.7 %all_gather.7 = bf16[32,4096]{1,0:T(8,128)(2,1)S(1)} all-gather(bf16[32,1024]{1,0:T(8,128)(2,1)S(1)} %fusion.34), channel_id=1, replica_groups=mesh['seq'=32,'tp'=4] {'tp'}, dimensions={1}, use_global_device_ids=true | all-gather | bytes 327680 | tf_op jit(solution)/shard_map/all_gather | solution.py:144
  288.4 60.8 %all_to_all.38 = bf16[32,16,4096]{2,1,0:T(8,128)(2,1)} all-to-all(bf16[32,16,4096]{2,1,0:T(8,128)(2,1)S(1)} %bitcast.91), channel_id=1, replica_groups=mesh['seq'=32,'tp'=4] {'seq'}, dimensions={0} | all-to-all | bytes 8388608 | tf_op jit(solution)/shard_map/all_to_all | solution.py:154
  349.1 16.6 %fusion.21 = bf16[512,4096]{1,0:T(8,128)(2,1)} fusion(bf16[1,768,4096]{2,1,0:T(8,128)(2,1)} %param.23, bf16[512,4096]{1,0:T(8,128)(2,1)} %bitcast.96, bf16[1,4096,768]{2,1,0:T(8,128)(2,1)} %param.22), kind=kOutput, calls=%fused_computation.28 | convolution fusion | flops 6446514176 | bytes 20971520 | tf_op jit(solution)/shard_map/dot_general | solution.py:159
  365.7 44.5 %reduce-scatter.2.cloned.1.call-done = bf16[512,1024]{1,0:T(8,128)(2,1)} async-done(((bf16[512,4096]{1,0:T(8,128)(2,1)}), bf16[512,1024]{1,0:T(8,128)(2,1)}) %reduce-scatter.2.cloned.1.call-update) | async-done | bytes 1048592 | tf_op jit(solution)/shard_map/reduce_scatter | solution.py:160
  410.2 7.6 %all-to-all-start.4 = ((bf16[32,16,1024]{2,1,0:T(8,128)(2,1)}), bf16[32,16,1024]{2,1,0:T(8,128)(2,1)S(1)}, u32[]{:S(2)}, u32[]{:S(2)}) async-start(bf16[32,16,1024]{2,1,0:T(8,128)(2,1)} %bitcast.97), calls=%async_computation.5 | async-start | bytes 2097152 | tf_op jit(solution)/shard_map/all_to_all | solution.py:163
  418.3 16.8 %all-to-all-done.4 = bf16[32,16,1024]{2,1,0:T(8,128)(2,1)S(1)} async-done(((bf16[32,16,1024]{2,1,0:T(8,128)(2,1)}), bf16[32,16,1024]{2,1,0:T(8,128)(2,1)S(1)}, u32[]{:S(2)}, u32[]{:S(2)}) %all-to-all-start.4) | async-done | bytes 1048608 | tf_op jit(solution)/shard_map/all_to_all | solution.py:163
  (170 shorter events, 41.1 us)
Async XLA Ops:
  7.2 50.8 %all-gather.2.cloned.1.call-start = ((), (), s32[]{:S(2)}) async-start(), calls=%async_computation.6 | async-start | bytes 2162688 | tf_op jit(solution)/shard_map/all_gather | solution.py:76
  194.6 12.5 %all-to-all-start.1 = ((f32[32,1,256]{2,1,0:T(1,128)}), f32[32,1,256]{2,1,0:T(1,128)S(1)}, u32[]{:S(2)}, u32[]{:S(2)}) async-start(f32[32,1,256]{2,1,0:T(1,128)} %reshape.169), calls=%async_computation.1 | async-start | bytes 65536 | tf_op jit(solution)/shard_map/all_to_all | solution.py:111
  217.9 5.2 %copy-start.2 = (s32[32,2]{0,1:T(2,128)S(1)}, s32[32,2]{0,1:T(2,128)}, u32[]{:S(2)}) copy-start(s32[32,2]{0,1:T(2,128)} %param.21) | copy-start | bytes 772
  217.9 55.3 %all-to-all-start.2 = ((f32[32,32,1024]{2,1,0:T(8,128)}), f32[32,32,1024]{2,1,0:T(8,128)}, u32[]{:S(2)}, u32[]{:S(2)}) async-start(f32[32,32,1024]{2,1,0:T(8,128)} %bitcast.95), calls=%async_computation.2 | async-start | bytes 8388608 | tf_op jit(solution)/shard_map/all_to_all | solution.py:104
  222.8 187.4 %reduce-scatter.2.cloned.1.call-start = ((), (), s32[]{:S(2)}) async-start(), calls=%async_computation.7 | async-start | bytes 5242880 | tf_op jit(solution)/shard_map/reduce_scatter | solution.py:160
  233.9 53.5 %copy-start.1 = (f32[4096]{0:T(1024)S(1)}, f32[4096]{0:T(1024)}, u32[]{:S(2)}) copy-start(f32[4096]{0:T(1024)} %param.19) | copy-start | bytes 49156
  277.5 71.6 %copy-start = (bf16[32,1024]{1,0:T(8,128)(2,1)}, bf16[32,1024]{1,0:T(8,128)(2,1)S(1)}, u32[]{:S(2)}) copy-start(bf16[32,1024]{1,0:T(8,128)(2,1)S(1)} %fusion.34) | copy-start | bytes 196612
  365.7 52.5 %copy-start.3 = (f32[32,2]{0,1:T(2,128)S(1)}, f32[32,2]{0,1:T(2,128)}, u32[]{:S(2)}) copy-start(f32[32,2]{0,1:T(2,128)} %param.20) | copy-start | bytes 772
  410.2 24.8 %all-to-all-start.4 = ((bf16[32,16,1024]{2,1,0:T(8,128)(2,1)}), bf16[32,16,1024]{2,1,0:T(8,128)(2,1)S(1)}, u32[]{:S(2)}, u32[]{:S(2)}) async-start(bf16[32,16,1024]{2,1,0:T(8,128)(2,1)} %bitcast.97), calls=%async_computation.5 | async-start | bytes 2097152 | tf_op jit(solution)/shard_map/all_to_all | solution.py:163
Sparse Core Ops, SparseCore 0:
  10.3 47.6 all-gather.1
  365.8 44.3 reduce-scatter.1
where the time goes:
time: 445 us; the launch traced here: 444 us
  waiting for transfers between devices  157 us (35%)
  blocking collectives  81.2 us (18%)
  matrix products  69.6 us (16%)
  other arithmetic  57.6 us (13%)
  local copies, waits for them, and re-layouts  41 us (9%)
  starting transfers between devices  18.1 us (4%)
  between operations  14.3 us (3%)
  loops' own time  5.72 us (1%)
    all_to_all x1, blocking collectives, per_device(): lax.all_to_all(outgoing, 'seq', split_axis=0, concat_axis=0, tiled=True)  60.8 us
    all_gather x1, waiting for transfers between devices, per_device(): every_query = lax.all_gather(queries, 'seq', axis=0, tiled=True)  48.3 us
    reduce_scatter x1, waiting for transfers between devices, per_device(): lax.psum_scatter(downward.astype(jnp.bfloat16), 'tp', scatter_dimension=1...  44.5 us
    all_to_all x1, waiting for transfers between devices, per_device(): lax.all_to_all(block_outs.reshape(token_total, out_width), 'seq', split_a...  39.3 us
    dot_general x8, matrix products, block_attention(): jnp.dot(weights.astype(jnp.bfloat16).reshape(block_tokens * head_ratio, k...  32.8 us
    reduce_sum x8, other arithmetic, block_attention(): weight_sum = jnp.sum(weights, axis=-1)  32.5 us
    dot_general x8, matrix products, block_attention(): lax.dot_general(head_queries, all_keys, (((1,), (1,)), ((), ())), preferr...  19.8 us
    all_to_all x1, waiting for transfers between devices, per_device(): lax.all_to_all(column_share.reshape(seq_count, capacity, column_share.sha...  16.8 us
  transfers between devices with their start and end apart: 5, of which 5 were waited for; matrix products, arithmetic and copies ran while one was open for 3% of the time, Pallas kernels for 0%

commit v1 on v0

v1 whole, which is shorter than its diff:
```python
import functools
import math

import jax
import jax.numpy as jnp
from jax import lax
from jax.experimental import pallas as pl
from jax.experimental.pallas import tpu as pltpu
from jax.sharding import PartitionSpec as P

HD = 128
E = 8
CAP = 16
EPSILON = 1e-05
NEG = -1e30
FLOOR = -1e20
BF = jnp.bfloat16
F32 = jnp.float32
SCALE = HD**-0.5 * math.log2(math.e)
MIB = 1024 * 1024
VM = pl.BlockSpec(memory_space=pltpu.VMEM)
SM = pl.BlockSpec(memory_space=pltpu.SMEM)

def attn_kernel(pos_ref, lim_ref, q_ref, k0_ref, k1_ref, v0_ref, v1_ref, nk_ref, nv_ref, o_ref, kk, vv, s_scr, m_scr, l_scr, *, R, CH, W):
    T=q_ref.shape[0]; KEYS=k0_ref.shape[0]; NT=(T//R)*8; NCH=KEYS//CH; WIN=2*KEYS
    for half,kr,vr in ((0,k0_ref,v0_ref),(1,k1_ref,v1_ref)):
        k=kr[...]; v=vr[...]
        kk[pl.ds(half*KEYS,KEYS),:]=jnp.concatenate([k,k],axis=1)
        vv[pl.ds(half*KEYS,KEYS),:]=jnp.concatenate([v,jnp.ones_like(v)],axis=1)
    nk=nk_ref[...]; nv=nv_ref[...]
    zero=jnp.zeros((128-2*W,HD),BF)
    nk=jnp.concatenate([nk,zero],axis=0); nv=jnp.concatenate([nv,zero],axis=0)
    kk[pl.ds(WIN,128),:]=jnp.concatenate([nk,nk],axis=1)
    vv[pl.ds(WIN,128),:]=jnp.concatenate([nv,jnp.ones_like(nv)],axis=1)
    l_scr[...]=jnp.zeros_like(l_scr)
    def tile(i):
        h=lax.rem(i,8); tb=lax.div(i,8)
        return pl.multiple_of(tb*R,R), pl.multiple_of(h*HD,HD), h
    def load_q(i):
        r,c,_=tile(i)
        qf=q_ref[pl.ds(r,R),pl.ds(c,HD)].astype(F32)*SCALE
        hi=qf.astype(BF); lo=(qf-hi.astype(F32)).astype(BF)
        return jnp.concatenate([hi,lo],axis=1)
    def dotk(qq,k):
        return lax.dot_general(qq,k,(((1,),(1,)),((),())),preferred_element_type=F32)
    def window_scores(i, qq):
        r,_,_=tile(i)
        s=dotk(qq,kk[pl.ds(WIN,128),:])
        lane=lax.broadcasted_iota(jnp.int32,(R,128),1)
        row=lax.broadcasted_iota(jnp.int32,(R,128),0)+r
        tok=lax.div(row,W)*(2*W)+lax.rem(row,W)+pos_ref[4]*W
        key=jnp.where(lane<W,lane+pos_ref[2],lane-W+pos_ref[3])
        return jnp.where((lane<2*W)&(key<=tok),s,NEG)
    def step(i, slot, do_qk, do_pv):
        if do_qk:
            qq=load_q(i+1)
            r1,_,_=tile(i+1)
            lim=lim_ref[pl.ds(r1,R),:]
            lane0=lax.broadcasted_iota(jnp.int32,(R,128),1)
            mx=jnp.full((R,128),FLOOR,F32)
            sw=window_scores(i+1,qq)
            s_scr[1-slot,:,pl.ds(WIN,128)]=sw
            mx=jnp.maximum(mx,sw)
        if do_pv:
            m=m_scr[...]
            p=jnp.exp2(s_scr[slot,:,pl.ds(WIN,128)]-m)
            acc=jnp.dot(p.astype(BF),vv[pl.ds(WIN,128),:],preferred_element_type=F32)
        for half in range(2):
            if do_qk:
                limh=lim-pos_ref[half]
            for j in range(NCH):
                ks=half*KEYS+j*CH
                if do_qk:
                    s=dotk(qq,kk[pl.ds(ks,CH),:])
                    for c in range(CH//128):
                        sc=jnp.where(lane0+(j*CH+c*128)<limh,s[:,c*128:(c+1)*128],NEG)
                        s_scr[1-slot,:,pl.ds(ks+c*128,128)]=sc
                        mx=jnp.maximum(mx,sc)
                if do_pv:
                    p=jnp.concatenate([jnp.exp2(s_scr[slot,:,pl.ds(ks+c*128,128)]-m).astype(BF) for c in range(CH//128)],axis=1)
                    acc=acc+jnp.dot(p,vv[pl.ds(ks,CH),:],preferred_element_type=F32)
        if do_pv:
            r,c,h=tile(i)
            l=acc[:,HD:]
            o_ref[pl.ds(r,R),pl.ds(c,HD)]=(acc[:,:HD]/jnp.maximum(l,1.0)).astype(BF)
            L=jnp.where(l>0,m+jnp.log2(jnp.maximum(l,1e-30)),NEG)
            lane=lax.broadcasted_iota(jnp.int32,(R,128),1)
            l_scr[pl.ds(r,R),:]=jnp.where(lax.rem(lane,8)==h,L,l_scr[pl.ds(r,R),:])
        if do_qk:
            m_scr[...]=jnp.broadcast_to(jnp.max(mx,axis=1,keepdims=True),(R,128))
    step(jnp.int32(-1),1,True,False)
    def two(t,_):
        step(2*t,0,True,True)
        step(2*t+1,1,True,True)
        return 0
    lax.fori_loop(0,NT//2-1,two,0)
    step(jnp.int32(NT-2),0,True,True)
    step(jnp.int32(NT-1),1,False,True)
    L=l_scr[...]
    hi=L.astype(BF); mid=(L-hi.astype(F32)).astype(BF); lo=(L-hi.astype(F32)-mid.astype(F32)).astype(BF)
    lane=lax.broadcasted_iota(jnp.int32,L.shape,1)
    o_ref[:,pl.ds(8*HD,128)]=jnp.where(lane<8,hi.astype(F32),jnp.where(lane<16,mid.astype(F32),jnp.where(lane<24,lo.astype(F32),0.0))).astype(BF)

def attention(pos, lim, q, k0, k1, v0, v1, nk, nv, R=256, CH=512):
    T=q.shape[0]; KEYS=k0.shape[0]; W=nk.shape[0]//2
    return pl.pallas_call(
        functools.partial(attn_kernel,R=R,CH=CH,W=W),
        out_shape=jax.ShapeDtypeStruct((T,9*HD),BF),
        in_specs=[SM]+[VM]*8,
        out_specs=VM,
        scratch_shapes=[pltpu.VMEM((2*KEYS+128,2*HD),BF),pltpu.VMEM((2*KEYS+128,2*HD),BF),
            pltpu.VMEM((2,R,2*KEYS+128),F32),pltpu.VMEM((R,128),F32),pltpu.VMEM((T,128),F32)],
        compiler_params=pltpu.CompilerParams(vmem_limit_bytes=60*MIB),
        cost_estimate=pl.CostEstimate(flops=4*T*8*2*KEYS*HD*2,bytes_accessed=8*1024*1024,transcendentals=T*8*2*KEYS),
    )(pos,lim,q,k0,k1,v0,v1,nk,nv)


def home_kernel(recv_ref, ids_ref, att_ref, msg_ref):
    blocks, tok, _ = recv_ref.shape
    heads = att_ref.shape[1] // HD
    logs = []
    for s in range(blocks):
        tail = recv_ref[s, :, pl.ds(heads * HD, 128)].astype(F32)
        logs.append(tail + pltpu.roll(tail, 120, 1) + pltpu.roll(tail, 112, 1))
    top = functools.reduce(jnp.maximum, logs)
    shares = [jnp.exp2(x - top) for x in logs]
    inverse = 1.0 / functools.reduce(jnp.add, shares)
    shares = [x * inverse for x in shares]
    for h in range(heads):
        total = jnp.zeros((tok, HD), F32)
        for s in range(blocks):
            total = total + shares[s][:, h : h + 1] * recv_ref[s, :, pl.ds(h * HD, HD)].astype(F32)
        att_ref[:, pl.ds(h * HD, HD)] = total.astype(BF)
    slot = lax.broadcasted_iota(jnp.int32, (E * CAP, tok), 0)
    expert = lax.div(slot, CAP)
    member = (ids_ref[0:1, :] == expert) | (ids_ref[1:2, :] == expert)
    earlier = lax.broadcasted_iota(jnp.int32, (tok, tok), 0) < lax.broadcasted_iota(jnp.int32, (tok, tok), 1)
    rank = jnp.dot(
        jnp.where(member, 1.0, 0.0).astype(BF), jnp.where(earlier, 1.0, 0.0).astype(BF), preferred_element_type=F32
    )
    placing = member & (rank == lax.rem(slot, CAP).astype(F32))
    rows = jnp.dot(
        jnp.where(placing, 1.0, 0.0).astype(BF), att_ref[...], preferred_element_type=F32
    ).astype(BF)
    half = rows.shape[1] // 2
    for e in range(E):
        for c in range(2):
            part = rows[e * CAP : (e + 1) * CAP, c * half : (c + 1) * half]
            for y in range(msg_ref.shape[1]):
                for x in range(msg_ref.shape[3]):
                    msg_ref[e, y, c, x] = part


def home(recv, ids_t, tp):
    tok, width = recv.shape[1], recv.shape[2] - 128
    return pl.pallas_call(
        home_kernel,
        out_shape=(
            jax.ShapeDtypeStruct((tok, width), BF),
            jax.ShapeDtypeStruct((E, 2, 2, tp, CAP, width // 2), BF),
        ),
        in_specs=[VM, VM],
        out_specs=(VM, VM),
        compiler_params=pltpu.CompilerParams(vmem_limit_bytes=32 * MIB),
    )(recv, ids_t)


def up_kernel(core_ref, own_ref, other_ref, gain_ref, up_ref, down_ref, hidden_ref, send_ref):
    seqs, tp, cap, half = own_ref.shape
    rows = seqs * cap
    core = core_ref[0]

    def part(ref, x):
        return ref[:, x].reshape(rows, half).astype(F32)

    square = jnp.zeros((rows, 128), F32)
    for ref in (own_ref, other_ref):
        for x in range(tp):
            a = part(ref, x)
            a = a * a
            for c in range(half // 128):
                square = square + a[:, c * 128 : (c + 1) * 128]
    mean = jnp.sum(square, axis=1, keepdims=True) / (2 * tp * half)
    inverse = lax.rsqrt(mean + EPSILON)
    total = jnp.zeros((rows, up_ref.shape[1]), F32)
    for ref, side in ((own_ref, core), (other_ref, 1 - core)):
        for x in range(tp):
            first = pl.multiple_of(x * 2 * half + side * half, half)
            normed = (part(ref, x) * inverse * gain_ref[:, pl.ds(first, half)]).astype(BF)
            total = total + jnp.dot(normed, up_ref[pl.ds(first, half), :], preferred_element_type=F32)
    hidden = (total / (1.0 + jnp.exp(-total))).astype(BF)
    hidden_ref[...] = hidden
    for x in range(tp):
        first = pl.multiple_of(x * 2 * half + (1 - core) * half, half)
        out = jnp.dot(hidden, down_ref[:, pl.ds(first, half)], preferred_element_type=F32)
        send_ref[:, x] = out.astype(BF).reshape(seqs, cap, half)


def up_project(core, own, other, gain, w_up, w_down):
    rows = own.shape[0] * own.shape[2]
    return pl.pallas_call(
        up_kernel,
        out_shape=(
            jax.ShapeDtypeStruct((rows, w_up.shape[1]), BF),
            jax.ShapeDtypeStruct(own.shape, BF),
        ),
        in_specs=[SM] + [VM] * 5,
        out_specs=(VM, VM),
        compiler_params=pltpu.CompilerParams(vmem_limit_bytes=48 * MIB),
    )(core, own, other, gain, w_up, w_down)


def down_kernel(core_ref, hidden_ref, down_ref, partner_ref, out_ref):
    seqs, tp, cap, half = out_ref.shape
    hidden = hidden_ref[...]
    for x in range(tp):
        first = pl.multiple_of(x * 2 * half + core_ref[0] * half, half)
        out = jnp.dot(hidden, down_ref[:, pl.ds(first, half)], preferred_element_type=F32)
        out = out + partner_ref[:, x].reshape(seqs * cap, half).astype(F32)
        out_ref[:, x] = out.astype(BF).reshape(seqs, cap, half)


def down_project(core, hidden, w_down, partner):
    return pl.pallas_call(
        down_kernel,
        out_shape=jax.ShapeDtypeStruct(partner.shape, BF),
        in_specs=[SM] + [VM] * 3,
        out_specs=VM,
        compiler_params=pltpu.CompilerParams(vmem_limit_bytes=40 * MIB),
    )(core, hidden, w_down, partner)


def mix_kernel(recv_ref, ids_ref, gate_ref, out_ref):
    experts, pair, cores, tp, cap, half = recv_ref.shape
    tok = ids_ref.shape[0]
    terms = experts * pair * tp * cap
    lane = lax.broadcasted_iota(jnp.int32, (tok, terms), 1)
    expert = lax.div(lane, pair * tp * cap)
    first, second = ids_ref[:, 0:1] == expert, ids_ref[:, 1:2] == expert
    gate = jnp.where(first, gate_ref[:, 0:1], 0.0) + jnp.where(second, gate_ref[:, 1:2], 0.0)
    earlier = lax.broadcasted_iota(jnp.int32, (tok, tok), 1) < lax.broadcasted_iota(jnp.int32, (tok, tok), 0)
    rank = jnp.dot(
        jnp.where(earlier, 1.0, 0.0).astype(BF), jnp.where(first | second, 1.0, 0.0).astype(BF), preferred_element_type=F32
    )
    gate = jnp.where(rank == lax.rem(lane, cap).astype(F32), gate, 0.0)
    high = gate.astype(BF)
    low = (gate - high.astype(F32)).astype(BF)
    both = jnp.concatenate([high, low], axis=0)
    for c in range(cores):
        values = recv_ref[:, :, c].reshape(terms, half)
        out = jnp.dot(both, values, preferred_element_type=F32)
        out_ref[:, pl.ds(c * half, half)] = (out[:tok] + out[tok:]).astype(BF)


def mix(recv, ids, gates):
    return pl.pallas_call(
        mix_kernel,
        out_shape=jax.ShapeDtypeStruct((ids.shape[0], 2 * recv.shape[5]), BF),
        in_specs=[VM] * 3,
        out_specs=VM,
        compiler_params=pltpu.CompilerParams(vmem_limit_bytes=32 * MIB),
    )(recv, ids, gates)


def per_device(
    queries, cache_keys, cache_values, new_keys, new_values, reach, norm_gain, gate_weights, expert_ids, w_up, w_down
):
    seqs, tp = lax.axis_size("seq"), lax.axis_size("tp")
    seq = lax.axis_index("seq")
    core = lax.rem(seq, 2)
    partner = seq + 1 - 2 * core
    tok, width = queries.shape
    ctx = cache_keys.shape[0]
    chips = seqs // 2
    same_core = [list(range(c, seqs, 2)) for c in range(2)]
    swap = [(i, i ^ 1) for i in range(seqs)]

    def swapped(value):
        return lax.ppermute(value, "seq", swap)

    other_keys, other_values = swapped(cache_keys), swapped(cache_values)
    other_new_keys, other_new_values = swapped(new_keys), swapped(new_values)
    all_queries = lax.all_to_all(
        jnp.broadcast_to(queries[None], (chips, tok, width)),
        "seq", 0, 0, axis_index_groups=same_core, tiled=True,
    ).reshape(chips * tok, width)
    limits = lax.dynamic_index_in_dim(reach.reshape(chips, 2, tok), core, 1, keepdims=False)
    limits = jnp.broadcast_to(limits.reshape(chips * tok, 1), (chips * tok, 128))
    places = jnp.stack([seq * ctx, partner * ctx, seq * tok, partner * tok, core]).astype(jnp.int32)
    outs = attention(
        places, limits, all_queries, cache_keys, other_keys, cache_values, other_values,
        jnp.concatenate([new_keys, other_new_keys], axis=0),
        jnp.concatenate([new_values, other_new_values], axis=0),
    )
    arrived = lax.all_to_all(
        outs.reshape(chips, tok, outs.shape[1]), "seq", 0, 0, axis_index_groups=same_core, tiled=True
    )
    attended, message = home(arrived, expert_ids.T, tp)
    half = width // 2
    rows = lax.all_to_all(
        message.reshape(seqs * tp, CAP, half), ("seq", "tp"), 0, 0, tiled=True
    ).reshape(seqs, tp, CAP, half)
    side = core.astype(jnp.int32).reshape(1)
    hidden, send = up_project(side, rows, swapped(rows), norm_gain.reshape(1, -1), w_up[0], w_down[0])
    result = down_project(side, hidden, w_down[0], swapped(send))
    returned = lax.all_to_all(
        result.reshape(seqs * tp, CAP, half), ("seq", "tp"), 0, 0, tiled=True
    ).reshape(E, 2, 2, tp, CAP, half)
    return attended, mix(returned, expert_ids, gate_weights)


def solution(mesh):
    placed = (
        P("seq", "tp"),
        P("seq", "tp"),
        P("seq", "tp"),
        P("seq", "tp"),
        P("seq", "tp"),
        P(),
        P(),
        P("seq", None),
        P("seq", None),
        P("seq", None, "tp"),
        P("seq", "tp", None),
    )
    return jax.shard_map(
        per_device,
        mesh=mesh,
        in_specs=placed,
        out_specs=(P("seq", "tp"), P("seq", "tp")),
        check_vma=False,
    )
```

time: 445 us -> 201 us (0.45)
  waiting for transfers between devices: 157 us -> 51.7 us
  matrix products: 69.6 us -> 0 us
  Pallas kernels: 0 us -> 64 us
  other arithmetic: 57.6 us -> 1.22 us
  local copies, waits for them, and re-layouts: 41 us -> 7.31 us
  blocking collectives: 81.2 us -> 60 us
  between operations: 14.3 us -> 0.75 us
  loops' own time: 5.72 us -> 0 us
    dot_general x18 -> x0, matrix products: 69.6 us -> none  [the longest x8 32.8 us: block_attention(): jnp.dot(weights.astype(jnp.bfloat16).reshape(block_tokens * head_ratio, k...]
    pallas_call x0 -> x5, Pallas kernels: none -> 64 us  [the longest x1 45.5 us: attention(): pl.pallas_call(functools.partial(attn_kernel, R=R, CH=CH, W=W), out_shape...]
    all_gather x1 -> x0, waiting for transfers between devices: 48.3 us -> none  [per_device(): every_query = lax.all_gather(queries, 'seq', axis=0, tiled=True)]
    reduce_scatter x1 -> x0, waiting for transfers between devices: 44.5 us -> none  [per_device(): lax.psum_scatter(downward.astype(jnp.bfloat16), 'tp', scatter_dimension=1...]
    reduce_sum x14 -> x0, other arithmetic: 38.3 us -> none  [the longest x8 32.5 us: block_attention(): weight_sum = jnp.sum(weights, axis=-1)]
    dynamic_slice x32 -> x1, local copies, waits for them, and re-layouts: 20.2 us -> 0.03 us  [per_device(): lax.dynamic_index_in_dim(reach.reshape(chips, 2, tok), core, 1, keepdims=...]
    all_to_all x3 -> x2, waiting for transfers between devices: 63 us -> 44.2 us  [the longest x1 30.8 us: per_device(): lax.all_to_all(result.reshape(seqs * tp, CAP, half), ('seq', 'tp'), 0, 0,...]
    lt x8 -> x0, other arithmetic: 14.8 us -> none  [block_attention(): cache_pos[None, :] < reach_block[:, None]]
  transfers between devices with their start and end apart: 5 -> 8, of which waited for: 5 -> 4; matrix products, arithmetic and copies ran while one was open for 3% -> 2% of each run, Pallas kernels for 0% -> 0%
where the time goes in v1:
time: 201 us; the launch traced here: 200 us
  Pallas kernels  64 us (32%)
  blocking collectives  60 us (30%)
  waiting for transfers between devices  51.7 us (26%)
  starting transfers between devices  15.1 us (8%)
  local copies, waits for them, and re-layouts  7.31 us (4%)
    pallas_call x1, Pallas kernels, attention(): pl.pallas_call(functools.partial(attn_kernel, R=R, CH=CH, W=W), out_shape...  45.5 us
    all_to_all x1, blocking collectives, per_device(): lax.all_to_all(message.reshape(seqs * tp, CAP, half), ('seq', 'tp'), 0, 0...  38.3 us
    all_to_all x1, waiting for transfers between devices, per_device(): lax.all_to_all(result.reshape(seqs * tp, CAP, half), ('seq', 'tp'), 0, 0,...  30.8 us
    all_to_all x1, blocking collectives, per_device(): lax.all_to_all(outs.reshape(chips, tok, outs.shape[1]), 'seq', 0, 0, axis...  21.6 us
    pallas_call x1, Pallas kernels, up_project(): pl.pallas_call(up_kernel, out_shape=(jax.ShapeDtypeStruct((rows, w_up.sha...  13.9 us
    all_to_all x1, waiting for transfers between devices, per_device(): lax.all_to_all(jnp.broadcast_to(queries[None], (chips, tok, width)), 'seq...  13.4 us
    all_to_all x1, starting transfers between devices, per_device(): lax.all_to_all(jnp.broadcast_to(queries[None], (chips, tok, width)), 'seq...  7.85 us
    ppermute x6, waiting for transfers between devices, swapped(): return lax.ppermute(value, 'seq', swap)  7.58 us
  transfers between devices with their start and end apart: 8, of which 4 were waited for; matrix products, arithmetic and copies ran while one was open for 2% of the time, Pallas kernels for 0%

profile of v1, /device:TPU:1, one launch (start us, length us, event | category | flops | bytes accessed | tf_op | source)
XLA Modules:
  0.0 200.1 jit_solution(16985544883921836348)
XLA Ops:
  0.6 0.0 copy-start.5
  0.6 0.0 copy-start.6
  0.7 0.0 copy-start.7
  0.7 1.5 collective-permute-start
  2.2 0.1 collective-permute-start.1
  2.3 2.0 broadcast_in_dim.15
  4.2 7.9 %all-to-all-start = ((bf16[16,32,1024]{2,1,0:T(8,128)(2,1)}), bf16[16,32,1024]{2,1,0:T(8,128)(2,1)S(1)}, u32[]{:S(2)}, u32[]{:S(2)}) async-start(bf16[16,32,1024]{2,1,0:T(8,128)(2,1)} %broadcast_in_dim.15), calls=%async_computation | async-start | bytes 2097152 | tf_op jit(solution)/shard_map/all_to_all | solution.py:283
  12.1 0.0 copy-done.5
  12.1 0.8 collective-permute-start.2
  12.9 0.0 copy-done.6
  12.9 0.1 collective-permute-start.3
  13.0 0.0 copy-done.7
  13.0 0.1 reshape.33
  13.1 0.1 broadcast_in_dim.6
  13.2 0.6 stack.23.pos_ref
  13.8 0.0 collective-permute-done.2
  13.8 0.6 pad_maximum_fusion.nk_ref
  14.4 0.0 collective-permute-done.3
  14.4 0.6 pad_maximum_fusion.1.nv_ref
  15.0 13.4 %all-to-all-done = bf16[16,32,1024]{2,1,0:T(8,128)(2,1)S(1)} async-done(((bf16[16,32,1024]{2,1,0:T(8,128)(2,1)}), bf16[16,32,1024]{2,1,0:T(8,128)(2,1)S(1)}, u32[]{:S(2)}, u32[]{:S(2)}) %all-to-all-start) | async-done | bytes 1048608 | tf_op jit(solution)/shard_map/all_to_all | solution.py:283
  28.4 0.0 collective-permute-done.k1_ref
  28.4 0.0 collective-permute-done.1.v1_ref
  28.4 0.0 copy-start.10
  28.4 1.0 broadcast_in_dim.14.lim_ref
  29.4 0.1 copy-done.4
  29.4 0.3 copy-done.9
  29.7 0.3 copy-done.10
  30.1 45.5 %shard_map.122 = bf16[512,1152]{1,0:T(8,128)(2,1)} custom-call(s32[5]{0:T(128)} %stack.23.pos_ref, s32[512,128]{1,0:T(8,128)} %broadcast_in_dim.14.lim_ref, bf16[512,1024]{1,0:T(8,128)(2,1)} %bitcast.28, bf16[4096,128]{1,0:T(8,128)(2,1)} %k0_ref.1, bf16[4096,128]{1,0:T(8,128)(2,1)} %copy-done.9, bf16[4096,128]{1,0:T(8,128)(2,1)} %v0_ref.1, ...), custom_call_target="tpu_custom_call" | custom-call | flops 34359738368 | bytes 8388608 | tf_op jit(solution)/shard_map/pallas_call | solution.py:106
  75.6 21.6 %all_to_all.20.recv_ref = bf16[16,32,1152]{2,1,0:T(8,128)(2,1)S(1)} all-to-all(bf16[16,32,1152]{2,1,0:T(8,128)(2,1)} %bitcast.27), channel_id=1, replica_groups={{0,8,16,24,32,40,48,56,64,72,80,88,96,104,112,120},{4,12,20,28,36,44,52..., dimensions={0} | all-to-all | bytes 2359296 | tf_op jit(solution)/shard_map/all_to_all | solution.py:295
  97.2 0.0 copy-done.2
  97.2 1.5 shard_map.123
  98.7 38.3 %all_to_all.21 = bf16[128,16,512]{2,1,0:T(8,128)(2,1)S(1)} all-to-all(bf16[128,16,512]{2,1,0:T(8,128)(2,1)S(1)} %bitcast.23), channel_id=1, replica_groups=mesh['seq'=32,'tp'=4] {'seq','tp'}, dimensions={0} | all-to-all | bytes 4194304 | tf_op jit(solution)/shard_map/all_to_all | solution.py:300
  137.1 0.4 collective-permute-start.4
  137.5 3.8 %collective-permute-done.4.other_ref = bf16[32,4,16,512]{3,2,1,0:T(8,128)(2,1)S(1)} collective-permute-done((bf16[32,4,16,512]{3,2,1,0:T(8,128)(2,1)S(1)}, bf16[32,4,16,512]{3,2,1,0:T(8,128)(2,1)S(1)}, u32[]{:S(2)}, u32[]{:S(2)}) %collective-permute-start.4) | collective-permute-done | bytes 2097184 | tf_op jit(solution)/shard_map/ppermute | solution.py:279
  141.3 1.3 copy-done.3
  142.6 0.0 copy-done.1
  142.6 13.9 %shard_map.124 = (bf16[512,768]{1,0:T(8,128)(2,1)S(1)}, bf16[32,4,16,512]{3,2,1,0:T(8,128)(2,1)S(1)}) custom-call(s32[1]{0:T(128)} %bitcast.4.core_ref, bf16[32,4,16,512]{3,2,1,0:T(8,128)(2,1)S(1)} %bitcast.22, bf16[32,4,16,512]{3,2,1,0:T(8,128)(2,1)} %copy-done.3, f32[1,4096]{1,0:T(1,128)S(1)} %bitcast.24, bf16[4096,768]{1,0:T(8,128)(2,1)} %bitcast.26, ...), custom_call_target="tpu_custom_call" | custom-call | tf_op jit(solution)/shard_map/pallas_call | solution.py:201
  156.5 0.5 collective-permute-start.5
  157.0 3.8 %collective-permute-done.5.partner_ref = bf16[32,4,16,512]{3,2,1,0:T(8,128)(2,1)S(1)} collective-permute-done((bf16[32,4,16,512]{3,2,1,0:T(8,128)(2,1)S(1)}, bf16[32,4,16,512]{3,2,1,0:T(8,128)(2,1)S(1)}, u32[]{:S(2)}, u32[]{:S(2)}) %collective-permute-start.5) | collective-permute-done | bytes 2097184 | tf_op jit(solution)/shard_map/ppermute | solution.py:279
  160.8 0.0 slice-done
  160.8 0.0 slice-done.1
  160.8 1.8 shard_map.125
  162.6 1.3 copy-done
  164.0 3.9 %all-to-all-start.3 = ((bf16[128,16,512]{2,1,0:T(8,128)(2,1)}), bf16[128,16,512]{2,1,0:T(8,128)(2,1)S(1)}, u32[]{:S(2)}, u32[]{:S(2)}) async-start(bf16[128,16,512]{2,1,0:T(8,128)(2,1)} %bitcast.20), calls=%async_computation.3 | async-start | bytes 4194304 | tf_op jit(solution)/shard_map/all_to_all | solution.py:306
  167.9 0.1 copy.13.ids_ref
  168.0 0.1 copy.14.gate_ref
  168.1 30.8 %all-to-all-done.3 = bf16[128,16,512]{2,1,0:T(8,128)(2,1)S(1)} async-done(((bf16[128,16,512]{2,1,0:T(8,128)(2,1)}), bf16[128,16,512]{2,1,0:T(8,128)(2,1)S(1)}, u32[]{:S(2)}, u32[]{:S(2)}) %all-to-all-start.3) | async-done | bytes 2097184 | tf_op jit(solution)/shard_map/all_to_all | solution.py:306
  198.9 1.3 shard_map.126
  (12 shorter events, 0.0 us)
Async XLA Ops:
  0.6 11.4 %copy-start.5 = (bf16[32,128]{1,0:T(8,128)(2,1)S(1)}, bf16[32,128]{1,0:T(8,128)(2,1)}, u32[]{:S(2)}) copy-start(bf16[32,128]{1,0:T(8,128)(2,1)} %param.14) | copy-start | bytes 24580
  0.6 12.2 %copy-start.6 = (bf16[32,128]{1,0:T(8,128)(2,1)S(1)}, bf16[32,128]{1,0:T(8,128)(2,1)}, u32[]{:S(2)}) copy-start(bf16[32,128]{1,0:T(8,128)(2,1)} %param.15) | copy-start | bytes 24580
  0.7 12.3 %copy-start.7 = (s32[1024]{0:T(1024)S(1)}, s32[1024]{0:T(1024)}, u32[]{:S(2)}) copy-start(s32[1024]{0:T(1024)} %param.16) | copy-start | bytes 12292
  0.7 27.7 %collective-permute-start = (bf16[4096,128]{1,0:T(8,128)(2,1)}, bf16[4096,128]{1,0:T(8,128)(2,1)S(1)}, u32[]{:S(2)}, u32[]{:S(2)}) collective-permute-start(bf16[4096,128]{1,0:T(8,128)(2,1)} %k0_ref.1), channel_id=1, source_target_pairs={{0,4},{4,0},{8,12},{12,8},{16,20},{20,16},{24,28},{28,24},{32,36},... | collective-permute-start | bytes 3145736 | tf_op jit(solution)/shard_map/ppermute | solution.py:279
  2.2 26.2 %collective-permute-start.1 = (bf16[4096,128]{1,0:T(8,128)(2,1)}, bf16[4096,128]{1,0:T(8,128)(2,1)S(1)}, u32[]{:S(2)}, u32[]{:S(2)}) collective-permute-start(bf16[4096,128]{1,0:T(8,128)(2,1)} %v0_ref.1), channel_id=1, source_target_pairs={{0,4},{4,0},{8,12},{12,8},{16,20},{20,16},{24,28},{28,24},{32,36},... | collective-permute-start | bytes 3145736 | tf_op jit(solution)/shard_map/ppermute | solution.py:279
  4.2 24.1 %all-to-all-start = ((bf16[16,32,1024]{2,1,0:T(8,128)(2,1)}), bf16[16,32,1024]{2,1,0:T(8,128)(2,1)S(1)}, u32[]{:S(2)}, u32[]{:S(2)}) async-start(bf16[16,32,1024]{2,1,0:T(8,128)(2,1)} %broadcast_in_dim.15), calls=%async_computation | async-start | bytes 2097152 | tf_op jit(solution)/shard_map/all_to_all | solution.py:283
  12.1 1.7 collective-permute-start.2
  12.9 1.5 collective-permute-start.3
  28.4 1.1 copy-start.4
  28.4 1.4 copy-start.9
  28.4 1.7 copy-start.10
  75.5 21.6 %copy-start.2 = (s32[32,2]{0,1:T(2,128)S(1)}, s32[32,2]{0,1:T(2,128)}, u32[]{:S(2)}) copy-start(s32[32,2]{0,1:T(2,128)} %param.19) | copy-start | bytes 772
  98.7 43.9 %copy-start.1 = (f32[4096]{0:T(1024)S(1)}, f32[4096]{0:T(1024)}, u32[]{:S(2)}) copy-start(f32[4096]{0:T(1024)} %param.17) | copy-start | bytes 49156
  137.1 4.2 %collective-permute-start.4 = (bf16[32,4,16,512]{3,2,1,0:T(8,128)(2,1)S(1)}, bf16[32,4,16,512]{3,2,1,0:T(8,128)(2,1)S(1)}, u32[]{:S(2)}, u32[]{:S(2)}) collective-permute-start(bf16[32,4,16,512]{3,2,1,0:T(8,128)(2,1)S(1)} %bitcast.21), channel_id=1, source_target_pairs={{0,4},{4,0},{8,12},{12,8},{16,20},{20,16},{24,28},{28,24},{32,36},... | collective-permute-start | bytes 6291464 | tf_op jit(solution)/shard_map/ppermute | solution.py:279
  141.2 1.3 copy-start.3
  141.2 19.5 %slice-start = ((s8[6291456]{0:T(1024)(128)(4,1)}), s8[4194304]{0:T(1024)(128)(4,1)S(1)}, s32[]{:S(2)}) async-start(s8[6291456]{0:T(1024)(128)(4,1)} %bitcast.16), calls=%async_computation.4 | async-start | bytes 8388608
  142.6 18.2 %slice-start.1 = ((s8[6291456]{0:T(1024)(128)(4,1)}), s8[2097152]{0:T(1024)(128)(4,1)S(1)}, s32[]{:S(2)}) async-start(s8[6291456]{0:T(1024)(128)(4,1)} %bitcast.16), calls=%async_computation.5 | async-start | bytes 4194304
  156.5 4.3 %collective-permute-start.5 = (bf16[32,4,16,512]{3,2,1,0:T(8,128)(2,1)S(1)}, bf16[32,4,16,512]{3,2,1,0:T(8,128)(2,1)S(1)}, u32[]{:S(2)}, u32[]{:S(2)}) collective-permute-start(bf16[32,4,16,512]{3,2,1,0:T(8,128)(2,1)S(1)} %get-tuple-element.9), channel_id=1, source_target_pairs={{0,4},{4,0},{8,12},{12,8},{16,20},{20,16},{24,28},{28,24},{32,36},... | collective-permute-start | bytes 6291464 | tf_op jit(solution)/shard_map/ppermute | solution.py:279
  162.6 1.3 copy-start
  164.0 4.0 %copy-start.8 = (f32[32,2]{0,1:T(2,128)S(1)}, f32[32,2]{0,1:T(2,128)}, u32[]{:S(2)}) copy-start(f32[32,2]{0,1:T(2,128)} %param.18) | copy-start | bytes 772
  164.0 34.9 %all-to-all-start.3 = ((bf16[128,16,512]{2,1,0:T(8,128)(2,1)}), bf16[128,16,512]{2,1,0:T(8,128)(2,1)S(1)}, u32[]{:S(2)}, u32[]{:S(2)}) async-start(bf16[128,16,512]{2,1,0:T(8,128)(2,1)} %bitcast.20), calls=%async_computation.3 | async-start | bytes 4194304 | tf_op jit(solution)/shard_map/all_to_all | solution.py:306

commit v2 on v1

--- a/solution.py
+++ b/solution.py
@@ -21,7 +21,7 @@
 VM = pl.BlockSpec(memory_space=pltpu.VMEM)
 SM = pl.BlockSpec(memory_space=pltpu.SMEM)
 
-def attn_kernel(pos_ref, lim_ref, q_ref, k0_ref, k1_ref, v0_ref, v1_ref, nk_ref, nv_ref, o_ref, kk, vv, s_scr, m_scr, l_scr, *, R, CH, W):
+def attn_kernel(pos_ref, reach_ref, q_ref, k0_ref, k1_ref, v0_ref, v1_ref, nk_ref, nv_ref, o_ref, kk, vv, s_scr, m_scr, l_scr, lim_ref, *, R, CH, W):
     T=q_ref.shape[0]; KEYS=k0_ref.shape[0]; NT=(T//R)*8; NCH=KEYS//CH; WIN=2*KEYS
     for half,kr,vr in ((0,k0_ref,v0_ref),(1,k1_ref,v1_ref)):
         k=kr[...]; v=vr[...]
@@ -33,6 +33,8 @@
     kk[pl.ds(WIN,128),:]=jnp.concatenate([nk,nk],axis=1)
     vv[pl.ds(WIN,128),:]=jnp.concatenate([nv,jnp.ones_like(nv)],axis=1)
     l_scr[...]=jnp.zeros_like(l_scr)
+    for t in range(T//R):
+        lim_ref[pl.ds(t*R,R),:]=jnp.transpose(jnp.broadcast_to(reach_ref[:,pl.ds(t*R,R)],(128,R)))
     def tile(i):
         h=lax.rem(i,8); tb=lax.div(i,8)
         return pl.multiple_of(tb*R,R), pl.multiple_of(h*HD,HD), h
@@ -109,13 +111,13 @@
         in_specs=[SM]+[VM]*8,
         out_specs=VM,
         scratch_shapes=[pltpu.VMEM((2*KEYS+128,2*HD),BF),pltpu.VMEM((2*KEYS+128,2*HD),BF),
-            pltpu.VMEM((2,R,2*KEYS+128),F32),pltpu.VMEM((R,128),F32),pltpu.VMEM((T,128),F32)],
-        compiler_params=pltpu.CompilerParams(vmem_limit_bytes=60*MIB),
+            pltpu.VMEM((2,R,2*KEYS+128),F32),pltpu.VMEM((R,128),F32),pltpu.VMEM((T,128),F32),pltpu.VMEM((T,128),jnp.int32)],
+        compiler_params=pltpu.CompilerParams(vmem_limit_bytes=42*MIB),
         cost_estimate=pl.CostEstimate(flops=4*T*8*2*KEYS*HD*2,bytes_accessed=8*1024*1024,transcendentals=T*8*2*KEYS),
     )(pos,lim,q,k0,k1,v0,v1,nk,nv)
 
 
-def home_kernel(recv_ref, ids_ref, att_ref, msg_ref):
+def home_kernel(recv_ref, ids_ref, idc_ref, gate_ref, att_ref, msg_ref, mat_ref):
     blocks, tok, _ = recv_ref.shape
     heads = att_ref.shape[1] // HD
     logs = []
@@ -149,117 +151,142 @@
             for y in range(msg_ref.shape[1]):
                 for x in range(msg_ref.shape[3]):
                     msg_ref[e, y, c, x] = part
-
-
-def home(recv, ids_t, tp):
-    tok, width = recv.shape[1], recv.shape[2] - 128
-    return pl.pallas_call(
-        home_kernel,
-        out_shape=(
-            jax.ShapeDtypeStruct((tok, width), BF),
-            jax.ShapeDtypeStruct((E, 2, 2, tp, CAP, width // 2), BF),
-        ),
-        in_specs=[VM, VM],
-        out_specs=(VM, VM),
-        compiler_params=pltpu.CompilerParams(vmem_limit_bytes=32 * MIB),
-    )(recv, ids_t)
-
-
-def up_kernel(core_ref, own_ref, other_ref, gain_ref, up_ref, down_ref, hidden_ref, send_ref):
-    seqs, tp, cap, half = own_ref.shape
-    rows = seqs * cap
-    core = core_ref[0]
-
-    def part(ref, x):
-        return ref[:, x].reshape(rows, half).astype(F32)
-
-    square = jnp.zeros((rows, 128), F32)
-    for ref in (own_ref, other_ref):
-        for x in range(tp):
-            a = part(ref, x)
-            a = a * a
-            for c in range(half // 128):
-                square = square + a[:, c * 128 : (c + 1) * 128]
-    mean = jnp.sum(square, axis=1, keepdims=True) / (2 * tp * half)
-    inverse = lax.rsqrt(mean + EPSILON)
-    total = jnp.zeros((rows, up_ref.shape[1]), F32)
-    for ref, side in ((own_ref, core), (other_ref, 1 - core)):
-        for x in range(tp):
-            first = pl.multiple_of(x * 2 * half + side * half, half)
-            normed = (part(ref, x) * inverse * gain_ref[:, pl.ds(first, half)]).astype(BF)
-            total = total + jnp.dot(normed, up_ref[pl.ds(first, half), :], preferred_element_type=F32)
-    hidden = (total / (1.0 + jnp.exp(-total))).astype(BF)
-    hidden_ref[...] = hidden
-    for x in range(tp):
-        first = pl.multiple_of(x * 2 * half + (1 - core) * half, half)
-        out = jnp.dot(hidden, down_ref[:, pl.ds(first, half)], preferred_element_type=F32)
-        send_ref[:, x] = out.astype(BF).reshape(seqs, cap, half)
-
-
-def up_project(core, own, other, gain, w_up, w_down):
-    rows = own.shape[0] * own.shape[2]
-    return pl.pallas_call(
-        up_kernel,
-        out_shape=(
-            jax.ShapeDtypeStruct((rows, w_up.shape[1]), BF),
-            jax.ShapeDtypeStruct(own.shape, BF),
-        ),
-        in_specs=[SM] + [VM] * 5,
-        out_specs=(VM, VM),
-        compiler_params=pltpu.CompilerParams(vmem_limit_bytes=48 * MIB),
-    )(core, own, other, gain, w_up, w_down)
-
-
-def down_kernel(core_ref, hidden_ref, down_ref, partner_ref, out_ref):
-    seqs, tp, cap, half = out_ref.shape
-    hidden = hidden_ref[...]
-    for x in range(tp):
-        first = pl.multiple_of(x * 2 * half + core_ref[0] * half, half)
-        out = jnp.dot(hidden, down_ref[:, pl.ds(first, half)], preferred_element_type=F32)
-        out = out + partner_ref[:, x].reshape(seqs * cap, half).astype(F32)
-        out_ref[:, x] = out.astype(BF).reshape(seqs, cap, half)
-
-
-def down_project(core, hidden, w_down, partner):
-    return pl.pallas_call(
-        down_kernel,
-        out_shape=jax.ShapeDtypeStruct(partner.shape, BF),
-        in_specs=[SM] + [VM] * 3,
-        out_specs=VM,
-        compiler_params=pltpu.CompilerParams(vmem_limit_bytes=40 * MIB),
-    )(core, hidden, w_down, partner)
-
-
-def mix_kernel(recv_ref, ids_ref, gate_ref, out_ref):
-    experts, pair, cores, tp, cap, half = recv_ref.shape
+    gate_matrix(idc_ref, gate_ref, mat_ref, msg_ref.shape[1] * msg_ref.shape[3])
+
+
+def gate_matrix(ids_ref, gate_ref, mat_ref, copies):
     tok = ids_ref.shape[0]
-    terms = experts * pair * tp * cap
+    terms = E * copies * CAP
     lane = lax.broadcasted_iota(jnp.int32, (tok, terms), 1)
-    expert = lax.div(lane, pair * tp * cap)
+    expert = lax.div(lane, copies * CAP)
     first, second = ids_ref[:, 0:1] == expert, ids_ref[:, 1:2] == expert
     gate = jnp.where(first, gate_ref[:, 0:1], 0.0) + jnp.where(second, gate_ref[:, 1:2], 0.0)
     earlier = lax.broadcasted_iota(jnp.int32, (tok, tok), 1) < lax.broadcasted_iota(jnp.int32, (tok, tok), 0)
     rank = jnp.dot(
         jnp.where(earlier, 1.0, 0.0).astype(BF), jnp.where(first | second, 1.0, 0.0).astype(BF), preferred_element_type=F32
     )
-    gate = jnp.where(rank == lax.rem(lane, cap).astype(F32), gate, 0.0)
+    gate = jnp.where(rank == lax.rem(lane, CAP).astype(F32), gate, 0.0)
     high = gate.astype(BF)
-    low = (gate - high.astype(F32)).astype(BF)
-    both = jnp.concatenate([high, low], axis=0)
+    mat_ref[pl.ds(0, tok), :] = high
+    mat_ref[pl.ds(tok, tok), :] = (gate - high.astype(F32)).astype(BF)
+
+
+def home(recv, ids, gates, tp):
+    tok, width = recv.shape[1], recv.shape[2] - 128
+    return pl.pallas_call(
+        home_kernel,
+        out_shape=(
+            jax.ShapeDtypeStruct((tok, width), BF),
+            jax.ShapeDtypeStruct((E, 2, 2, tp, CAP, width // 2), BF),
+            jax.ShapeDtypeStruct((2 * tok, E * 2 * tp * CAP), BF),
+        ),
+        in_specs=[VM] * 4,
+        out_specs=(VM, VM, VM),
+        compiler_params=pltpu.CompilerParams(vmem_limit_bytes=24 * MIB),
+    )(recv, ids.T, ids, gates)
+
+
+def columns(x, side, half):
+    return pl.ds(pl.multiple_of(x * 2 * half + side * half, half), half)
+
+
+def up_part(ref, side, gain_ref, up_ref, total, square):
+    seqs, tp, cap, half = ref.shape
+    for x in range(tp):
+        a = ref[:, x].reshape(seqs * cap, half).astype(F32)
+        scaled = (a * gain_ref[:, columns(x, side, half)]).astype(BF)
+        total = total + jnp.dot(scaled, up_ref[columns(x, side, half), :], preferred_element_type=F32)
+        for c in range(half // 128):
+            part = a[:, c * 128 : (c + 1) * 128]
+            square = square + part * part
+    return total, square
+
+
+def up_first_kernel(core_ref, own_ref, gain_ref, up_ref, total_ref, square_ref):
+    total, square = up_part(
+        own_ref, core_ref[0], gain_ref, up_ref, jnp.zeros(total_ref.shape, F32), jnp.zeros(square_ref.shape, F32)
+    )
+    total_ref[...] = total
+    square_ref[...] = square
+
+
+def up_first(core, own, gain, w_up):
+    rows = own.shape[0] * own.shape[2]
+    return pl.pallas_call(
+        up_first_kernel,
+        out_shape=(
+            jax.ShapeDtypeStruct((rows, w_up.shape[1]), F32),
+            jax.ShapeDtypeStruct((rows, 128), F32),
+        ),
+        in_specs=[SM] + [VM] * 3,
+        out_specs=(VM, VM),
+        compiler_params=pltpu.CompilerParams(vmem_limit_bytes=24 * MIB),
+        cost_estimate=pl.CostEstimate(flops=rows * own.shape[3] * 8 * w_up.shape[1], bytes_accessed=8 * MIB, transcendentals=0),
+    )(core, own, gain, w_up)
+
+
+def up_second_kernel(core_ref, other_ref, gain_ref, up_ref, down_ref, total_ref, square_ref, hidden_ref, send_ref):
+    seqs, tp, cap, half = other_ref.shape
+    other = 1 - core_ref[0]
+    total, square = up_part(other_ref, other, gain_ref, up_ref, total_ref[...], square_ref[...])
+    mean = jnp.sum(square, axis=1, keepdims=True) / (2 * tp * half)
+    total = total * lax.rsqrt(mean + EPSILON)
+    hidden = (total / (1.0 + jnp.exp(-total))).astype(BF)
+    hidden_ref[...] = hidden
+    for x in range(tp):
+        out = jnp.dot(hidden, down_ref[:, columns(x, other, half)], preferred_element_type=F32)
+        send_ref[:, x] = out.astype(BF).reshape(seqs, cap, half)
+
+
+def up_second(core, other, gain, w_up, w_down, total, square):
+    return pl.pallas_call(
+        up_second_kernel,
+        out_shape=(
+            jax.ShapeDtypeStruct(total.shape, BF),
+            jax.ShapeDtypeStruct(other.shape, BF),
+        ),
+        in_specs=[SM] + [VM] * 6,
+        out_specs=(VM, VM),
+        compiler_params=pltpu.CompilerParams(vmem_limit_bytes=32 * MIB),
+    )(core, other, gain, w_up, w_down, total, square)
+
+
+def down_kernel(core_ref, hidden_ref, down_ref, partner_ref, out_ref):
+    seqs, tp, cap, half = out_ref.shape
+    hidden = hidden_ref[...]
+    for x in range(tp):
+        out = jnp.dot(hidden, down_ref[:, columns(x, core_ref[0], half)], preferred_element_type=F32)
+        out = out + partner_ref[:, x].reshape(seqs * cap, half).astype(F32)
+        out_ref[:, x] = out.astype(BF).reshape(seqs, cap, half)
+
+
+def down_project(core, hidden, w_down, partner):
+    return pl.pallas_call(
+        down_kernel,
+        out_shape=jax.ShapeDtypeStruct(partner.shape, BF),
+        in_specs=[SM] + [VM] * 3,
+        out_specs=VM,
+        compiler_params=pltpu.CompilerParams(vmem_limit_bytes=24 * MIB),
+    )(core, hidden, w_down, partner)
+
+
+def mix_kernel(recv_ref, mat_ref, out_ref):
+    experts, pair, cores, tp, cap, half = recv_ref.shape
+    tok = out_ref.shape[0]
     for c in range(cores):
-        values = recv_ref[:, :, c].reshape(terms, half)
-        out = jnp.dot(both, values, preferred_element_type=F32)
+        values = recv_ref[:, :, c].reshape(experts * pair * tp * cap, half)
+        out = jnp.dot(mat_ref[...], values, preferred_element_type=F32)
         out_ref[:, pl.ds(c * half, half)] = (out[:tok] + out[tok:]).astype(BF)
 
 
-def mix(recv, ids, gates):
+def mix(recv, matrix):
     return pl.pallas_call(
         mix_kernel,
-        out_shape=jax.ShapeDtypeStruct((ids.shape[0], 2 * recv.shape[5]), BF),
-        in_specs=[VM] * 3,
+        out_shape=jax.ShapeDtypeStruct((matrix.shape[0] // 2, 2 * recv.shape[5]), BF),
+        in_specs=[VM] * 2,
         out_specs=VM,
-        compiler_params=pltpu.CompilerParams(vmem_limit_bytes=32 * MIB),
-    )(recv, ids, gates)
+        compiler_params=pltpu.CompilerParams(vmem_limit_bytes=24 * MIB),
+    )(recv, matrix)
 
 
 def per_device(
@@ -285,7 +312,7 @@
         "seq", 0, 0, axis_index_groups=same_core, tiled=True,
     ).reshape(chips * tok, width)
     limits = lax.dynamic_index_in_dim(reach.reshape(chips, 2, tok), core, 1, keepdims=False)
-    limits = jnp.broadcast_to(limits.reshape(chips * tok, 1), (chips * tok, 128))
+    limits = limits.reshape(1, chips * tok)
     places = jnp.stack([seq * ctx, partner * ctx, seq * tok, partner * tok, core]).astype(jnp.int32)
     outs = attention(
         places, limits, all_queries, cache_keys, other_keys, cache_values, other_values,
@@ -295,18 +322,20 @@
     arrived = lax.all_to_all(
         outs.reshape(chips, tok, outs.shape[1]), "seq", 0, 0, axis_index_groups=same_core, tiled=True
     )
-    attended, message = home(arrived, expert_ids.T, tp)
+    attended, message, matrix = home(arrived, expert_ids, gate_weights, tp)
     half = width // 2
     rows = lax.all_to_all(
         message.reshape(seqs * tp, CAP, half), ("seq", "tp"), 0, 0, tiled=True
     ).reshape(seqs, tp, CAP, half)
     side = core.astype(jnp.int32).reshape(1)
-    hidden, send = up_project(side, rows, swapped(rows), norm_gain.reshape(1, -1), w_up[0], w_down[0])
+    gain = norm_gain.reshape(1, -1)
+    total, square = up_first(side, rows, gain, w_up[0])
+    hidden, send = up_second(side, swapped(rows), gain, w_up[0], w_down[0], total, square)
     result = down_project(side, hidden, w_down[0], swapped(send))
     returned = lax.all_to_all(
         result.reshape(seqs * tp, CAP, half), ("seq", "tp"), 0, 0, tiled=True
     ).reshape(E, 2, 2, tp, CAP, half)
-    return attended, mix(returned, expert_ids, gate_weights)
+    return attended, mix(returned, matrix)
 
 
 def solution(mesh):

time: 201 us -> 191 us (0.950)
  waiting for transfers between devices: 51.7 us -> 35.8 us
  blocking collectives: 60 us -> 72.4 us
  Pallas kernels: 64 us -> 53.8 us
  local copies, waits for them, and re-layouts: 7.31 us -> 12.2 us
    all_to_all x1, waiting for transfers between devices: 30.8 us -> 16.7 us  [per_device(): lax.all_to_all(outs.reshape(chips, tok, outs.shape[1]), 'seq', 0, 0, axis...]
    all_to_all x1, blocking collectives: 21.6 us -> 34.2 us  [per_device(): lax.all_to_all(result.reshape(seqs * tp, CAP, half), ('seq', 'tp'), 0, 0,...]
    pallas_call x2 -> x3, Pallas kernels: 15.2 us -> 6.97 us  [the longest x1 4.04 us: up_second(): pl.pallas_call(up_second_kernel, out_shape=(jax.ShapeDtypeStruct(total.sh...]
    unnamed x28 -> x30, local copies, waits for them, and re-layouts: 3.58 us -> 9.95 us
    ppermute x6, waiting for transfers between devices: 7.58 us -> 4.81 us  [swapped(): return lax.ppermute(value, 'seq', swap)]
    pallas_call x1, Pallas kernels: 45.5 us -> 43.4 us  [attention(): pl.pallas_call(functools.partial(attn_kernel, R=R, CH=CH, W=W), out_shape...]
  transfers between devices with their start and end apart: 8 -> 8, of which waited for: 4 -> 5; matrix products, arithmetic and copies ran while one was open for 2% -> 1% of each run, Pallas kernels for 0% -> 1%
where the time goes in v2:
time: 191 us
  blocking collectives  72.4 us (38%)
  Pallas kernels  53.8 us (28%)
  waiting for transfers between devices  35.8 us (19%)
  starting transfers between devices  15.6 us (8%)
  local copies, waits for them, and re-layouts  12.2 us (6%)
    pallas_call x1, Pallas kernels, attention(): pl.pallas_call(functools.partial(attn_kernel, R=R, CH=CH, W=W), out_shape...  43.4 us
    all_to_all x1, blocking collectives, per_device(): lax.all_to_all(message.reshape(seqs * tp, CAP, half), ('seq', 'tp'), 0, 0...  38.2 us
    all_to_all x1, blocking collectives, per_device(): lax.all_to_all(result.reshape(seqs * tp, CAP, half), ('seq', 'tp'), 0, 0,...  34.2 us
    all_to_all x1, waiting for transfers between devices, per_device(): lax.all_to_all(outs.reshape(chips, tok, outs.shape[1]), 'seq', 0, 0, axis...  16.7 us
    all_to_all x1, waiting for transfers between devices, per_device(): lax.all_to_all(jnp.broadcast_to(queries[None], (chips, tok, width)), 'seq...  14.2 us
    unnamed x30, local copies, waits for them, and re-layouts  9.95 us
    all_to_all x1, starting transfers between devices, per_device(): lax.all_to_all(jnp.broadcast_to(queries[None], (chips, tok, width)), 'seq...  7.85 us
    ppermute x6, waiting for transfers between devices, swapped(): return lax.ppermute(value, 'seq', swap)  4.81 us
  transfers between devices with their start and end apart: 8, of which 5 were waited for; matrix products, arithmetic and copies ran while one was open for 1% of the time, Pallas kernels for 1%

profile of v2, /device:TPU:1, one launch (start us, length us, event | category | flops | bytes accessed | tf_op | source)
XLA Modules:
  0.0 190.6 jit_solution(9848747972614759890)
XLA Ops:
  0.6 0.0 copy-start.6
  0.6 0.0 copy-start.7
  0.7 0.0 copy-start.8
  0.7 0.0 copy-start.9
  0.7 0.0 copy-start.10
  0.7 1.5 collective-permute-start
  2.2 0.1 collective-permute-start.1
  2.3 1.9 %broadcast_in_dim.2 = bf16[16,32,1024]{2,1,0:T(8,128)(2,1)} broadcast(bf16[32,1024]{1,0:T(8,128)(2,1)} %param.11), dimensions={1,2} | broadcast | bytes 1114112 | tf_op jit(solution)/shard_map/broadcast_in_dim | solution.py:311
  4.2 7.9 %all-to-all-start = ((bf16[16,32,1024]{2,1,0:T(8,128)(2,1)}), bf16[16,32,1024]{2,1,0:T(8,128)(2,1)S(1)}, u32[]{:S(2)}, u32[]{:S(2)}) async-start(bf16[16,32,1024]{2,1,0:T(8,128)(2,1)} %broadcast_in_dim.2), calls=%async_computation | async-start | bytes 2097152 | tf_op jit(solution)/shard_map/all_to_all | solution.py:310
  12.1 0.0 copy-done.8
  12.1 0.8 collective-permute-start.2
  12.9 0.0 copy-done.9
  12.9 0.1 collective-permute-start.3
  13.0 0.0 copy-done.10
  13.0 0.1 reshape.34
  13.1 0.1 reshape.35.reach_ref
  13.2 0.1 stack.23.pos_ref
  13.3 0.4 collective-permute-done.2
  13.7 0.3 collective-permute-done.3
  14.1 14.2 %all-to-all-done = bf16[16,32,1024]{2,1,0:T(8,128)(2,1)S(1)} async-done(((bf16[16,32,1024]{2,1,0:T(8,128)(2,1)}), bf16[16,32,1024]{2,1,0:T(8,128)(2,1)S(1)}, u32[]{:S(2)}, u32[]{:S(2)}) %all-to-all-start) | async-done | bytes 1048608 | tf_op jit(solution)/shard_map/all_to_all | solution.py:310
  28.3 0.0 collective-permute-done.k1_ref
  28.3 0.0 collective-permute-done.1.v1_ref
  28.3 0.0 copy-done.6
  28.3 0.0 copy-done.7
  28.3 43.4 %shard_map.122 = bf16[512,1152]{1,0:T(8,128)(2,1)S(1)} custom-call(s32[5]{0:T(128)S(1)} %stack.23.pos_ref, s32[1,512]{1,0:T(1,128)S(1)} %reshape.35.reach_ref, bf16[512,1024]{1,0:T(8,128)(2,1)S(1)} %bitcast.27, bf16[4096,128]{1,0:T(8,128)(2,1)S(1)} %copy-done.6, bf16[4096,128]{1,0:T(8,128)(2,1)} %collective-permute-done.k1_ref, ...), custom_call_target="tpu_custom_call" | custom-call | flops 34359738368 | bytes 8388608 | tf_op jit(solution)/shard_map/pallas_call | solution.py:108
  71.8 0.0 copy-start.3
  71.8 1.0 copy-done.3
  72.9 4.7 %all-to-all-start.1 = ((bf16[16,32,1152]{2,1,0:T(8,128)(2,1)}), bf16[16,32,1152]{2,1,0:T(8,128)(2,1)S(1)}, u32[]{:S(2)}, u32[]{:S(2)}) async-start(bf16[16,32,1152]{2,1,0:T(8,128)(2,1)} %bitcast.26), calls=%async_computation.1 | async-start | bytes 2359296 | tf_op jit(solution)/shard_map/all_to_all | solution.py:322
  77.5 0.0 copy-done.11
  77.5 0.1 copy.16.gate_ref
  77.6 0.0 copy-done.5
  77.6 0.1 copy.15.idc_ref
  77.7 16.7 %all-to-all-done.1.recv_ref = bf16[16,32,1152]{2,1,0:T(8,128)(2,1)S(1)} async-done(((bf16[16,32,1152]{2,1,0:T(8,128)(2,1)}), bf16[16,32,1152]{2,1,0:T(8,128)(2,1)S(1)}, u32[]{:S(2)}, u32[]{:S(2)}) %all-to-all-start.1) | async-done | bytes 1179680 | tf_op jit(solution)/shard_map/all_to_all | solution.py:322
  94.4 1.6 shard_map.123
  96.0 38.2 %all_to_all.20 = bf16[128,16,512]{2,1,0:T(8,128)(2,1)S(1)} all-to-all(bf16[128,16,512]{2,1,0:T(8,128)(2,1)S(1)} %bitcast.25), channel_id=1, replica_groups=mesh['seq'=32,'tp'=4] {'seq','tp'}, dimensions={0} | all-to-all | bytes 4194304 | tf_op jit(solution)/shard_map/all_to_all | solution.py:327
  134.3 0.4 collective-permute-start.4
  134.7 2.8 %copy-done = bf16[1,4096,768]{2,1,0:T(8,128)(2,1)S(1)} copy-done((bf16[1,4096,768]{2,1,0:T(8,128)(2,1)S(1)}, bf16[1,4096,768]{2,1,0:T(8,128)(2,1)}, u32[]{:S(2)}) %copy-start) | copy-done | bytes 6291480
  137.5 1.8 shard_map.124
  139.3 0.0 collective-permute-done.4.other_ref
  139.3 0.3 slice-done.1
  139.6 2.8 %copy-done.1 = bf16[1,768,4096]{2,1,0:T(8,128)(2,1)S(1)} copy-done((bf16[1,768,4096]{2,1,0:T(8,128)(2,1)S(1)}, bf16[1,768,4096]{2,1,0:T(8,128)(2,1)}, u32[]{:S(2)}) %copy-start.1) | copy-done | bytes 6291480
  142.4 4.0 %shard_map.125 = (bf16[512,768]{1,0:T(8,128)(2,1)S(1)}, bf16[32,4,16,512]{3,2,1,0:T(8,128)(2,1)S(1)}) custom-call(s32[1]{0:T(128)} %bitcast.4.core_ref, bf16[32,4,16,512]{3,2,1,0:T(8,128)(2,1)S(1)} %collective-permute-done.4.other_ref, f32[1,4096]{1,0:T(1,128)S(1)} %bitcast.29, bf16[4096,768]{1,0:T(8,128)(2,1)S(1)} %bitcast.18, ...), custom_call_target="tpu_custom_call" | custom-call | tf_op jit(solution)/shard_map/pallas_call | solution.py:242
  146.5 0.2 collective-permute-start.5
  146.7 4.0 %collective-permute-done.5.partner_ref = bf16[32,4,16,512]{3,2,1,0:T(8,128)(2,1)S(1)} collective-permute-done((bf16[32,4,16,512]{3,2,1,0:T(8,128)(2,1)S(1)}, bf16[32,4,16,512]{3,2,1,0:T(8,128)(2,1)S(1)}, u32[]{:S(2)}, u32[]{:S(2)}) %collective-permute-start.5) | collective-permute-done | bytes 2097184 | tf_op jit(solution)/shard_map/ppermute | solution.py:306
  150.7 2.8 %copy-done.2 = bf16[1,768,4096]{2,1,0:T(8,128)(2,1)S(1)} copy-done((bf16[1,768,4096]{2,1,0:T(8,128)(2,1)S(1)}, bf16[1,768,4096]{2,1,0:T(8,128)(2,1)}, u32[]{:S(2)}) %copy-start.2) | copy-done | bytes 6291480
  153.5 1.8 shard_map.126
  155.3 34.2 %all_to_all.21 = bf16[128,16,512]{2,1,0:T(8,128)(2,1)S(1)} all-to-all(bf16[128,16,512]{2,1,0:T(8,128)(2,1)S(1)} %bitcast.24), channel_id=1, replica_groups=mesh['seq'=32,'tp'=4] {'seq','tp'}, dimensions={0} | all-to-all | bytes 4194304 | tf_op jit(solution)/shard_map/all_to_all | solution.py:335
  189.5 1.1 shard_map.127
  (14 shorter events, 0.1 us)
Async XLA Ops:
  0.6 27.7 %copy-start.6 = (bf16[4096,128]{1,0:T(8,128)(2,1)S(1)}, bf16[4096,128]{1,0:T(8,128)(2,1)}, u32[]{:S(2)}) copy-start(bf16[4096,128]{1,0:T(8,128)(2,1)} %k0_ref.1) | copy-start | bytes 3145732
  0.6 27.7 %copy-start.7 = (bf16[4096,128]{1,0:T(8,128)(2,1)S(1)}, bf16[4096,128]{1,0:T(8,128)(2,1)}, u32[]{:S(2)}) copy-start(bf16[4096,128]{1,0:T(8,128)(2,1)} %v0_ref.1) | copy-start | bytes 3145732
  0.7 11.4 %copy-start.8 = (bf16[32,128]{1,0:T(8,128)(2,1)S(1)}, bf16[32,128]{1,0:T(8,128)(2,1)}, u32[]{:S(2)}) copy-start(bf16[32,128]{1,0:T(8,128)(2,1)} %param.14) | copy-start | bytes 24580
  0.7 12.2 %copy-start.9 = (bf16[32,128]{1,0:T(8,128)(2,1)S(1)}, bf16[32,128]{1,0:T(8,128)(2,1)}, u32[]{:S(2)}) copy-start(bf16[32,128]{1,0:T(8,128)(2,1)} %param.15) | copy-start | bytes 24580
  0.7 12.3 %copy-start.10 = (s32[1024]{0:T(1024)S(1)}, s32[1024]{0:T(1024)}, u32[]{:S(2)}) copy-start(s32[1024]{0:T(1024)} %param.16) | copy-start | bytes 12292
  0.7 27.6 %collective-permute-start = (bf16[4096,128]{1,0:T(8,128)(2,1)}, bf16[4096,128]{1,0:T(8,128)(2,1)}, u32[]{:S(2)}, u32[]{:S(2)}) collective-permute-start(bf16[4096,128]{1,0:T(8,128)(2,1)} %k0_ref.1), channel_id=1, source_target_pairs={{0,4},{4,0},{8,12},{12,8},{16,20},{20,16},{24,28},{28,24},{32,36},... | collective-permute-start | bytes 3145736 | tf_op jit(solution)/shard_map/ppermute | solution.py:306
  2.2 26.1 %collective-permute-start.1 = (bf16[4096,128]{1,0:T(8,128)(2,1)}, bf16[4096,128]{1,0:T(8,128)(2,1)}, u32[]{:S(2)}, u32[]{:S(2)}) collective-permute-start(bf16[4096,128]{1,0:T(8,128)(2,1)} %v0_ref.1), channel_id=1, source_target_pairs={{0,4},{4,0},{8,12},{12,8},{16,20},{20,16},{24,28},{28,24},{32,36},... | collective-permute-start | bytes 3145736 | tf_op jit(solution)/shard_map/ppermute | solution.py:306
  4.2 24.1 %all-to-all-start = ((bf16[16,32,1024]{2,1,0:T(8,128)(2,1)}), bf16[16,32,1024]{2,1,0:T(8,128)(2,1)S(1)}, u32[]{:S(2)}, u32[]{:S(2)}) async-start(bf16[16,32,1024]{2,1,0:T(8,128)(2,1)} %broadcast_in_dim.2), calls=%async_computation | async-start | bytes 2097152 | tf_op jit(solution)/shard_map/all_to_all | solution.py:310
  12.1 1.6 collective-permute-start.2
  12.9 1.2 collective-permute-start.3
  71.8 1.1 copy-start.3
  72.8 4.7 %copy-start.11 = (f32[32,2]{0,1:T(2,128)S(1)}, f32[32,2]{0,1:T(2,128)}, u32[]{:S(2)}) copy-start(f32[32,2]{0,1:T(2,128)} %param.18) | copy-start | bytes 772
  72.8 4.8 %copy-start.5 = (s32[32,2]{0,1:T(2,128)S(1)}, s32[32,2]{0,1:T(2,128)}, u32[]{:S(2)}) copy-start(s32[32,2]{0,1:T(2,128)} %param.19) | copy-start | bytes 772
  72.9 66.4 %slice-start = ((s8[6291456]{0:T(1024)(128)(4,1)}), s8[2097152]{0:T(1024)(128)(4,1)S(1)}, s32[]{:S(2)}) async-start(s8[6291456]{0:T(1024)(128)(4,1)} %bitcast.16), calls=%async_computation.4 | async-start | bytes 4194304
  72.9 21.6 %all-to-all-start.1 = ((bf16[16,32,1152]{2,1,0:T(8,128)(2,1)}), bf16[16,32,1152]{2,1,0:T(8,128)(2,1)S(1)}, u32[]{:S(2)}, u32[]{:S(2)}) async-start(bf16[16,32,1152]{2,1,0:T(8,128)(2,1)} %bitcast.26), calls=%async_computation.1 | async-start | bytes 2359296 | tf_op jit(solution)/shard_map/all_to_all | solution.py:322
  96.0 38.6 %copy-start.4 = (f32[4096]{0:T(1024)S(1)}, f32[4096]{0:T(1024)}, u32[]{:S(2)}) copy-start(f32[4096]{0:T(1024)} %param.17) | copy-start | bytes 49156
  134.3 5.0 %collective-permute-start.4 = (bf16[32,4,16,512]{3,2,1,0:T(8,128)(2,1)S(1)}, bf16[32,4,16,512]{3,2,1,0:T(8,128)(2,1)S(1)}, u32[]{:S(2)}, u32[]{:S(2)}) collective-permute-start(bf16[32,4,16,512]{3,2,1,0:T(8,128)(2,1)S(1)} %bitcast.22), channel_id=1, source_target_pairs={{0,4},{4,0},{8,12},{12,8},{16,20},{20,16},{24,28},{28,24},{32,36},... | collective-permute-start | bytes 6291464 | tf_op jit(solution)/shard_map/ppermute | solution.py:306
  134.7 2.8 %copy-start = (bf16[1,4096,768]{2,1,0:T(8,128)(2,1)S(1)}, bf16[1,4096,768]{2,1,0:T(8,128)(2,1)}, u32[]{:S(2)}) copy-start(bf16[1,4096,768]{2,1,0:T(8,128)(2,1)} %param.20) | copy-start | bytes 18874372
  137.5 2.2 %slice-start.1 = ((s8[6291456]{0:T(1024)(128)(4,1)}), s8[4194304]{0:T(1024)(128)(4,1)S(1)}, s32[]{:S(2)}) async-start(s8[6291456]{0:T(1024)(128)(4,1)} %bitcast.16), calls=%async_computation.5 | async-start | bytes 8388608
  139.6 2.8 %copy-start.1 = (bf16[1,768,4096]{2,1,0:T(8,128)(2,1)S(1)}, bf16[1,768,4096]{2,1,0:T(8,128)(2,1)}, u32[]{:S(2)}) copy-start(bf16[1,768,4096]{2,1,0:T(8,128)(2,1)} %param.21) | copy-start | bytes 18874372
  146.5 4.2 %collective-permute-start.5 = (bf16[32,4,16,512]{3,2,1,0:T(8,128)(2,1)S(1)}, bf16[32,4,16,512]{3,2,1,0:T(8,128)(2,1)S(1)}, u32[]{:S(2)}, u32[]{:S(2)}) collective-permute-start(bf16[32,4,16,512]{3,2,1,0:T(8,128)(2,1)S(1)} %get-tuple-element.14), channel_id=1, source_target_pairs={{0,4},{4,0},{8,12},{12,8},{16,20},{20,16},{24,28},{28,24},{32,36},... | collective-permute-start | bytes 6291464 | tf_op jit(solution)/shard_map/ppermute | solution.py:306
  150.7 2.8 %copy-start.2 = (bf16[1,768,4096]{2,1,0:T(8,128)(2,1)S(1)}, bf16[1,768,4096]{2,1,0:T(8,128)(2,1)}, u32[]{:S(2)}) copy-start(bf16[1,768,4096]{2,1,0:T(8,128)(2,1)} %param.21) | copy-start | bytes 18874372

commit v3 on v2

--- a/solution.py
+++ b/solution.py
@@ -20,18 +20,10 @@
 MIB = 1024 * 1024
 VM = pl.BlockSpec(memory_space=pltpu.VMEM)
 SM = pl.BlockSpec(memory_space=pltpu.SMEM)
-
-def attn_kernel(pos_ref, reach_ref, q_ref, k0_ref, k1_ref, v0_ref, v1_ref, nk_ref, nv_ref, o_ref, kk, vv, s_scr, m_scr, l_scr, lim_ref, *, R, CH, W):
-    T=q_ref.shape[0]; KEYS=k0_ref.shape[0]; NT=(T//R)*8; NCH=KEYS//CH; WIN=2*KEYS
-    for half,kr,vr in ((0,k0_ref,v0_ref),(1,k1_ref,v1_ref)):
-        k=kr[...]; v=vr[...]
-        kk[pl.ds(half*KEYS,KEYS),:]=jnp.concatenate([k,k],axis=1)
-        vv[pl.ds(half*KEYS,KEYS),:]=jnp.concatenate([v,jnp.ones_like(v)],axis=1)
-    nk=nk_ref[...]; nv=nv_ref[...]
-    zero=jnp.zeros((128-2*W,HD),BF)
-    nk=jnp.concatenate([nk,zero],axis=0); nv=jnp.concatenate([nv,zero],axis=0)
-    kk[pl.ds(WIN,128),:]=jnp.concatenate([nk,nk],axis=1)
-    vv[pl.ds(WIN,128),:]=jnp.concatenate([nv,jnp.ones_like(nv)],axis=1)
+HBM = pl.BlockSpec(memory_space=pltpu.HBM)
+
+def attn_kernel(pos_ref, reach_ref, q_ref, kk, vv, o_ref, s_scr, m_scr, l_scr, lim_ref, *, R, CH, W):
+    T=q_ref.shape[0]; KEYS=(kk.shape[0]-128)//2; NT=(T//R)*8; NCH=KEYS//CH; WIN=2*KEYS
     l_scr[...]=jnp.zeros_like(l_scr)
     for t in range(T//R):
         lim_ref[pl.ds(t*R,R),:]=jnp.transpose(jnp.broadcast_to(reach_ref[:,pl.ds(t*R,R)],(128,R)))
@@ -103,21 +95,48 @@
     lane=lax.broadcasted_iota(jnp.int32,L.shape,1)
     o_ref[:,pl.ds(8*HD,128)]=jnp.where(lane<8,hi.astype(F32),jnp.where(lane<16,mid.astype(F32),jnp.where(lane<24,lo.astype(F32),0.0))).astype(BF)
 
-def attention(pos, lim, q, k0, k1, v0, v1, nk, nv, R=256, CH=512):
-    T=q.shape[0]; KEYS=k0.shape[0]; W=nk.shape[0]//2
+def attention(pos, reach, q, kk, vv, W, R=256, CH=512):
+    T=q.shape[0]; keys=kk.shape[0]
     return pl.pallas_call(
         functools.partial(attn_kernel,R=R,CH=CH,W=W),
         out_shape=jax.ShapeDtypeStruct((T,9*HD),BF),
-        in_specs=[SM]+[VM]*8,
+        in_specs=[SM]+[VM]*4,
         out_specs=VM,
-        scratch_shapes=[pltpu.VMEM((2*KEYS+128,2*HD),BF),pltpu.VMEM((2*KEYS+128,2*HD),BF),
-            pltpu.VMEM((2,R,2*KEYS+128),F32),pltpu.VMEM((R,128),F32),pltpu.VMEM((T,128),F32),pltpu.VMEM((T,128),jnp.int32)],
-        compiler_params=pltpu.CompilerParams(vmem_limit_bytes=42*MIB),
-        cost_estimate=pl.CostEstimate(flops=4*T*8*2*KEYS*HD*2,bytes_accessed=8*1024*1024,transcendentals=T*8*2*KEYS),
-    )(pos,lim,q,k0,k1,v0,v1,nk,nv)
-
-
-def home_kernel(recv_ref, ids_ref, idc_ref, gate_ref, att_ref, msg_ref, mat_ref):
+        scratch_shapes=[pltpu.VMEM((2,R,keys),F32),pltpu.VMEM((R,128),F32),pltpu.VMEM((T,128),F32),pltpu.VMEM((T,128),jnp.int32)],
+        compiler_params=pltpu.CompilerParams(vmem_limit_bytes=36*MIB),
+        cost_estimate=pl.CostEstimate(flops=32*T*keys*HD,bytes_accessed=8*MIB,transcendentals=T*8*keys),
+    )(pos,reach,q,kk,vv)
+
+
+def tables_kernel(k0_ref, k1_ref, v0_ref, v1_ref, nk0_ref, nk1_ref, nv0_ref, nv1_ref, kk_ref, vv_ref):
+    first = 0
+    for keys, values in ((k0_ref, v0_ref), (k1_ref, v1_ref), (nk0_ref, nv0_ref), (nk1_ref, nv1_ref)):
+        count = keys.shape[0]
+        rows = pl.ds(first, count)
+        kk_ref[rows, pl.ds(0, HD)] = keys[...]
+        kk_ref[rows, pl.ds(HD, HD)] = keys[...]
+        vv_ref[rows, pl.ds(0, HD)] = values[...]
+        vv_ref[rows, pl.ds(HD, HD)] = jnp.ones((count, HD), BF)
+        first += count
+    rest = kk_ref.shape[0] - first
+    kk_ref[pl.ds(first, rest), :] = jnp.zeros((rest, 2 * HD), BF)
+    vv_ref[pl.ds(first, rest), :] = jnp.zeros((rest, 2 * HD), BF)
+
+
+def tables(*rows):
+    keys = 2 * rows[0].shape[0] + 128
+    shape = jax.ShapeDtypeStruct((keys, 2 * HD), BF)
+    return pl.pallas_call(
+        tables_kernel,
+        out_shape=(shape, shape),
+        in_specs=[VM] * 8,
+        out_specs=(VM, VM),
+        compiler_params=pltpu.CompilerParams(vmem_limit_bytes=20 * MIB),
+        cost_estimate=pl.CostEstimate(flops=0, bytes_accessed=12 * MIB, transcendentals=0),
+    )(*rows)
+
+
+def home_kernel(recv_ref, ids_ref, gate_ref, att_ref, msg_ref, mat_ref):
     blocks, tok, _ = recv_ref.shape
     heads = att_ref.shape[1] // HD
     logs = []
@@ -151,16 +170,22 @@
             for y in range(msg_ref.shape[1]):
                 for x in range(msg_ref.shape[3]):
                     msg_ref[e, y, c, x] = part
-    gate_matrix(idc_ref, gate_ref, mat_ref, msg_ref.shape[1] * msg_ref.shape[3])
+    gate_matrix(ids_ref, gate_ref, mat_ref, msg_ref.shape[1] * msg_ref.shape[3])
 
 
 def gate_matrix(ids_ref, gate_ref, mat_ref, copies):
-    tok = ids_ref.shape[0]
+    tok = ids_ref.shape[1]
     terms = E * copies * CAP
+    same = lax.broadcasted_iota(jnp.int32, (tok, tok), 0) == lax.broadcasted_iota(jnp.int32, (tok, tok), 1)
+
+    def column(ref, k):
+        row = jnp.broadcast_to(ref[k : k + 1, :], (tok, tok))
+        return jnp.sum(jnp.where(same, row, jnp.zeros_like(row)), axis=1, keepdims=True)
+
     lane = lax.broadcasted_iota(jnp.int32, (tok, terms), 1)
     expert = lax.div(lane, copies * CAP)
-    first, second = ids_ref[:, 0:1] == expert, ids_ref[:, 1:2] == expert
-    gate = jnp.where(first, gate_ref[:, 0:1], 0.0) + jnp.where(second, gate_ref[:, 1:2], 0.0)
+    first, second = column(ids_ref, 0) == expert, column(ids_ref, 1) == expert
+    gate = jnp.where(first, column(gate_ref, 0), 0.0) + jnp.where(second, column(gate_ref, 1), 0.0)
     earlier = lax.broadcasted_iota(jnp.int32, (tok, tok), 1) < lax.broadcasted_iota(jnp.int32, (tok, tok), 0)
     rank = jnp.dot(
         jnp.where(earlier, 1.0, 0.0).astype(BF), jnp.where(first | second, 1.0, 0.0).astype(BF), preferred_element_type=F32
@@ -180,94 +205,133 @@
             jax.ShapeDtypeStruct((E, 2, 2, tp, CAP, width // 2), BF),
             jax.ShapeDtypeStruct((2 * tok, E * 2 * tp * CAP), BF),
         ),
-        in_specs=[VM] * 4,
+        in_specs=[VM] * 3,
         out_specs=(VM, VM, VM),
         compiler_params=pltpu.CompilerParams(vmem_limit_bytes=24 * MIB),
-    )(recv, ids.T, ids, gates)
+    )(recv, ids.T, gates.T)
 
 
 def columns(x, side, half):
     return pl.ds(pl.multiple_of(x * 2 * half + side * half, half), half)
 
 
-def up_part(ref, side, gain_ref, up_ref, total, square):
+def up_part(ref, side, gain_ref, up_ref, w_buf, sems, total, square):
     seqs, tp, cap, half = ref.shape
+    copies = [pltpu.make_async_copy(up_ref.at[columns(x, side, half), :], w_buf.at[x], sems.at[x]) for x in range(tp)]
+    for copy in copies:
+        copy.start()
     for x in range(tp):
         a = ref[:, x].reshape(seqs * cap, half).astype(F32)
         scaled = (a * gain_ref[:, columns(x, side, half)]).astype(BF)
-        total = total + jnp.dot(scaled, up_ref[columns(x, side, half), :], preferred_element_type=F32)
         for c in range(half // 128):
             part = a[:, c * 128 : (c + 1) * 128]
             square = square + part * part
+        copies[x].wait()
+        total = total + jnp.dot(scaled, w_buf[x], preferred_element_type=F32)
     return total, square
 
 
-def up_first_kernel(core_ref, own_ref, gain_ref, up_ref, total_ref, square_ref):
+def up_first_kernel(core_ref, own_ref, gain_ref, up_ref, total_ref, square_ref, w_buf, sems):
     total, square = up_part(
-        own_ref, core_ref[0], gain_ref, up_ref, jnp.zeros(total_ref.shape, F32), jnp.zeros(square_ref.shape, F32)
+        own_ref, core_ref[0], gain_ref, up_ref, w_buf, sems, jnp.zeros(total_ref.shape, F32), jnp.zeros(square_ref.shape, F32)
     )
     total_ref[...] = total
     square_ref[...] = square
 
 
 def up_first(core, own, gain, w_up):
-    rows = own.shape[0] * own.shape[2]
+    rows, tp, half, hid = own.shape[0] * own.shape[2], own.shape[1], own.shape[3], w_up.shape[1]
     return pl.pallas_call(
         up_first_kernel,
         out_shape=(
-            jax.ShapeDtypeStruct((rows, w_up.shape[1]), F32),
+            jax.ShapeDtypeStruct((rows, hid), F32),
             jax.ShapeDtypeStruct((rows, 128), F32),
         ),
-        in_specs=[SM] + [VM] * 3,
+        in_specs=[SM, VM, VM, HBM],
         out_specs=(VM, VM),
+        scratch_shapes=[pltpu.VMEM((tp, half, hid), BF), pltpu.SemaphoreType.DMA((tp,))],
         compiler_params=pltpu.CompilerParams(vmem_limit_bytes=24 * MIB),
-        cost_estimate=pl.CostEstimate(flops=rows * own.shape[3] * 8 * w_up.shape[1], bytes_accessed=8 * MIB, transcendentals=0),
+        cost_estimate=pl.CostEstimate(flops=2 * rows * tp * half * hid, bytes_accessed=5 * MIB, transcendentals=0),
     )(core, own, gain, w_up)
 
 
-def up_second_kernel(core_ref, other_ref, gain_ref, up_ref, down_ref, total_ref, square_ref, hidden_ref, send_ref):
+def up_second_kernel(
+    core_ref, other_ref, gain_ref, up_ref, down_ref, total_ref, square_ref, hidden_ref, send_ref, w_buf, d_buf, sems
+):
     seqs, tp, cap, half = other_ref.shape
     other = 1 - core_ref[0]
-    total, square = up_part(other_ref, other, gain_ref, up_ref, total_ref[...], square_ref[...])
+    copies = [pltpu.make_async_copy(down_ref.at[:, columns(x, other, half)], d_buf.at[x], sems.at[tp + x]) for x in range(tp)]
+    for copy in copies:
+        copy.start()
+    total, square = up_part(other_ref, other, gain_ref, up_ref, w_buf, sems, total_ref[...], square_ref[...])
     mean = jnp.sum(square, axis=1, keepdims=True) / (2 * tp * half)
     total = total * lax.rsqrt(mean + EPSILON)
     hidden = (total / (1.0 + jnp.exp(-total))).astype(BF)
     hidden_ref[...] = hidden
     for x in range(tp):
-        out = jnp.dot(hidden, down_ref[:, columns(x, other, half)], preferred_element_type=F32)
+        copies[x].wait()
+        out = jnp.dot(hidden, d_buf[x], preferred_element_type=F32)
         send_ref[:, x] = out.astype(BF).reshape(seqs, cap, half)
 
 
 def up_second(core, other, gain, w_up, w_down, total, square):
+    tp, half, hid = other.shape[1], other.shape[3], w_up.shape[1]
     return pl.pallas_call(
         up_second_kernel,
         out_shape=(
             jax.ShapeDtypeStruct(total.shape, BF),
             jax.ShapeDtypeStruct(other.shape, BF),
         ),
-        in_specs=[SM] + [VM] * 6,
+        in_specs=[SM, VM, VM, HBM, HBM, VM, VM],
         out_specs=(VM, VM),
-        compiler_params=pltpu.CompilerParams(vmem_limit_bytes=32 * MIB),
+        scratch_shapes=[
+            pltpu.VMEM((tp, half, hid), BF),
+            pltpu.VMEM((tp, hid, half), BF),
+            pltpu.SemaphoreType.DMA((2 * tp,)),
+        ],
+        compiler_params=pltpu.CompilerParams(vmem_limit_bytes=28 * MIB),
     )(core, other, gain, w_up, w_down, total, square)
 
 
-def down_kernel(core_ref, hidden_ref, down_ref, partner_ref, out_ref):
+def down_kernel(core_ref, hidden_ref, down_ref, out_ref, d_buf, sems):
     seqs, tp, cap, half = out_ref.shape
+    copies = [
+        pltpu.make_async_copy(down_ref.at[:, columns(x, core_ref[0], half)], d_buf.at[x], sems.at[x]) for x in range(tp)
+    ]
+    for copy in copies:
+        copy.start()
     hidden = hidden_ref[...]
     for x in range(tp):
-        out = jnp.dot(hidden, down_ref[:, columns(x, core_ref[0], half)], preferred_element_type=F32)
-        out = out + partner_ref[:, x].reshape(seqs * cap, half).astype(F32)
-        out_ref[:, x] = out.astype(BF).reshape(seqs, cap, half)
-
-
-def down_project(core, hidden, w_down, partner):
+        copies[x].wait()
+        out_ref[:, x] = jnp.dot(hidden, d_buf[x], preferred_element_type=F32).reshape(seqs, cap, half)
+
+
+def down_project(core, hidden, w_down, shape):
+    tp, half, hid = shape[1], shape[3], hidden.shape[1]
     return pl.pallas_call(
         down_kernel,
+        out_shape=jax.ShapeDtypeStruct(shape, F32),
+        in_specs=[SM, VM, HBM],
+        out_specs=VM,
+        scratch_shapes=[pltpu.VMEM((tp, hid, half), BF), pltpu.SemaphoreType.DMA((tp,))],
+        compiler_params=pltpu.CompilerParams(vmem_limit_bytes=24 * MIB),
+        cost_estimate=pl.CostEstimate(flops=2 * hidden.shape[0] * tp * half * hid, bytes_accessed=5 * MIB, transcendentals=0),
+    )(core, hidden, w_down)
+
+
+def join_kernel(keep_ref, partner_ref, out_ref):
+    for x in range(out_ref.shape[1]):
+        out_ref[:, x] = (keep_ref[:, x] + partner_ref[:, x].astype(F32)).astype(BF)
+
+
+def join(keep, partner):
+    return pl.pallas_call(
+        join_kernel,
         out_shape=jax.ShapeDtypeStruct(partner.shape, BF),
-        in_specs=[SM] + [VM] * 3,
+        in_specs=[VM] * 2,
         out_specs=VM,
-        compiler_params=pltpu.CompilerParams(vmem_limit_bytes=24 * MIB),
-    )(core, hidden, w_down, partner)
+        compiler_params=pltpu.CompilerParams(vmem_limit_bytes=16 * MIB),
+    )(keep, partner)
 
 
 def mix_kernel(recv_ref, mat_ref, out_ref):
@@ -314,11 +378,10 @@
     limits = lax.dynamic_index_in_dim(reach.reshape(chips, 2, tok), core, 1, keepdims=False)
     limits = limits.reshape(1, chips * tok)
     places = jnp.stack([seq * ctx, partner * ctx, seq * tok, partner * tok, core]).astype(jnp.int32)
-    outs = attention(
-        places, limits, all_queries, cache_keys, other_keys, cache_values, other_values,
-        jnp.concatenate([new_keys, other_new_keys], axis=0),
-        jnp.concatenate([new_values, other_new_values], axis=0),
-    )
+    kk, vv = tables(
+        cache_keys, other_keys, cache_values, other_values, new_keys, other_new_keys, new_values, other_new_values
+    )
+    outs = attention(places, limits, all_queries, kk, vv, tok)
     arrived = lax.all_to_all(
         outs.reshape(chips, tok, outs.shape[1]), "seq", 0, 0, axis_index_groups=same_core, tiled=True
     )
@@ -329,9 +392,11 @@
     ).reshape(seqs, tp, CAP, half)
     side = core.astype(jnp.int32).reshape(1)
     gain = norm_gain.reshape(1, -1)
-    total, square = up_first(side, rows, gain, w_up[0])
-    hidden, send = up_second(side, swapped(rows), gain, w_up[0], w_down[0], total, square)
-    result = down_project(side, hidden, w_down[0], swapped(send))
+    up_rows = pltpu.with_memory_space_constraint(w_up[0], pltpu.HBM)
+    down_rows = pltpu.with_memory_space_constraint(w_down[0], pltpu.HBM)
+    total, square = up_first(side, rows, gain, up_rows)
+    hidden, send = up_second(side, swapped(rows), gain, up_rows, down_rows, total, square)
+    result = join(down_project(side, hidden, down_rows, send.shape), swapped(send))
     returned = lax.all_to_all(
         result.reshape(seqs * tp, CAP, half), ("seq", "tp"), 0, 0, tiled=True
     ).reshape(E, 2, 2, tp, CAP, half)

time: 191 us -> 189 us (0.990)
  waiting for transfers between devices: 35.8 us -> 8.67 us
  blocking collectives: 72.4 us -> 93.9 us
  Pallas kernels: 53.8 us -> 63.9 us
  starting transfers between devices: 15.6 us -> 11 us
    all_to_all x0 -> x1, blocking collectives: none -> 22 us  [per_device(): lax.all_to_all(outs.reshape(chips, tok, outs.shape[1]), 'seq', 0, 0, axis...]
    all_to_all x1 -> x0, waiting for transfers between devices: 16.7 us -> none  [per_device(): lax.all_to_all(outs.reshape(chips, tok, outs.shape[1]), 'seq', 0, 0, axis...]
    pallas_call x2 -> x4, Pallas kernels: 3.65 us -> 11.3 us  [the longest x1 4.57 us: up_first(): pl.pallas_call(up_first_kernel, out_shape=(jax.ShapeDtypeStruct((rows, hi...]
    all_to_all x1, waiting for transfers between devices: 14.2 us -> 7.31 us  [per_device(): lax.all_to_all(jnp.broadcast_to(queries[None], (chips, tok, width)), 'seq...]
    all_to_all x1 -> x0, starting transfers between devices: 4.66 us -> none  [per_device(): lax.all_to_all(outs.reshape(chips, tok, outs.shape[1]), 'seq', 0, 0, axis...]
    pallas_call x1, Pallas kernels: 4.04 us -> 8.12 us  [up_second(): pl.pallas_call(up_second_kernel, out_shape=(jax.ShapeDtypeStruct(total.sh...]
    ppermute x6, waiting for transfers between devices: 4.81 us -> 1.36 us  [swapped(): return lax.ppermute(value, 'seq', swap)]
    unnamed x30 -> x24, local copies, waits for them, and re-layouts: 9.95 us -> 8.45 us
  transfers between devices with their start and end apart: 8 -> 7, of which waited for: 5 -> 4; matrix products, arithmetic and copies ran while one was open for 1% -> 1% of each run, Pallas kernels for 1% -> 6%
where the time goes in v3:
time: 189 us
  blocking collectives  93.9 us (50%)
  Pallas kernels  63.9 us (34%)
  starting transfers between devices  11 us (6%)
  local copies, waits for them, and re-layouts  10.7 us (6%)
  waiting for transfers between devices  8.67 us (5%)
    pallas_call x1, Pallas kernels, attention(): pl.pallas_call(functools.partial(attn_kernel, R=R, CH=CH, W=W), out_shape...  41.7 us
    all_to_all x1, blocking collectives, per_device(): lax.all_to_all(message.reshape(seqs * tp, CAP, half), ('seq', 'tp'), 0, 0...  37.7 us
    all_to_all x1, blocking collectives, per_device(): lax.all_to_all(result.reshape(seqs * tp, CAP, half), ('seq', 'tp'), 0, 0,...  34.2 us
    all_to_all x1, blocking collectives, per_device(): lax.all_to_all(outs.reshape(chips, tok, outs.shape[1]), 'seq', 0, 0, axis...  22 us
    unnamed x24, local copies, waits for them, and re-layouts  8.45 us
    pallas_call x1, Pallas kernels, up_second(): pl.pallas_call(up_second_kernel, out_shape=(jax.ShapeDtypeStruct(total.sh...  8.12 us
    all_to_all x1, starting transfers between devices, per_device(): lax.all_to_all(jnp.broadcast_to(queries[None], (chips, tok, width)), 'seq...  7.85 us
    all_to_all x1, waiting for transfers between devices, per_device(): lax.all_to_all(jnp.broadcast_to(queries[None], (chips, tok, width)), 'seq...  7.31 us
  transfers between devices with their start and end apart: 7, of which 4 were waited for; matrix products, arithmetic and copies ran while one was open for 1% of the time, Pallas kernels for 6%

profile of v3, /device:TPU:1, one launch (start us, length us, event | category | flops | bytes accessed | tf_op | source)
XLA Modules:
  0.0 188.9 jit_solution(3825487123081100860)
XLA Ops:
  0.6 0.0 copy-start
  0.6 0.0 copy-start.1
  0.7 0.0 copy-start.3
  0.7 0.0 copy-start.4
  0.7 0.0 copy-start.11
  0.7 1.5 collective-permute-start
  2.2 0.1 collective-permute-start.1
  2.3 2.0 %broadcast_in_dim.2 = bf16[16,32,1024]{2,1,0:T(8,128)(2,1)} broadcast(bf16[32,1024]{1,0:T(8,128)(2,1)} %param.11), dimensions={1,2} | broadcast | bytes 1114112 | tf_op jit(solution)/shard_map/broadcast_in_dim | solution.py:375
  4.3 7.9 %all-to-all-start = ((bf16[16,32,1024]{2,1,0:T(8,128)(2,1)}), bf16[16,32,1024]{2,1,0:T(8,128)(2,1)S(1)}, u32[]{:S(2)}, u32[]{:S(2)}) async-start(bf16[16,32,1024]{2,1,0:T(8,128)(2,1)} %broadcast_in_dim.2), calls=%async_computation | async-start | bytes 2097152 | tf_op jit(solution)/shard_map/all_to_all | solution.py:374
  12.2 0.0 copy-done.3
  12.2 0.8 collective-permute-start.2
  13.0 0.0 copy-done.4
  13.0 0.1 collective-permute-start.3
  13.1 0.0 copy-done.11
  13.1 0.1 reshape.34
  13.2 0.1 reshape.35.reach_ref
  13.3 0.1 stack.23.pos_ref
  13.4 0.4 collective-permute-done.2.nk1_ref
  13.8 0.3 collective-permute-done.3.nv1_ref
  14.2 0.0 collective-permute-done.k1_ref
  14.2 0.0 collective-permute-done.1.v1_ref
  14.2 0.0 copy-done
  14.2 0.0 copy-done.1
  14.2 2.9 %shard_map.122 = (bf16[8320,256]{1,0:T(8,128)(2,1)S(1)}, bf16[8320,256]{1,0:T(8,128)(2,1)S(1)}) custom-call(bf16[4096,128]{1,0:T(8,128)(2,1)S(1)} %copy-done, bf16[4096,128]{1,0:T(8,128)(2,1)} %collective-permute-done.k1_ref, bf16[4096,128]{1,0:T(8,128)(2,1)S(1)} %copy-done.1, bf16[4096,128]{1,0:T(8,128)(2,1)} %collective-permute-done.1.v1_ref, ...), custom_call_target="tpu_custom_call" | custom-call | bytes 12582912 | tf_op jit(solution)/shard_map/pallas_call | solution.py:129
  17.1 0.0 copy-start.7
  17.1 2.0 %copy-done.7 = bf16[8320,256]{1,0:T(8,128)(2,1)} copy-done((bf16[8320,256]{1,0:T(8,128)(2,1)}, bf16[8320,256]{1,0:T(8,128)(2,1)S(1)}, u32[]{:S(2)}) %copy-start.7) | copy-done | bytes 4259864
  19.0 2.0 %copy-done.9 = bf16[8320,256]{1,0:T(8,128)(2,1)} copy-done((bf16[8320,256]{1,0:T(8,128)(2,1)}, bf16[8320,256]{1,0:T(8,128)(2,1)S(1)}, u32[]{:S(2)}) %copy-start.9) | copy-done | bytes 4259864
  21.1 7.3 %all-to-all-done = bf16[16,32,1024]{2,1,0:T(8,128)(2,1)S(1)} async-done(((bf16[16,32,1024]{2,1,0:T(8,128)(2,1)}), bf16[16,32,1024]{2,1,0:T(8,128)(2,1)S(1)}, u32[]{:S(2)}, u32[]{:S(2)}) %all-to-all-start) | async-done | bytes 1048608 | tf_op jit(solution)/shard_map/all_to_all | solution.py:374
  28.4 2.2 %copy-done.8 = bf16[8320,256]{1,0:T(8,128)(2,1)S(1)} copy-done((bf16[8320,256]{1,0:T(8,128)(2,1)S(1)}, bf16[8320,256]{1,0:T(8,128)(2,1)}, u32[]{:S(2)}) %copy-start.8) | copy-done | bytes 4259864
  30.6 2.2 %copy-done.10 = bf16[8320,256]{1,0:T(8,128)(2,1)S(1)} copy-done((bf16[8320,256]{1,0:T(8,128)(2,1)S(1)}, bf16[8320,256]{1,0:T(8,128)(2,1)}, u32[]{:S(2)}) %copy-start.10) | copy-done | bytes 4259864
  32.8 41.7 %shard_map.123 = bf16[512,1152]{1,0:T(8,128)(2,1)S(1)} custom-call(s32[5]{0:T(128)S(1)} %stack.23.pos_ref, s32[1,512]{1,0:T(1,128)S(1)} %reshape.35.reach_ref, bf16[512,1024]{1,0:T(8,128)(2,1)S(1)} %bitcast.22, bf16[8320,256]{1,0:T(8,128)(2,1)S(1)} %copy-done.8, bf16[8320,256]{1,0:T(8,128)(2,1)S(1)} %copy-done.10), custom_call_target="tpu_custom_call" | custom-call | flops 17448304640 | bytes 8388608 | tf_op jit(solution)/shard_map/pallas_call | solution.py:100
  74.6 0.0 copy-start.5
  74.6 0.0 copy-start.6
  74.6 22.0 %all_to_all.20.recv_ref = bf16[16,32,1152]{2,1,0:T(8,128)(2,1)S(1)} all-to-all(bf16[16,32,1152]{2,1,0:T(8,128)(2,1)S(1)} %bitcast.21), channel_id=1, replica_groups={{0,8,16,24,32,40,48,56,64,72,80,88,96,104,112,120},{4,12,20,28,36,44,52..., dimensions={0} | all-to-all | bytes 2359296 | tf_op jit(solution)/shard_map/all_to_all | solution.py:385
  96.5 0.0 copy-done.5
  96.5 0.0 copy-done.6
  96.5 1.6 shard_map.124
  98.2 37.7 %all_to_all.21 = bf16[128,16,512]{2,1,0:T(8,128)(2,1)S(1)} all-to-all(bf16[128,16,512]{2,1,0:T(8,128)(2,1)S(1)} %bitcast.20), channel_id=1, replica_groups=mesh['seq'=32,'tp'=4] {'seq','tp'}, dimensions={0} | all-to-all | bytes 4194304 | tf_op jit(solution)/shard_map/all_to_all | solution.py:390
  135.9 0.4 collective-permute-start.4
  136.3 4.6 %shard_map.125 = (f32[512,768]{1,0:T(8,128)S(1)}, f32[512,128]{1,0:T(8,128)S(1)}) custom-call(s32[1]{0:T(128)} %bitcast.4.core_ref, bf16[32,4,16,512]{3,2,1,0:T(8,128)(2,1)S(1)} %bitcast.18, f32[1,4096]{1,0:T(1,128)S(1)} %bitcast.23, bf16[4096,768]{1,0:T(8,128)(2,1)} %bitcast.27), custom_call_target="tpu_custom_call" | custom-call | flops 1610612736 | bytes 5242880 | tf_op jit(solution)/shard_map/pallas_call | solution.py:244
  140.9 0.0 collective-permute-done.4.other_ref
  140.9 8.1 %shard_map.126 = (bf16[512,768]{1,0:T(8,128)(2,1)S(1)}, bf16[32,4,16,512]{3,2,1,0:T(8,128)(2,1)S(1)}) custom-call(s32[1]{0:T(128)} %bitcast.4.core_ref, bf16[32,4,16,512]{3,2,1,0:T(8,128)(2,1)S(1)} %collective-permute-done.4.other_ref, f32[1,4096]{1,0:T(1,128)S(1)} %bitcast.24, bf16[4096,768]{1,0:T(8,128)(2,1)} %bitcast.28, bf16[768,4096]{1,0:T(8,128)(2,1)} %bitcast.29, ...), custom_call_target="tpu_custom_call" | custom-call | tf_op jit(solution)/shard_map/pallas_call | solution.py:279
  149.0 0.2 collective-permute-start.5
  149.2 3.5 %shard_map.127.keep_ref = f32[32,4,16,512]{3,2,1,0:T(8,128)S(1)} custom-call(s32[1]{0:T(128)} %bitcast.4.core_ref, bf16[512,768]{1,0:T(8,128)(2,1)S(1)} %get-tuple-element.17.hidden_ref, bf16[768,4096]{1,0:T(8,128)(2,1)} %bitcast.30), custom_call_target="tpu_custom_call" | custom-call | flops 1610612736 | bytes 5242880 | tf_op jit(solution)/shard_map/pallas_call | solution.py:311
  152.7 0.6 collective-permute-done.5.partner_ref
  153.2 0.3 shard_map.128
  153.6 34.2 %all_to_all.22 = bf16[128,16,512]{2,1,0:T(8,128)(2,1)S(1)} all-to-all(bf16[128,16,512]{2,1,0:T(8,128)(2,1)S(1)} %bitcast.19), channel_id=1, replica_groups=mesh['seq'=32,'tp'=4] {'seq','tp'}, dimensions={0} | all-to-all | bytes 4194304 | tf_op jit(solution)/shard_map/all_to_all | solution.py:400
  187.8 1.1 shard_map.129
  (6 shorter events, 0.0 us)
Async XLA Ops:
  0.6 13.5 %copy-start = (bf16[4096,128]{1,0:T(8,128)(2,1)S(1)}, bf16[4096,128]{1,0:T(8,128)(2,1)}, u32[]{:S(2)}) copy-start(bf16[4096,128]{1,0:T(8,128)(2,1)} %k0_ref.1) | copy-start | bytes 3145732
  0.6 13.5 %copy-start.1 = (bf16[4096,128]{1,0:T(8,128)(2,1)S(1)}, bf16[4096,128]{1,0:T(8,128)(2,1)}, u32[]{:S(2)}) copy-start(bf16[4096,128]{1,0:T(8,128)(2,1)} %v0_ref.1) | copy-start | bytes 3145732
  0.7 11.5 %copy-start.3 = (bf16[32,128]{1,0:T(8,128)(2,1)S(1)}, bf16[32,128]{1,0:T(8,128)(2,1)}, u32[]{:S(2)}) copy-start(bf16[32,128]{1,0:T(8,128)(2,1)} %nk0_ref.1) | copy-start | bytes 24580
  0.7 12.3 %copy-start.4 = (bf16[32,128]{1,0:T(8,128)(2,1)S(1)}, bf16[32,128]{1,0:T(8,128)(2,1)}, u32[]{:S(2)}) copy-start(bf16[32,128]{1,0:T(8,128)(2,1)} %nv0_ref.1) | copy-start | bytes 24580
  0.7 12.4 %copy-start.11 = (s32[1024]{0:T(1024)S(1)}, s32[1024]{0:T(1024)}, u32[]{:S(2)}) copy-start(s32[1024]{0:T(1024)} %param.16) | copy-start | bytes 12292
  0.7 13.5 %collective-permute-start = (bf16[4096,128]{1,0:T(8,128)(2,1)}, bf16[4096,128]{1,0:T(8,128)(2,1)}, u32[]{:S(2)}, u32[]{:S(2)}) collective-permute-start(bf16[4096,128]{1,0:T(8,128)(2,1)} %k0_ref.1), channel_id=1, source_target_pairs={{0,4},{4,0},{8,12},{12,8},{16,20},{20,16},{24,28},{28,24},{32,36},... | collective-permute-start | bytes 3145736 | tf_op jit(solution)/shard_map/ppermute | solution.py:370
  2.2 12.0 %collective-permute-start.1 = (bf16[4096,128]{1,0:T(8,128)(2,1)}, bf16[4096,128]{1,0:T(8,128)(2,1)}, u32[]{:S(2)}, u32[]{:S(2)}) collective-permute-start(bf16[4096,128]{1,0:T(8,128)(2,1)} %v0_ref.1), channel_id=1, source_target_pairs={{0,4},{4,0},{8,12},{12,8},{16,20},{20,16},{24,28},{28,24},{32,36},... | collective-permute-start | bytes 3145736 | tf_op jit(solution)/shard_map/ppermute | solution.py:370
  4.3 24.1 %all-to-all-start = ((bf16[16,32,1024]{2,1,0:T(8,128)(2,1)}), bf16[16,32,1024]{2,1,0:T(8,128)(2,1)S(1)}, u32[]{:S(2)}, u32[]{:S(2)}) async-start(bf16[16,32,1024]{2,1,0:T(8,128)(2,1)} %broadcast_in_dim.2), calls=%async_computation | async-start | bytes 2097152 | tf_op jit(solution)/shard_map/all_to_all | solution.py:374
  12.2 1.6 collective-permute-start.2
  13.0 1.2 collective-permute-start.3
  17.1 2.0 %copy-start.7 = (bf16[8320,256]{1,0:T(8,128)(2,1)}, bf16[8320,256]{1,0:T(8,128)(2,1)S(1)}, u32[]{:S(2)}) copy-start(bf16[8320,256]{1,0:T(8,128)(2,1)S(1)} %get-tuple-element.11.kk) | copy-start | bytes 12779524
  19.0 2.0 %copy-start.9 = (bf16[8320,256]{1,0:T(8,128)(2,1)}, bf16[8320,256]{1,0:T(8,128)(2,1)S(1)}, u32[]{:S(2)}) copy-start(bf16[8320,256]{1,0:T(8,128)(2,1)S(1)} %get-tuple-element.12.vv) | copy-start | bytes 12779524
  28.4 2.2 %copy-start.8 = (bf16[8320,256]{1,0:T(8,128)(2,1)S(1)}, bf16[8320,256]{1,0:T(8,128)(2,1)}, u32[]{:S(2)}) copy-start(bf16[8320,256]{1,0:T(8,128)(2,1)} %copy-done.7) | copy-start | bytes 12779524
  30.6 2.2 %copy-start.10 = (bf16[8320,256]{1,0:T(8,128)(2,1)S(1)}, bf16[8320,256]{1,0:T(8,128)(2,1)}, u32[]{:S(2)}) copy-start(bf16[8320,256]{1,0:T(8,128)(2,1)} %copy-done.9) | copy-start | bytes 12779524
  74.6 22.0 %copy-start.5 = (s32[32,2]{0,1:T(2,128)S(1)}, s32[32,2]{0,1:T(2,128)}, u32[]{:S(2)}) copy-start(s32[32,2]{0,1:T(2,128)} %param.19) | copy-start | bytes 772
  74.6 22.0 %copy-start.6 = (f32[32,2]{0,1:T(2,128)S(1)}, f32[32,2]{0,1:T(2,128)}, u32[]{:S(2)}) copy-start(f32[32,2]{0,1:T(2,128)} %param.18) | copy-start | bytes 772
  98.2 38.1 %copy-start.2 = (f32[4096]{0:T(1024)S(1)}, f32[4096]{0:T(1024)}, u32[]{:S(2)}) copy-start(f32[4096]{0:T(1024)} %param.17) | copy-start | bytes 49156
  135.9 5.0 %collective-permute-start.4 = (bf16[32,4,16,512]{3,2,1,0:T(8,128)(2,1)S(1)}, bf16[32,4,16,512]{3,2,1,0:T(8,128)(2,1)S(1)}, u32[]{:S(2)}, u32[]{:S(2)}) collective-permute-start(bf16[32,4,16,512]{3,2,1,0:T(8,128)(2,1)S(1)} %bitcast.17), channel_id=1, source_target_pairs={{0,4},{4,0},{8,12},{12,8},{16,20},{20,16},{24,28},{28,24},{32,36},... | collective-permute-start | bytes 6291464 | tf_op jit(solution)/shard_map/ppermute | solution.py:370
  149.0 4.2 %collective-permute-start.5 = (bf16[32,4,16,512]{3,2,1,0:T(8,128)(2,1)S(1)}, bf16[32,4,16,512]{3,2,1,0:T(8,128)(2,1)S(1)}, u32[]{:S(2)}, u32[]{:S(2)}) collective-permute-start(bf16[32,4,16,512]{3,2,1,0:T(8,128)(2,1)S(1)} %get-tuple-element.18), channel_id=1, source_target_pairs={{0,4},{4,0},{8,12},{12,8},{16,20},{20,16},{24,28},{28,24},{32,36},... | collective-permute-start | bytes 6291464 | tf_op jit(solution)/shard_map/ppermute | solution.py:370

commit v4 on v3

v4 whole, which is shorter than its diff:
```python
import functools
import math

import jax
import jax.numpy as jnp
from jax import lax
from jax.experimental import pallas as pl
from jax.experimental.pallas import tpu as pltpu
from jax.sharding import PartitionSpec as P

HD = 128
E = 8
CAP = 16
EPSILON = 1e-05
NEG = -1e30
FLOOR = -1e20
BF = jnp.bfloat16
F32 = jnp.float32
SCALE = HD**-0.5 * math.log2(math.e)
MIB = 1024 * 1024
VM = pl.BlockSpec(memory_space=pltpu.VMEM)
HBM = pl.BlockSpec(memory_space=pltpu.HBM)

def attn_kernel(*refs, parts, earlier, CH):
    reach_ref = refs[0]
    q_refs, refs = refs[1 : 1 + parts], refs[1 + parts :]
    (k0_ref, v0_ref, k1_ref, v1_ref, n0_ref, n1_ref), refs = refs[:6], refs[6:]
    if earlier:
        prev_ref, refs = refs[0], refs[1:]
    o_ref, q_all, kk, vv, k_own, v_own, s_scr, m_scr, l_scr, lim_ref, tok_ref, sems = refs
    copies = [pltpu.make_async_copy(k0_ref, k_own, sems.at[0]), pltpu.make_async_copy(v0_ref, v_own, sems.at[1])]
    for copy in copies:
        copy.start(priority=1)
    tokens = q_refs[0].shape[0]
    W = n0_ref.shape[0] // 2
    blocks = tokens // W
    T = parts * tokens
    KEYS = k_own.shape[0]
    WIN = 2 * KEYS
    NCH = KEYS // CH
    R = 2 * tokens
    NT = parts * 4
    side = blocks
    seq = lax.axis_index("seq")
    core = lax.rem(seq, 2)
    partner = seq + 1 - 2 * core
    z, y = lax.div(seq, 2 * side), lax.rem(lax.div(seq, 2), side)

    def block(b):
        return lax.rem(z + b // side, side) * side + lax.rem(y + b % side, side)

    def fill(rows, keys, values):
        kk[rows, pl.ds(0, HD)] = keys
        kk[rows, pl.ds(HD, HD)] = keys
        vv[rows, pl.ds(0, HD)] = values
        vv[rows, pl.ds(HD, HD)] = jnp.ones_like(values)

    for p in range(parts):
        rows = pl.ds(p * tokens, tokens)
        q_all[rows, :] = q_refs[p][...]
        lim_ref[rows, :] = jnp.transpose(jnp.broadcast_to(reach_ref[:, p * tokens : (p + 1) * tokens], (128, tokens)))
    for b in range(T // W):
        tok_ref[pl.ds(b * W, W), :] = lax.broadcasted_iota(jnp.int32, (W, 128), 0) + (
            block(b + blocks * earlier) * 2 + core
        ) * W
    l_scr[...] = jnp.zeros_like(l_scr)
    if earlier:
        for b in range(blocks):
            o_ref[pl.ds(pl.multiple_of(block(b) * W, W), W), :] = prev_ref[pl.ds(b * W, W), :]
    fill(pl.ds(KEYS, KEYS), k1_ref[...], v1_ref[...])
    fill(pl.ds(WIN, W), n0_ref[pl.ds(0, W), :], n0_ref[pl.ds(W, W), :])
    fill(pl.ds(WIN + W, W), n1_ref[pl.ds(0, W), :], n1_ref[pl.ds(W, W), :])
    rest = pl.ds(WIN + 2 * W, 128 - 2 * W)
    fill(rest, jnp.zeros((128 - 2 * W, HD), BF), jnp.zeros((128 - 2 * W, HD), BF))
    for copy in copies:
        copy.wait()
    fill(pl.ds(0, KEYS), k_own[...], v_own[...])

    def target(i, b):
        if not earlier:
            return pl.multiple_of((lax.div(i, 4) * blocks + b) * W, W)
        place = lax.rem(z + lax.div(i, 4) + 1, side) * side + lax.rem(y + b, side)
        return pl.multiple_of(place * W, W)

    def tile(i):
        return pl.multiple_of(lax.div(i, 4) * tokens, tokens), lax.rem(i, 4) * 2

    def twice(x):
        return jnp.concatenate([x, x], axis=0)

    def load_q(i):
        r, h = tile(i)
        out = []
        for k in range(2):
            qf = q_all[pl.ds(r, tokens), pl.ds(pl.multiple_of((h + k) * HD, HD), HD)].astype(F32) * SCALE
            hi = qf.astype(BF)
            out.append(jnp.concatenate([hi, (qf - hi.astype(F32)).astype(BF)], axis=1))
        return jnp.concatenate(out, axis=0)

    def dotk(qq, k):
        return lax.dot_general(qq, k, (((1,), (1,)), ((), ())), preferred_element_type=F32)

    def window_scores(i, qq):
        r, _ = tile(i)
        s = dotk(qq, kk[pl.ds(WIN, 128), :])
        lane = lax.broadcasted_iota(jnp.int32, (R, 128), 1)
        key = jnp.where(lane < W, lane + seq * W, lane - W + partner * W)
        return jnp.where((lane < 2 * W) & (key <= twice(tok_ref[pl.ds(r, tokens), :])), s, NEG)

    def step(i, do_qk, do_pv):
        if do_qk:
            qq = load_q(i + 1)
            r1, _ = tile(i + 1)
            lim = twice(lim_ref[pl.ds(r1, tokens), :])
            lane0 = lax.broadcasted_iota(jnp.int32, (R, 128), 1)
            sw = window_scores(i + 1, qq)
            mx = jnp.maximum(sw, FLOOR)
        if do_pv:
            m = m_scr[...]
            p = jnp.exp2(s_scr[:, pl.ds(WIN, 128)] - m)
            acc = jnp.dot(p.astype(BF), vv[pl.ds(WIN, 128), :], preferred_element_type=F32)
        if do_qk:
            s_scr[:, pl.ds(WIN, 128)] = sw
        for half in range(2):
            if do_qk:
                limh = lim - (seq, partner)[half] * KEYS
            for j in range(NCH):
                ks = half * KEYS + j * CH
                if do_pv:
                    p = jnp.concatenate(
                        [jnp.exp2(s_scr[:, pl.ds(ks + c * 128, 128)] - m).astype(BF) for c in range(CH // 128)], axis=1
                    )
                    acc = acc + jnp.dot(p, vv[pl.ds(ks, CH), :], preferred_element_type=F32)
                if do_qk:
                    s = dotk(qq, kk[pl.ds(ks, CH), :])
                    for c in range(CH // 128):
                        sc = jnp.where(lane0 + (j * CH + c * 128) < limh, s[:, c * 128 : (c + 1) * 128], NEG)
                        s_scr[:, pl.ds(ks + c * 128, 128)] = sc
                        mx = jnp.maximum(mx, sc)
        if do_pv:
            r, h = tile(i)
            l = acc[:, HD:]
            out = (acc[:, :HD] / jnp.maximum(l, 1.0)).astype(BF)
            L = jnp.where(l > 0, m + jnp.log2(jnp.maximum(l, 1e-30)), NEG)
            lane = lax.rem(lax.broadcasted_iota(jnp.int32, (tokens, 128), 1), 8)
            old = l_scr[pl.ds(r, tokens), :]
            for k in range(2):
                old = jnp.where(lane == h + k, L[k * tokens : (k + 1) * tokens], old)
                cols = pl.ds(pl.multiple_of((h + k) * HD, HD), HD)
                for b in range(blocks):
                    o_ref[pl.ds(target(i, b), W), cols] = out[k * tokens + b * W : k * tokens + (b + 1) * W]
            l_scr[pl.ds(r, tokens), :] = old
        if do_qk:
            m_scr[...] = jnp.broadcast_to(jnp.max(mx, axis=1, keepdims=True), (R, 128))

    step(jnp.int32(-1), True, False)

    def both(i, _):
        step(i, True, True)
        return 0

    lax.fori_loop(0, NT - 1, both, 0)
    step(jnp.int32(NT - 1), False, True)
    L = l_scr[...]
    hi = L.astype(BF).astype(F32)
    mid = (L - hi).astype(BF).astype(F32)
    lane = lax.broadcasted_iota(jnp.int32, L.shape, 1)
    packed = jnp.where(lane < 8, hi, jnp.where(lane < 16, mid, jnp.where(lane < 24, L - hi - mid, 0.0))).astype(BF)
    for b in range(T // W):
        place = block(b + blocks) if earlier else b
        o_ref[pl.ds(pl.multiple_of(place * W, W), W), pl.ds(8 * HD, 128)] = packed[b * W : (b + 1) * W]


def attention(reach, qs, tables, prev=None, CH=512):
    tokens = qs[0].shape[0]
    T = len(qs) * tokens
    keys = 2 * tables[0].shape[0] + 128
    rows = T + (0 if prev is None else tokens)
    more = () if prev is None else (prev,)
    return pl.pallas_call(
        functools.partial(attn_kernel, parts=len(qs), earlier=prev is not None, CH=CH),
        out_shape=jax.ShapeDtypeStruct((rows, 9 * HD), BF),
        in_specs=[VM] * (1 + len(qs)) + [HBM] * 2 + [VM] * (4 + len(more)),
        out_specs=VM,
        scratch_shapes=[
            pltpu.VMEM((T, 8 * HD), BF),
            pltpu.VMEM((keys, 2 * HD), BF),
            pltpu.VMEM((keys, 2 * HD), BF),
            pltpu.VMEM(tables[0].shape, BF),
            pltpu.VMEM(tables[0].shape, BF),
            pltpu.VMEM((2 * tokens, keys), F32),
            pltpu.VMEM((2 * tokens, 128), F32),
            pltpu.VMEM((T, 128), F32),
            pltpu.VMEM((T, 128), jnp.int32),
            pltpu.VMEM((T, 128), jnp.int32),
            pltpu.SemaphoreType.DMA((2,)),
        ],
        compiler_params=pltpu.CompilerParams(vmem_limit_bytes=36 * MIB),
        cost_estimate=pl.CostEstimate(flops=32 * T * keys * HD, bytes_accessed=8 * MIB, transcendentals=T * 8 * keys),
    )(reach, *qs, *tables, *more)


def home_kernel(recv_ref, ids_ref, gate_ref, att_ref, msg_ref, mat_ref):
    blocks, tok, _ = recv_ref.shape
    heads = att_ref.shape[1] // HD
    logs = []
    for s in range(blocks):
        tail = recv_ref[s, :, pl.ds(heads * HD, 128)].astype(F32)
        logs.append(tail + pltpu.roll(tail, 120, 1) + pltpu.roll(tail, 112, 1))
    top = functools.reduce(jnp.maximum, logs)
    shares = [jnp.exp2(x - top) for x in logs]
    inverse = 1.0 / functools.reduce(jnp.add, shares)
    shares = [x * inverse for x in shares]
    for h in range(heads):
        total = jnp.zeros((tok, HD), F32)
        for s in range(blocks):
            total = total + shares[s][:, h : h + 1] * recv_ref[s, :, pl.ds(h * HD, HD)].astype(F32)
        att_ref[:, pl.ds(h * HD, HD)] = total.astype(BF)
    slot = lax.broadcasted_iota(jnp.int32, (E * CAP, tok), 0)
    expert = lax.div(slot, CAP)
    member = (ids_ref[0:1, :] == expert) | (ids_ref[1:2, :] == expert)
    earlier = lax.broadcasted_iota(jnp.int32, (tok, tok), 0) < lax.broadcasted_iota(jnp.int32, (tok, tok), 1)
    rank = jnp.dot(
        jnp.where(member, 1.0, 0.0).astype(BF), jnp.where(earlier, 1.0, 0.0).astype(BF), preferred_element_type=F32
    )
    placing = member & (rank == lax.rem(slot, CAP).astype(F32))
    rows = jnp.dot(
        jnp.where(placing, 1.0, 0.0).astype(BF), att_ref[...], preferred_element_type=F32
    ).astype(BF)
    half = rows.shape[1] // 2
    for e in range(E):
        for c in range(2):
            part = rows[e * CAP : (e + 1) * CAP, c * half : (c + 1) * half]
            for y in range(msg_ref.shape[1]):
                for x in range(msg_ref.shape[3]):
                    msg_ref[e, y, c, x] = part
    gate_matrix(ids_ref, gate_ref, mat_ref, msg_ref.shape[1] * msg_ref.shape[3])


def gate_matrix(ids_ref, gate_ref, mat_ref, copies):
    tok = ids_ref.shape[1]
    terms = E * copies * CAP
    same = lax.broadcasted_iota(jnp.int32, (tok, tok), 0) == lax.broadcasted_iota(jnp.int32, (tok, tok), 1)

    def column(ref, k):
        row = jnp.broadcast_to(ref[k : k + 1, :], (tok, tok))
        return jnp.sum(jnp.where(same, row, jnp.zeros_like(row)), axis=1, keepdims=True)

    lane = lax.broadcasted_iota(jnp.int32, (tok, terms), 1)
    expert = lax.div(lane, copies * CAP)
    first, second = column(ids_ref, 0) == expert, column(ids_ref, 1) == expert
    gate = jnp.where(first, column(gate_ref, 0), 0.0) + jnp.where(second, column(gate_ref, 1), 0.0)
    earlier = lax.broadcasted_iota(jnp.int32, (tok, tok), 1) < lax.broadcasted_iota(jnp.int32, (tok, tok), 0)
    rank = jnp.dot(
        jnp.where(earlier, 1.0, 0.0).astype(BF), jnp.where(first | second, 1.0, 0.0).astype(BF), preferred_element_type=F32
    )
    gate = jnp.where(rank == lax.rem(lane, CAP).astype(F32), gate, 0.0)
    high = gate.astype(BF)
    mat_ref[pl.ds(0, tok), :] = high
    mat_ref[pl.ds(tok, tok), :] = (gate - high.astype(F32)).astype(BF)


def home(recv, ids, gates, tp):
    tok, width = recv.shape[1], recv.shape[2] - 128
    return pl.pallas_call(
        home_kernel,
        out_shape=(
            jax.ShapeDtypeStruct((tok, width), BF),
            jax.ShapeDtypeStruct((E, 2, 2, tp, CAP, width // 2), BF),
            jax.ShapeDtypeStruct((2 * tok, E * 2 * tp * CAP), BF),
        ),
        in_specs=[VM] * 3,
        out_specs=(VM, VM, VM),
        compiler_params=pltpu.CompilerParams(vmem_limit_bytes=24 * MIB),
    )(recv, ids.T, gates.T)


def columns(x, side, half):
    return pl.ds(pl.multiple_of(x * 2 * half + side * half, half), half)


def this_core():
    return lax.rem(lax.axis_index("seq"), 2)


def start_rows(up_ref, w_buf, side, sems):
    half = w_buf.shape[1]
    copies = [pltpu.make_async_copy(up_ref.at[columns(x, side, half), :], w_buf.at[x], sems.at[x]) for x in range(w_buf.shape[0])]
    for copy in copies:
        copy.start()
    return copies


def start_columns(down_ref, d_buf, side, sems):
    half = d_buf.shape[2]
    copies = [pltpu.make_async_copy(down_ref.at[:, columns(x, side, half)], d_buf.at[x], sems.at[x]) for x in range(d_buf.shape[0])]
    for copy in copies:
        copy.start()
    return copies


def up_part(ref, side, gain_ref, s_buf, w_buf, copies, square):
    seqs, tp, cap, half = ref.shape
    for x in range(tp):
        a = ref[:, x].reshape(seqs * cap, half).astype(F32)
        s_buf[:, pl.ds(x * half, half)] = (a * gain_ref[:, columns(x, side, half)]).astype(BF)
        for c in range(half // 128):
            part = a[:, c * 128 : (c + 1) * 128]
            square = square + part * part
    for copy in copies:
        copy.wait()
    weights = w_buf[...].reshape(tp * half, w_buf.shape[2])
    return jnp.dot(s_buf[...], weights, preferred_element_type=F32), square


def up_first_kernel(own_ref, gain_ref, up_ref, total_ref, square_ref, s_buf, w_buf, sems):
    copies = start_rows(up_ref, w_buf, this_core(), sems)
    total, square = up_part(own_ref, this_core(), gain_ref, s_buf, w_buf, copies, jnp.zeros(square_ref.shape, F32))
    total_ref[...] = total
    square_ref[...] = square


def up_first(own, gain, w_up):
    rows, tp, half, hid = own.shape[0] * own.shape[2], own.shape[1], own.shape[3], w_up.shape[1]
    return pl.pallas_call(
        up_first_kernel,
        out_shape=(
            jax.ShapeDtypeStruct((rows, hid), F32),
            jax.ShapeDtypeStruct((rows, 128), F32),
        ),
        in_specs=[VM, VM, HBM],
        out_specs=(VM, VM),
        scratch_shapes=[
            pltpu.VMEM((rows, tp * half), BF),
            pltpu.VMEM((tp, half, hid), BF),
            pltpu.SemaphoreType.DMA((tp,)),
        ],
        compiler_params=pltpu.CompilerParams(vmem_limit_bytes=24 * MIB),
        cost_estimate=pl.CostEstimate(flops=2 * rows * tp * half * hid, bytes_accessed=5 * MIB, transcendentals=0),
    )(own, gain, w_up)


def up_second_kernel(
    other_ref, gain_ref, up_ref, down_ref, total_ref, square_ref, hidden_ref, send_ref, s_buf, w_buf, d_buf, sems, d_sems
):
    seqs, tp, cap, half = other_ref.shape
    other = 1 - this_core()
    copies = start_rows(up_ref, w_buf, other, sems)
    down_copies = start_columns(down_ref, d_buf, other, d_sems)
    total, square = up_part(other_ref, other, gain_ref, s_buf, w_buf, copies, square_ref[...])
    mean = jnp.sum(square, axis=1, keepdims=True) / (2 * tp * half)
    total = (total + total_ref[...]) * lax.rsqrt(mean + EPSILON)
    hidden = (total / (1.0 + jnp.exp(-total))).astype(BF)
    hidden_ref[...] = hidden
    for copy in down_copies:
        copy.wait()
    for x in range(tp):
        out = jnp.dot(hidden, d_buf[x], preferred_element_type=F32)
        send_ref[:, x] = out.astype(BF).reshape(seqs, cap, half)


def up_second(other, gain, w_up, w_down, total, square):
    rows, tp, half, hid = total.shape[0], other.shape[1], other.shape[3], w_up.shape[1]
    return pl.pallas_call(
        up_second_kernel,
        out_shape=(
            jax.ShapeDtypeStruct(total.shape, BF),
            jax.ShapeDtypeStruct(other.shape, BF),
        ),
        in_specs=[VM, VM, HBM, HBM, VM, VM],
        out_specs=(VM, VM),
        scratch_shapes=[
            pltpu.VMEM((rows, tp * half), BF),
            pltpu.VMEM((tp, half, hid), BF),
            pltpu.VMEM((tp, hid, half), BF),
            pltpu.SemaphoreType.DMA((tp,)),
            pltpu.SemaphoreType.DMA((tp,)),
        ],
        compiler_params=pltpu.CompilerParams(vmem_limit_bytes=30 * MIB),
    )(other, gain, w_up, w_down, total, square)


def down_kernel(hidden_ref, down_ref, out_ref, d_buf, sems):
    seqs, tp, cap, half = out_ref.shape
    copies = start_columns(down_ref, d_buf, this_core(), sems)
    hidden = hidden_ref[...]
    for copy in copies:
        copy.wait()
    for x in range(tp):
        out_ref[:, x] = jnp.dot(hidden, d_buf[x], preferred_element_type=F32).reshape(seqs, cap, half)


def down_project(hidden, w_down, shape):
    tp, half, hid = shape[1], shape[3], hidden.shape[1]
    return pl.pallas_call(
        down_kernel,
        out_shape=jax.ShapeDtypeStruct(shape, F32),
        in_specs=[VM, HBM],
        out_specs=VM,
        scratch_shapes=[pltpu.VMEM((tp, hid, half), BF), pltpu.SemaphoreType.DMA((tp,))],
        compiler_params=pltpu.CompilerParams(vmem_limit_bytes=24 * MIB),
        cost_estimate=pl.CostEstimate(flops=2 * hidden.shape[0] * tp * half * hid, bytes_accessed=5 * MIB, transcendentals=0),
    )(hidden, w_down)


def join_kernel(keep_ref, partner_ref, out_ref):
    for x in range(out_ref.shape[1]):
        out_ref[:, x] = (keep_ref[:, x] + partner_ref[:, x].astype(F32)).astype(BF)


def join(keep, partner):
    return pl.pallas_call(
        join_kernel,
        out_shape=jax.ShapeDtypeStruct(partner.shape, BF),
        in_specs=[VM] * 2,
        out_specs=VM,
        compiler_params=pltpu.CompilerParams(vmem_limit_bytes=16 * MIB),
    )(keep, partner)


def mix_kernel(recv_ref, mat_ref, out_ref):
    experts, pair, cores, tp, cap, half = recv_ref.shape
    tok = out_ref.shape[0]
    for c in range(cores):
        values = recv_ref[:, :, c].reshape(experts * pair * tp * cap, half)
        out = jnp.dot(mat_ref[...], values, preferred_element_type=F32)
        out_ref[:, pl.ds(c * half, half)] = (out[:tok] + out[tok:]).astype(BF)


def mix(recv, matrix):
    return pl.pallas_call(
        mix_kernel,
        out_shape=jax.ShapeDtypeStruct((matrix.shape[0] // 2, 2 * recv.shape[5]), BF),
        in_specs=[VM] * 2,
        out_specs=VM,
        compiler_params=pltpu.CompilerParams(vmem_limit_bytes=24 * MIB),
    )(recv, matrix)


def per_device(
    queries, cache_keys, cache_values, new_keys, new_values, reach, norm_gain, gate_weights, expert_ids, w_up, w_down
):
    seqs, tp = lax.axis_size("seq"), lax.axis_size("tp")
    seq = lax.axis_index("seq")
    core = lax.rem(seq, 2)
    tok, width = queries.shape
    chips = seqs // 2
    same_core = [list(range(c, seqs, 2)) for c in range(2)]
    swap = [(i, i ^ 1) for i in range(seqs)]

    def swapped(value):
        return lax.ppermute(value, "seq", swap)

    def moved(value, dz, dy):
        pairs = []
        for i in range(seqs):
            z, y, c = i // 2 // side, i // 2 % side, i % 2
            pairs.append((i, (((z - dz) % side) * side + (y - dy) % side) * 2 + c))
        return lax.ppermute(value, "seq", pairs)

    side = math.isqrt(chips)
    z, y = seq // 2 // side, seq // 2 % side
    near = jnp.concatenate([queries] + [moved(queries, 0, d) for d in range(1, side)], axis=0)
    far = [moved(near, d, 0) for d in range(1, side)]
    window = jnp.concatenate([new_keys, new_values], axis=0)
    own = [pltpu.with_memory_space_constraint(value, pltpu.HBM) for value in (cache_keys, cache_values)]
    rows_in = (*own, swapped(cache_keys), swapped(cache_values), window, swapped(window))
    limits = lax.dynamic_index_in_dim(reach.reshape(side, side, 2, tok), core, 2, keepdims=False)
    limits = jnp.concatenate([limits, limits], axis=0)
    limits = jnp.concatenate([limits, limits], axis=1)
    limits = lax.dynamic_slice(limits, (z, y, 0), (side, side, tok)).reshape(1, chips * tok)
    first = attention(limits[:, : side * tok], (near,), rows_in)
    outs = attention(limits[:, side * tok :], far, rows_in, first)
    arrived = lax.all_to_all(
        outs.reshape(chips, tok, outs.shape[1]), "seq", 0, 0, axis_index_groups=same_core, tiled=True
    )
    attended, message, matrix = home(arrived, expert_ids, gate_weights, tp)
    half = width // 2
    rows = lax.all_to_all(
        message.reshape(seqs * tp, CAP, half), ("seq", "tp"), 0, 0, tiled=True
    ).reshape(seqs, tp, CAP, half)
    gain = norm_gain.reshape(1, -1)
    up_rows = pltpu.with_memory_space_constraint(w_up[0], pltpu.HBM)
    down_rows = pltpu.with_memory_space_constraint(w_down[0], pltpu.HBM)
    total, square = up_first(rows, gain, up_rows)
    hidden, send = up_second(swapped(rows), gain, up_rows, down_rows, total, square)
    result = join(down_project(hidden, down_rows, send.shape), swapped(send))
    returned = lax.all_to_all(
        result.reshape(seqs * tp, CAP, half), ("seq", "tp"), 0, 0, tiled=True
    ).reshape(E, 2, 2, tp, CAP, half)
    return attended, mix(returned, matrix)


def solution(mesh):
    placed = (
        P("seq", "tp"),
        P("seq", "tp"),
        P("seq", "tp"),
        P("seq", "tp"),
        P("seq", "tp"),
        P(),
        P(),
        P("seq", None),
        P("seq", None),
        P("seq", None, "tp"),
        P("seq", "tp", None),
    )
    return jax.shard_map(
        per_device,
        mesh=mesh,
        in_specs=placed,
        out_specs=(P("seq", "tp"), P("seq", "tp")),
        check_vma=False,
    )
```

time: 189 us -> 175 us (0.926)
  waiting for transfers between devices: 8.67 us -> 0.16 us
  local copies, waits for them, and re-layouts: 10.7 us -> 3.15 us
  starting transfers between devices: 11 us -> 13.8 us
    ppermute x0 -> x6, starting transfers between devices: none -> 10.2 us  [moved(): return lax.ppermute(value, 'seq', pairs)]
    all_to_all x1 -> x0, starting transfers between devices: 7.85 us -> none  [per_device(): lax.all_to_all(jnp.broadcast_to(queries[None], (chips, tok, width)), 'seq...]
    all_to_all x1 -> x0, waiting for transfers between devices: 7.31 us -> none  [per_device(): lax.all_to_all(jnp.broadcast_to(queries[None], (chips, tok, width)), 'seq...]
    unnamed x24 -> x10, local copies, waits for them, and re-layouts: 8.45 us -> 1.57 us
    broadcast_in_dim x1 -> x0, local copies, waits for them, and re-layouts: 2.01 us -> none  [per_device(): jnp.broadcast_to(queries[None], (chips, tok, width))]
  transfers between devices with their start and end apart: 7 -> 11, of which waited for: 4 -> 1; matrix products, arithmetic and copies ran while one was open for 1% -> 2% of each run, Pallas kernels for 6% -> 12%
where the time goes in v4:
time: 175 us; the launch traced here: 174 us
  blocking collectives  93.2 us (53%)
  Pallas kernels  62.8 us (36%)
  starting transfers between devices  13.8 us (8%)
  local copies, waits for them, and re-layouts  3.15 us (2%)
    pallas_call x2, Pallas kernels, attention(): pl.pallas_call(functools.partial(attn_kernel, parts=len(qs), earlier=prev...  45.6 us
    all_to_all x1, blocking collectives, per_device(): lax.all_to_all(message.reshape(seqs * tp, CAP, half), ('seq', 'tp'), 0, 0...  38.2 us
    all_to_all x1, blocking collectives, per_device(): lax.all_to_all(result.reshape(seqs * tp, CAP, half), ('seq', 'tp'), 0, 0,...  34.2 us
    all_to_all x1, blocking collectives, per_device(): lax.all_to_all(outs.reshape(chips, tok, outs.shape[1]), 'seq', 0, 0, axis...  20.8 us
    ppermute x6, starting transfers between devices, moved(): return lax.ppermute(value, 'seq', pairs)  10.2 us
    pallas_call x1, Pallas kernels, up_second(): pl.pallas_call(up_second_kernel, out_shape=(jax.ShapeDtypeStruct(total.sh...  6.63 us
    pallas_call x1, Pallas kernels, up_first(): pl.pallas_call(up_first_kernel, out_shape=(jax.ShapeDtypeStruct((rows, hi...  3.83 us
    pallas_call x1, Pallas kernels, down_project(): pl.pallas_call(down_kernel, out_shape=jax.ShapeDtypeStruct(shape, F32), i...  3.71 us
  transfers between devices with their start and end apart: 11, of which 1 were waited for; matrix products, arithmetic and copies ran while one was open for 2% of the time, Pallas kernels for 12%

profile of v4, /device:TPU:1, one launch (start us, length us, event | category | flops | bytes accessed | tf_op | source)
XLA Modules:
  0.0 174.0 jit_solution(17992761850815935756)
XLA Ops:
  0.6 1.5 collective-permute-start.6
  2.1 0.1 collective-permute-start.7
  2.2 3.0 %collective-permute-start.1 = (bf16[32,1024]{1,0:T(8,128)(2,1)}, bf16[32,1024]{1,0:T(8,128)(2,1)S(1)}, u32[]{:S(2)}, u32[]{:S(2)}) collective-permute-start(bf16[32,1024]{1,0:T(8,128)(2,1)} %param.11), channel_id=1, source_target_pairs={{0,16},{4,20},{8,24},{12,28},{16,0},{20,4},{24,8},{28,12},{32,48},... | collective-permute-start | bytes 196616 | tf_op jit(solution)/shard_map/ppermute | solution.py:459
  5.2 0.8 collective-permute-start
  6.0 0.7 collective-permute-start.2
  6.7 0.8 reshape.28
  7.5 0.1 fusion.1
  7.6 0.1 reshape.29
  7.6 0.7 constant_dynamic-update-slice_fusion.5
  8.3 0.8 constant_dynamic-update-slice_fusion.3
  9.2 0.7 constant_dynamic-update-slice_fusion.4.refs_6_.refs_8_
  9.9 0.0 collective-permute-done
  9.9 1.3 collective-permute-start.8
  11.2 0.0 collective-permute-done.1
  11.2 0.0 collective-permute-done.2
  11.2 1.7 collective-permute-start.5
  12.9 3.3 %collective-permute-start.4 = (bf16[128,1024]{1,0:T(8,128)(2,1)S(1)}, bf16[128,1024]{1,0:T(8,128)(2,1)S(1)}, u32[]{:S(2)}, u32[]{:S(2)}) collective-permute-start(bf16[128,1024]{1,0:T(8,128)(2,1)S(1)} %constant_dynamic-update-slice_fusion.refs_1_), channel_id=1, source_target_pairs={{0,64},{4,68},{8,72},{12,76},{16,80},{20,84},{24,88},{28,92},{32,9... | collective-permute-start | bytes 786440 | tf_op jit(solution)/shard_map/ppermute | solution.py:459
  16.2 0.0 collective-permute-done.8.refs_7_.refs_9_
  16.2 0.7 collective-permute-start.3
  16.9 0.0 collective-permute-done.6.refs_4_.refs_6_
  16.9 0.0 collective-permute-done.7.refs_5_.refs_7_
  17.0 12.7 %shard_map.122.refs_10_ = bf16[128,1152]{1,0:T(8,128)(2,1)S(1)} custom-call(s32[1,128]{1,0:T(1,128)S(1)} %slice.9.refs_0_, bf16[128,1024]{1,0:T(8,128)(2,1)S(1)} %constant_dynamic-update-slice_fusion.refs_1_, bf16[4096,128]{1,0:T(8,128)(2,1)} %refs_4_.1, bf16[4096,128]{1,0:T(8,128)(2,1)} %refs_5_.1, ...), custom_call_target="tpu_custom_call" | custom-call | flops 4362076160 | bytes 8388608 | tf_op jit(solution)/shard_map/pallas_call | solution.py:180
  29.7 0.0 collective-permute-done.5.refs_3_
  29.7 0.0 collective-permute-done.4.refs_2_
  29.7 0.0 collective-permute-done.3.refs_1_
  29.7 32.9 %shard_map.123 = bf16[512,1152]{1,0:T(8,128)(2,1)S(1)} custom-call(s32[1,384]{1,0:T(1,128)S(1)} %slice.8.refs_0_, bf16[128,1024]{1,0:T(8,128)(2,1)S(1)} %collective-permute-done.3.refs_1_, bf16[128,1024]{1,0:T(8,128)(2,1)S(1)} %collective-permute-done.4.refs_2_, bf16[128,1024]{1,0:T(8,128)(2,1)S(1)} %collective-permute-done.5.refs_3_, ...), custom_call_target="tpu_custom_call" | custom-call | flops 13086228480 | bytes 8388608 | tf_op jit(solution)/shard_map/pallas_call | solution.py:180
  62.6 0.0 copy-start.1
  62.6 0.0 copy-start.2
  62.6 20.8 %all_to_all.15.recv_ref = bf16[16,32,1152]{2,1,0:T(8,128)(2,1)S(1)} all-to-all(bf16[16,32,1152]{2,1,0:T(8,128)(2,1)S(1)} %bitcast.16), channel_id=1, replica_groups={{0,8,16,24,32,40,48,56,64,72,80,88,96,104,112,120},{4,12,20,28,36,44,52..., dimensions={0} | all-to-all | bytes 2359296 | tf_op jit(solution)/shard_map/all_to_all | solution.py:474
  83.4 0.0 copy-done.1
  83.5 0.0 copy-done.2
  83.5 1.6 shard_map.124
  85.1 0.0 copy-start
  85.1 38.2 %all_to_all.16 = bf16[128,16,512]{2,1,0:T(8,128)(2,1)S(1)} all-to-all(bf16[128,16,512]{2,1,0:T(8,128)(2,1)S(1)} %bitcast.15), channel_id=1, replica_groups=mesh['seq'=32,'tp'=4] {'seq','tp'}, dimensions={0} | all-to-all | bytes 4194304 | tf_op jit(solution)/shard_map/all_to_all | solution.py:479
  123.3 0.4 collective-permute-start.9
  123.6 0.0 copy-done
  123.7 3.8 %shard_map.125 = (f32[512,768]{1,0:T(8,128)S(1)}, f32[512,128]{1,0:T(8,128)S(1)}) custom-call(bf16[32,4,16,512]{3,2,1,0:T(8,128)(2,1)S(1)} %bitcast.13, f32[1,4096]{1,0:T(1,128)S(1)} %bitcast.17, bf16[4096,768]{1,0:T(8,128)(2,1)} %bitcast.21), custom_call_target="tpu_custom_call" | custom-call | flops 1610612736 | bytes 5242880 | tf_op jit(solution)/shard_map/pallas_call | solution.py:325
  127.5 0.0 collective-permute-done.9.other_ref
  127.5 6.6 %shard_map.126 = (bf16[512,768]{1,0:T(8,128)(2,1)S(1)}, bf16[32,4,16,512]{3,2,1,0:T(8,128)(2,1)S(1)}) custom-call(bf16[32,4,16,512]{3,2,1,0:T(8,128)(2,1)S(1)} %collective-permute-done.9.other_ref, f32[1,4096]{1,0:T(1,128)S(1)} %bitcast.18, bf16[4096,768]{1,0:T(8,128)(2,1)} %bitcast.22, bf16[768,4096]{1,0:T(8,128)(2,1)} %bitcast.23, ...), custom_call_target="tpu_custom_call" | custom-call | tf_op jit(solution)/shard_map/pallas_call | solution.py:364
  134.1 0.4 collective-permute-start.10
  134.5 3.7 %shard_map.127.keep_ref = f32[32,4,16,512]{3,2,1,0:T(8,128)S(1)} custom-call(bf16[512,768]{1,0:T(8,128)(2,1)S(1)} %get-tuple-element.13.hidden_ref, bf16[768,4096]{1,0:T(8,128)(2,1)} %bitcast.24), custom_call_target="tpu_custom_call" | custom-call | flops 1610612736 | bytes 5242880 | tf_op jit(solution)/shard_map/pallas_call | solution.py:395
  138.2 0.1 collective-permute-done.10.partner_ref
  138.4 0.3 shard_map.128
  138.7 34.2 %all_to_all.17 = bf16[128,16,512]{2,1,0:T(8,128)(2,1)S(1)} all-to-all(bf16[128,16,512]{2,1,0:T(8,128)(2,1)S(1)} %bitcast.14), channel_id=1, replica_groups=mesh['seq'=32,'tp'=4] {'seq','tp'}, dimensions={0} | all-to-all | bytes 4194304 | tf_op jit(solution)/shard_map/all_to_all | solution.py:488
  172.9 1.1 shard_map.129
  (6 shorter events, 0.0 us)
Async XLA Ops:
  0.6 16.3 %collective-permute-start.6 = (bf16[4096,128]{1,0:T(8,128)(2,1)}, bf16[4096,128]{1,0:T(8,128)(2,1)S(1)}, u32[]{:S(2)}, u32[]{:S(2)}) collective-permute-start(bf16[4096,128]{1,0:T(8,128)(2,1)} %refs_4_.1), channel_id=1, source_target_pairs={{0,4},{4,0},{8,12},{12,8},{16,20},{20,16},{24,28},{28,24},{32,36},... | collective-permute-start | bytes 3145736 | tf_op jit(solution)/shard_map/ppermute | solution.py:452
  2.1 14.8 %collective-permute-start.7 = (bf16[4096,128]{1,0:T(8,128)(2,1)}, bf16[4096,128]{1,0:T(8,128)(2,1)S(1)}, u32[]{:S(2)}, u32[]{:S(2)}) collective-permute-start(bf16[4096,128]{1,0:T(8,128)(2,1)} %refs_5_.1), channel_id=1, source_target_pairs={{0,4},{4,0},{8,12},{12,8},{16,20},{20,16},{24,28},{28,24},{32,36},... | collective-permute-start | bytes 3145736 | tf_op jit(solution)/shard_map/ppermute | solution.py:452
  2.2 8.9 %collective-permute-start.1 = (bf16[32,1024]{1,0:T(8,128)(2,1)}, bf16[32,1024]{1,0:T(8,128)(2,1)S(1)}, u32[]{:S(2)}, u32[]{:S(2)}) collective-permute-start(bf16[32,1024]{1,0:T(8,128)(2,1)} %param.11), channel_id=1, source_target_pairs={{0,16},{4,20},{8,24},{12,28},{16,0},{20,4},{24,8},{28,12},{32,48},... | collective-permute-start | bytes 196616 | tf_op jit(solution)/shard_map/ppermute | solution.py:459
  5.2 4.7 %collective-permute-start = (bf16[32,1024]{1,0:T(8,128)(2,1)}, bf16[32,1024]{1,0:T(8,128)(2,1)S(1)}, u32[]{:S(2)}, u32[]{:S(2)}) collective-permute-start(bf16[32,1024]{1,0:T(8,128)(2,1)} %param.11), channel_id=1, source_target_pairs={{0,24},{4,28},{8,0},{12,4},{16,8},{20,12},{24,16},{28,20},{32,56},... | collective-permute-start | bytes 196616 | tf_op jit(solution)/shard_map/ppermute | solution.py:459
  6.0 5.2 %collective-permute-start.2 = (bf16[32,1024]{1,0:T(8,128)(2,1)}, bf16[32,1024]{1,0:T(8,128)(2,1)S(1)}, u32[]{:S(2)}, u32[]{:S(2)}) collective-permute-start(bf16[32,1024]{1,0:T(8,128)(2,1)} %param.11), channel_id=1, source_target_pairs={{0,8},{4,12},{8,16},{12,20},{16,24},{20,28},{24,0},{28,4},{32,40},... | collective-permute-start | bytes 196616 | tf_op jit(solution)/shard_map/ppermute | solution.py:459
  9.9 6.3 %collective-permute-start.8 = (bf16[64,128]{1,0:T(8,128)(2,1)S(1)}, bf16[64,128]{1,0:T(8,128)(2,1)S(1)}, u32[]{:S(2)}, u32[]{:S(2)}) collective-permute-start(bf16[64,128]{1,0:T(8,128)(2,1)S(1)} %constant_dynamic-update-slice_fusion.4.refs_6_.refs_8_), channel_id=1, source_target_pairs={{0,4},{4,0},{8,12},{12,8},{16,20},{20,16},{24,28},{28,24},{32,36},... | collective-permute-start | bytes 49160 | tf_op jit(solution)/shard_map/ppermute | solution.py:452
  11.2 18.5 %collective-permute-start.5 = (bf16[128,1024]{1,0:T(8,128)(2,1)S(1)}, bf16[128,1024]{1,0:T(8,128)(2,1)S(1)}, u32[]{:S(2)}, u32[]{:S(2)}) collective-permute-start(bf16[128,1024]{1,0:T(8,128)(2,1)S(1)} %constant_dynamic-update-slice_fusion.refs_1_), channel_id=1, source_target_pairs={{0,32},{4,36},{8,40},{12,44},{16,48},{20,52},{24,56},{28,60},{32,6... | collective-permute-start | bytes 786440 | tf_op jit(solution)/shard_map/ppermute | solution.py:459
  12.9 16.8 %collective-permute-start.4 = (bf16[128,1024]{1,0:T(8,128)(2,1)S(1)}, bf16[128,1024]{1,0:T(8,128)(2,1)S(1)}, u32[]{:S(2)}, u32[]{:S(2)}) collective-permute-start(bf16[128,1024]{1,0:T(8,128)(2,1)S(1)} %constant_dynamic-update-slice_fusion.refs_1_), channel_id=1, source_target_pairs={{0,64},{4,68},{8,72},{12,76},{16,80},{20,84},{24,88},{28,92},{32,9... | collective-permute-start | bytes 786440 | tf_op jit(solution)/shard_map/ppermute | solution.py:459
  16.2 13.5 %collective-permute-start.3 = (bf16[128,1024]{1,0:T(8,128)(2,1)S(1)}, bf16[128,1024]{1,0:T(8,128)(2,1)S(1)}, u32[]{:S(2)}, u32[]{:S(2)}) collective-permute-start(bf16[128,1024]{1,0:T(8,128)(2,1)S(1)} %constant_dynamic-update-slice_fusion.refs_1_), channel_id=1, source_target_pairs={{0,96},{4,100},{8,104},{12,108},{16,112},{20,116},{24,120},{28,124... | collective-permute-start | bytes 786440 | tf_op jit(solution)/shard_map/ppermute | solution.py:459
  62.6 20.8 %copy-start.1 = (s32[32,2]{0,1:T(2,128)S(1)}, s32[32,2]{0,1:T(2,128)}, u32[]{:S(2)}) copy-start(s32[32,2]{0,1:T(2,128)} %param.19) | copy-start | bytes 772
  62.6 20.8 %copy-start.2 = (f32[32,2]{0,1:T(2,128)S(1)}, f32[32,2]{0,1:T(2,128)}, u32[]{:S(2)}) copy-start(f32[32,2]{0,1:T(2,128)} %param.18) | copy-start | bytes 772
  85.1 38.6 %copy-start = (f32[4096]{0:T(1024)S(1)}, f32[4096]{0:T(1024)}, u32[]{:S(2)}) copy-start(f32[4096]{0:T(1024)} %param.17) | copy-start | bytes 49156
  123.3 4.2 %collective-permute-start.9 = (bf16[32,4,16,512]{3,2,1,0:T(8,128)(2,1)S(1)}, bf16[32,4,16,512]{3,2,1,0:T(8,128)(2,1)S(1)}, u32[]{:S(2)}, u32[]{:S(2)}) collective-permute-start(bf16[32,4,16,512]{3,2,1,0:T(8,128)(2,1)S(1)} %bitcast.12), channel_id=1, source_target_pairs={{0,4},{4,0},{8,12},{12,8},{16,20},{20,16},{24,28},{28,24},{32,36},... | collective-permute-start | bytes 6291464 | tf_op jit(solution)/shard_map/ppermute | solution.py:452
  134.1 4.2 %collective-permute-start.10 = (bf16[32,4,16,512]{3,2,1,0:T(8,128)(2,1)S(1)}, bf16[32,4,16,512]{3,2,1,0:T(8,128)(2,1)S(1)}, u32[]{:S(2)}, u32[]{:S(2)}) collective-permute-start(bf16[32,4,16,512]{3,2,1,0:T(8,128)(2,1)S(1)} %get-tuple-element.14), channel_id=1, source_target_pairs={{0,4},{4,0},{8,12},{12,8},{16,20},{20,16},{24,28},{28,24},{32,36},... | collective-permute-start | bytes 6291464 | tf_op jit(solution)/shard_map/ppermute | solution.py:452

commit v5 on v4

--- a/solution.py
+++ b/solution.py
@@ -21,7 +21,7 @@
 VM = pl.BlockSpec(memory_space=pltpu.VMEM)
 HBM = pl.BlockSpec(memory_space=pltpu.HBM)
 
-def attn_kernel(*refs, parts, earlier, CH):
+def attn_kernel(*refs, parts, earlier, per, CH):
     reach_ref = refs[0]
     q_refs, refs = refs[1 : 1 + parts], refs[1 + parts :]
     (k0_ref, v0_ref, k1_ref, v1_ref, n0_ref, n1_ref), refs = refs[:6], refs[6:]
@@ -38,8 +38,9 @@
     KEYS = k_own.shape[0]
     WIN = 2 * KEYS
     NCH = KEYS // CH
-    R = 2 * tokens
-    NT = parts * 4
+    R = per * tokens
+    groups = 8 // per
+    NT = parts * groups
     side = blocks
     seq = lax.axis_index("seq")
     core = lax.rem(seq, 2)
@@ -78,20 +79,20 @@
 
     def target(i, b):
         if not earlier:
-            return pl.multiple_of((lax.div(i, 4) * blocks + b) * W, W)
-        place = lax.rem(z + lax.div(i, 4) + 1, side) * side + lax.rem(y + b, side)
+            return pl.multiple_of((lax.div(i, groups) * blocks + b) * W, W)
+        place = lax.rem(z + lax.div(i, groups) + 1, side) * side + lax.rem(y + b, side)
         return pl.multiple_of(place * W, W)
 
     def tile(i):
-        return pl.multiple_of(lax.div(i, 4) * tokens, tokens), lax.rem(i, 4) * 2
-
-    def twice(x):
-        return jnp.concatenate([x, x], axis=0)
+        return pl.multiple_of(lax.div(i, groups) * tokens, tokens), lax.rem(i, groups) * per
+
+    def repeated(x):
+        return jnp.concatenate([x] * per, axis=0)
 
     def load_q(i):
         r, h = tile(i)
         out = []
-        for k in range(2):
+        for k in range(per):
             qf = q_all[pl.ds(r, tokens), pl.ds(pl.multiple_of((h + k) * HD, HD), HD)].astype(F32) * SCALE
             hi = qf.astype(BF)
             out.append(jnp.concatenate([hi, (qf - hi.astype(F32)).astype(BF)], axis=1))
@@ -105,13 +106,13 @@
         s = dotk(qq, kk[pl.ds(WIN, 128), :])
         lane = lax.broadcasted_iota(jnp.int32, (R, 128), 1)
         key = jnp.where(lane < W, lane + seq * W, lane - W + partner * W)
-        return jnp.where((lane < 2 * W) & (key <= twice(tok_ref[pl.ds(r, tokens), :])), s, NEG)
+        return jnp.where((lane < 2 * W) & (key <= repeated(tok_ref[pl.ds(r, tokens), :])), s, NEG)
 
     def step(i, do_qk, do_pv):
         if do_qk:
             qq = load_q(i + 1)
             r1, _ = tile(i + 1)
-            lim = twice(lim_ref[pl.ds(r1, tokens), :])
+            lim = repeated(lim_ref[pl.ds(r1, tokens), :])
             lane0 = lax.broadcasted_iota(jnp.int32, (R, 128), 1)
             sw = window_scores(i + 1, qq)
             mx = jnp.maximum(sw, FLOOR)
@@ -144,7 +145,7 @@
             L = jnp.where(l > 0, m + jnp.log2(jnp.maximum(l, 1e-30)), NEG)
             lane = lax.rem(lax.broadcasted_iota(jnp.int32, (tokens, 128), 1), 8)
             old = l_scr[pl.ds(r, tokens), :]
-            for k in range(2):
+            for k in range(per):
                 old = jnp.where(lane == h + k, L[k * tokens : (k + 1) * tokens], old)
                 cols = pl.ds(pl.multiple_of((h + k) * HD, HD), HD)
                 for b in range(blocks):
@@ -171,14 +172,14 @@
         o_ref[pl.ds(pl.multiple_of(place * W, W), W), pl.ds(8 * HD, 128)] = packed[b * W : (b + 1) * W]
 
 
-def attention(reach, qs, tables, prev=None, CH=512):
+def attention(reach, qs, tables, per, prev=None, CH=512):
     tokens = qs[0].shape[0]
     T = len(qs) * tokens
     keys = 2 * tables[0].shape[0] + 128
     rows = T + (0 if prev is None else tokens)
     more = () if prev is None else (prev,)
     return pl.pallas_call(
-        functools.partial(attn_kernel, parts=len(qs), earlier=prev is not None, CH=CH),
+        functools.partial(attn_kernel, parts=len(qs), earlier=prev is not None, per=per, CH=CH),
         out_shape=jax.ShapeDtypeStruct((rows, 9 * HD), BF),
         in_specs=[VM] * (1 + len(qs)) + [HBM] * 2 + [VM] * (4 + len(more)),
         out_specs=VM,
@@ -188,14 +189,14 @@
             pltpu.VMEM((keys, 2 * HD), BF),
             pltpu.VMEM(tables[0].shape, BF),
             pltpu.VMEM(tables[0].shape, BF),
-            pltpu.VMEM((2 * tokens, keys), F32),
-            pltpu.VMEM((2 * tokens, 128), F32),
+            pltpu.VMEM((per * tokens, keys), F32),
+            pltpu.VMEM((per * tokens, 128), F32),
             pltpu.VMEM((T, 128), F32),
             pltpu.VMEM((T, 128), jnp.int32),
             pltpu.VMEM((T, 128), jnp.int32),
             pltpu.SemaphoreType.DMA((2,)),
         ],
-        compiler_params=pltpu.CompilerParams(vmem_limit_bytes=36 * MIB),
+        compiler_params=pltpu.CompilerParams(vmem_limit_bytes=(28 + 4 * per) * MIB),
         cost_estimate=pl.CostEstimate(flops=32 * T * keys * HD, bytes_accessed=8 * MIB, transcendentals=T * 8 * keys),
     )(reach, *qs, *tables, *more)
 
@@ -313,71 +314,72 @@
     return jnp.dot(s_buf[...], weights, preferred_element_type=F32), square
 
 
-def up_first_kernel(own_ref, gain_ref, up_ref, total_ref, square_ref, s_buf, w_buf, sems):
+def up_first_kernel(
+    own_ref, gain_ref, up_ref, down_ref, total_ref, square_ref, next_up, next_down, s_buf, w_buf, sems, next_sems, down_sems
+):
     copies = start_rows(up_ref, w_buf, this_core(), sems)
+    later = start_rows(up_ref, next_up, 1 - this_core(), next_sems) + start_columns(down_ref, next_down, 1 - this_core(), down_sems)
     total, square = up_part(own_ref, this_core(), gain_ref, s_buf, w_buf, copies, jnp.zeros(square_ref.shape, F32))
     total_ref[...] = total
     square_ref[...] = square
-
-
-def up_first(own, gain, w_up):
+    for copy in later:
+        copy.wait()
+
+
+def up_first(own, gain, w_up, w_down):
     rows, tp, half, hid = own.shape[0] * own.shape[2], own.shape[1], own.shape[3], w_up.shape[1]
     return pl.pallas_call(
         up_first_kernel,
         out_shape=(
             jax.ShapeDtypeStruct((rows, hid), F32),
             jax.ShapeDtypeStruct((rows, 128), F32),
+            jax.ShapeDtypeStruct((tp, half, hid), BF),
+            jax.ShapeDtypeStruct((tp, hid, half), BF),
         ),
-        in_specs=[VM, VM, HBM],
-        out_specs=(VM, VM),
+        in_specs=[VM, VM, HBM, HBM],
+        out_specs=(VM,) * 4,
         scratch_shapes=[
             pltpu.VMEM((rows, tp * half), BF),
             pltpu.VMEM((tp, half, hid), BF),
             pltpu.SemaphoreType.DMA((tp,)),
+            pltpu.SemaphoreType.DMA((tp,)),
+            pltpu.SemaphoreType.DMA((tp,)),
         ],
         compiler_params=pltpu.CompilerParams(vmem_limit_bytes=24 * MIB),
         cost_estimate=pl.CostEstimate(flops=2 * rows * tp * half * hid, bytes_accessed=5 * MIB, transcendentals=0),
-    )(own, gain, w_up)
-
-
-def up_second_kernel(
-    other_ref, gain_ref, up_ref, down_ref, total_ref, square_ref, hidden_ref, send_ref, s_buf, w_buf, d_buf, sems, d_sems
-):
+    )(own, gain, w_up, w_down)
+
+
+def up_second_kernel(other_ref, gain_ref, up_ref, down_ref, total_ref, square_ref, hidden_ref, send_ref):
     seqs, tp, cap, half = other_ref.shape
-    other = 1 - this_core()
-    copies = start_rows(up_ref, w_buf, other, sems)
-    down_copies = start_columns(down_ref, d_buf, other, d_sems)
-    total, square = up_part(other_ref, other, gain_ref, s_buf, w_buf, copies, square_ref[...])
+    total, square = total_ref[...], square_ref[...]
+    for x in range(tp):
+        a = other_ref[:, x].reshape(seqs * cap, half).astype(F32)
+        scaled = (a * gain_ref[:, columns(x, 1 - this_core(), half)]).astype(BF)
+        total = total + jnp.dot(scaled, up_ref[x], preferred_element_type=F32)
+        for c in range(half // 128):
+            part = a[:, c * 128 : (c + 1) * 128]
+            square = square + part * part
     mean = jnp.sum(square, axis=1, keepdims=True) / (2 * tp * half)
-    total = (total + total_ref[...]) * lax.rsqrt(mean + EPSILON)
+    total = total * lax.rsqrt(mean + EPSILON)
     hidden = (total / (1.0 + jnp.exp(-total))).astype(BF)
     hidden_ref[...] = hidden
-    for copy in down_copies:
-        copy.wait()
     for x in range(tp):
-        out = jnp.dot(hidden, d_buf[x], preferred_element_type=F32)
+        out = jnp.dot(hidden, down_ref[x], preferred_element_type=F32)
         send_ref[:, x] = out.astype(BF).reshape(seqs, cap, half)
 
 
-def up_second(other, gain, w_up, w_down, total, square):
-    rows, tp, half, hid = total.shape[0], other.shape[1], other.shape[3], w_up.shape[1]
+def up_second(other, gain, up_rows, down_columns, total, square):
     return pl.pallas_call(
         up_second_kernel,
         out_shape=(
             jax.ShapeDtypeStruct(total.shape, BF),
             jax.ShapeDtypeStruct(other.shape, BF),
         ),
-        in_specs=[VM, VM, HBM, HBM, VM, VM],
+        in_specs=[VM] * 6,
         out_specs=(VM, VM),
-        scratch_shapes=[
-            pltpu.VMEM((rows, tp * half), BF),
-            pltpu.VMEM((tp, half, hid), BF),
-            pltpu.VMEM((tp, hid, half), BF),
-            pltpu.SemaphoreType.DMA((tp,)),
-            pltpu.SemaphoreType.DMA((tp,)),
-        ],
-        compiler_params=pltpu.CompilerParams(vmem_limit_bytes=30 * MIB),
-    )(other, gain, w_up, w_down, total, square)
+        compiler_params=pltpu.CompilerParams(vmem_limit_bytes=28 * MIB),
+    )(other, gain, up_rows, down_columns, total, square)
 
 
 def down_kernel(hidden_ref, down_ref, out_ref, d_buf, sems):
@@ -469,8 +471,8 @@
     limits = jnp.concatenate([limits, limits], axis=0)
     limits = jnp.concatenate([limits, limits], axis=1)
     limits = lax.dynamic_slice(limits, (z, y, 0), (side, side, tok)).reshape(1, chips * tok)
-    first = attention(limits[:, : side * tok], (near,), rows_in)
-    outs = attention(limits[:, side * tok :], far, rows_in, first)
+    first = attention(limits[:, : side * tok], (near,), rows_in, 2)
+    outs = attention(limits[:, side * tok :], far, rows_in, 4, first)
     arrived = lax.all_to_all(
         outs.reshape(chips, tok, outs.shape[1]), "seq", 0, 0, axis_index_groups=same_core, tiled=True
     )
@@ -482,8 +484,8 @@
     gain = norm_gain.reshape(1, -1)
     up_rows = pltpu.with_memory_space_constraint(w_up[0], pltpu.HBM)
     down_rows = pltpu.with_memory_space_constraint(w_down[0], pltpu.HBM)
-    total, square = up_first(rows, gain, up_rows)
-    hidden, send = up_second(swapped(rows), gain, up_rows, down_rows, total, square)
+    total, square, next_up, next_down = up_first(rows, gain, up_rows, down_rows)
+    hidden, send = up_second(swapped(rows), gain, next_up, next_down, total, square)
     result = join(down_project(hidden, down_rows, send.shape), swapped(send))
     returned = lax.all_to_all(
         result.reshape(seqs * tp, CAP, half), ("seq", "tp"), 0, 0, tiled=True

time: 175 us -> 172 us (0.983)
  Pallas kernels: 62.8 us -> 60.1 us
    pallas_call x1, Pallas kernels: 6.63 us -> 4.04 us  [up_second(): pl.pallas_call(up_second_kernel, out_shape=(jax.ShapeDtypeStruct(total.sh...]
  transfers between devices with their start and end apart: 11 -> 11, of which waited for: 1 -> 1; matrix products, arithmetic and copies ran while one was open for 2% -> 2% of each run, Pallas kernels for 12% -> 13%
where the time goes in v5:
time: 172 us; the launch traced here: 171 us
  blocking collectives  93.4 us (54%)
  Pallas kernels  60.1 us (35%)
  starting transfers between devices  13.6 us (8%)
  local copies, waits for them, and re-layouts  3.15 us (2%)
    pallas_call x2, Pallas kernels, attention(): pl.pallas_call(functools.partial(attn_kernel, parts=len(qs), earlier=prev...  44 us
    all_to_all x1, blocking collectives, per_device(): lax.all_to_all(message.reshape(seqs * tp, CAP, half), ('seq', 'tp'), 0, 0...  38 us
    all_to_all x1, blocking collectives, per_device(): lax.all_to_all(result.reshape(seqs * tp, CAP, half), ('seq', 'tp'), 0, 0,...  34.2 us
    all_to_all x1, blocking collectives, per_device(): lax.all_to_all(outs.reshape(chips, tok, outs.shape[1]), 'seq', 0, 0, axis...  21.2 us
    ppermute x6, starting transfers between devices, moved(): return lax.ppermute(value, 'seq', pairs)  10.2 us
    pallas_call x1, Pallas kernels, up_first(): pl.pallas_call(up_first_kernel, out_shape=(jax.ShapeDtypeStruct((rows, hi...  5.35 us
    pallas_call x1, Pallas kernels, up_second(): pl.pallas_call(up_second_kernel, out_shape=(jax.ShapeDtypeStruct(total.sh...  4.04 us
    pallas_call x1, Pallas kernels, down_project(): pl.pallas_call(down_kernel, out_shape=jax.ShapeDtypeStruct(shape, F32), i...  3.71 us
  transfers between devices with their start and end apart: 11, of which 1 were waited for; matrix products, arithmetic and copies ran while one was open for 2% of the time, Pallas kernels for 13%

profile of v5, /device:TPU:1, one launch (start us, length us, event | category | flops | bytes accessed | tf_op | source)
XLA Modules:
  0.0 171.5 jit_solution(11634538511019690673)
XLA Ops:
  0.6 1.5 collective-permute-start.6
  2.1 0.1 collective-permute-start.7
  2.2 3.0 %collective-permute-start.1 = (bf16[32,1024]{1,0:T(8,128)(2,1)}, bf16[32,1024]{1,0:T(8,128)(2,1)S(1)}, u32[]{:S(2)}, u32[]{:S(2)}) collective-permute-start(bf16[32,1024]{1,0:T(8,128)(2,1)} %param.11), channel_id=1, source_target_pairs={{0,16},{4,20},{8,24},{12,28},{16,0},{20,4},{24,8},{28,12},{32,48},... | collective-permute-start | bytes 196616 | tf_op jit(solution)/shard_map/ppermute | solution.py:461
  5.2 0.8 collective-permute-start
  6.0 0.7 collective-permute-start.2
  6.7 0.8 reshape.28
  7.5 0.1 fusion.1
  7.6 0.1 reshape.29
  7.6 0.7 constant_dynamic-update-slice_fusion.5
  8.3 0.8 constant_dynamic-update-slice_fusion.3
  9.2 0.7 constant_dynamic-update-slice_fusion.4.refs_6_.refs_8_
  9.9 0.0 collective-permute-done
  9.9 1.3 collective-permute-start.8
  11.2 0.0 collective-permute-done.1
  11.2 0.0 collective-permute-done.2
  11.2 1.7 collective-permute-start.5
  12.9 3.3 %collective-permute-start.4 = (bf16[128,1024]{1,0:T(8,128)(2,1)S(1)}, bf16[128,1024]{1,0:T(8,128)(2,1)S(1)}, u32[]{:S(2)}, u32[]{:S(2)}) collective-permute-start(bf16[128,1024]{1,0:T(8,128)(2,1)S(1)} %constant_dynamic-update-slice_fusion.refs_1_), channel_id=1, source_target_pairs={{0,64},{4,68},{8,72},{12,76},{16,80},{20,84},{24,88},{28,92},{32,9... | collective-permute-start | bytes 786440 | tf_op jit(solution)/shard_map/ppermute | solution.py:461
  16.2 0.0 collective-permute-done.8.refs_7_.refs_9_
  16.2 0.7 collective-permute-start.3
  16.9 0.0 collective-permute-done.6.refs_4_.refs_6_
  17.0 0.0 collective-permute-done.7.refs_5_.refs_7_
  17.0 12.5 %shard_map.122.refs_10_ = bf16[128,1152]{1,0:T(8,128)(2,1)S(1)} custom-call(s32[1,128]{1,0:T(1,128)S(1)} %slice.9.refs_0_, bf16[128,1024]{1,0:T(8,128)(2,1)S(1)} %constant_dynamic-update-slice_fusion.refs_1_, bf16[4096,128]{1,0:T(8,128)(2,1)} %refs_4_.1, bf16[4096,128]{1,0:T(8,128)(2,1)} %refs_5_.1, ...), custom_call_target="tpu_custom_call" | custom-call | flops 4362076160 | bytes 8388608 | tf_op jit(solution)/shard_map/pallas_call | solution.py:181
  29.5 0.0 collective-permute-done.5.refs_3_
  29.5 0.0 collective-permute-done.4.refs_2_
  29.5 0.0 collective-permute-done.3.refs_1_
  29.5 31.4 %shard_map.123 = bf16[512,1152]{1,0:T(8,128)(2,1)S(1)} custom-call(s32[1,384]{1,0:T(1,128)S(1)} %slice.8.refs_0_, bf16[128,1024]{1,0:T(8,128)(2,1)S(1)} %collective-permute-done.3.refs_1_, bf16[128,1024]{1,0:T(8,128)(2,1)S(1)} %collective-permute-done.4.refs_2_, bf16[128,1024]{1,0:T(8,128)(2,1)S(1)} %collective-permute-done.5.refs_3_, ...), custom_call_target="tpu_custom_call" | custom-call | flops 13086228480 | bytes 8388608 | tf_op jit(solution)/shard_map/pallas_call | solution.py:181
  61.0 0.0 copy-start.1
  61.0 0.0 copy-start.2
  61.0 21.2 %all_to_all.15.recv_ref = bf16[16,32,1152]{2,1,0:T(8,128)(2,1)S(1)} all-to-all(bf16[16,32,1152]{2,1,0:T(8,128)(2,1)S(1)} %bitcast.16), channel_id=1, replica_groups={{0,8,16,24,32,40,48,56,64,72,80,88,96,104,112,120},{4,12,20,28,36,44,52..., dimensions={0} | all-to-all | bytes 2359296 | tf_op jit(solution)/shard_map/all_to_all | solution.py:476
  82.2 0.0 copy-done.1
  82.2 0.0 copy-done.2
  82.2 1.6 shard_map.124
  83.8 0.0 copy-start
  83.8 38.0 %all_to_all.16 = bf16[128,16,512]{2,1,0:T(8,128)(2,1)S(1)} all-to-all(bf16[128,16,512]{2,1,0:T(8,128)(2,1)S(1)} %bitcast.15), channel_id=1, replica_groups=mesh['seq'=32,'tp'=4] {'seq','tp'}, dimensions={0} | all-to-all | bytes 4194304 | tf_op jit(solution)/shard_map/all_to_all | solution.py:481
  121.8 0.4 collective-permute-start.9
  122.2 0.0 copy-done
  122.2 5.3 %shard_map.125 = (f32[512,768]{1,0:T(8,128)S(1)}, f32[512,128]{1,0:T(8,128)S(1)}, bf16[4,512,768]{2,1,0:T(8,128)(2,1)S(1)}, bf16[4,768,512]{2,1,0:T(8,128)(2,1)S(1)}) custom-call(bf16[32,4,16,512]{3,2,1,0:T(8,128)(2,1)S(1)} %bitcast.13, f32[1,4096]{1,0:T(1,128)S(1)} %bitcast.17, bf16[4096,768]{1,0:T(8,128)(2,1)} %bitcast.23, bf16[768,4096]{1,0:T(8,128)(2,1)} %bitcast.21), custom_call_target="tpu_custom_call" | custom-call | flops 1610612736 | bytes 5242880 | tf_op jit(solution)/shard_map/pallas_call | solution.py:331
  127.5 0.0 collective-permute-done.9.other_ref
  127.6 4.0 %shard_map.126 = (bf16[512,768]{1,0:T(8,128)(2,1)S(1)}, bf16[32,4,16,512]{3,2,1,0:T(8,128)(2,1)S(1)}) custom-call(bf16[32,4,16,512]{3,2,1,0:T(8,128)(2,1)S(1)} %collective-permute-done.9.other_ref, f32[1,4096]{1,0:T(1,128)S(1)} %bitcast.18, bf16[4,512,768]{2,1,0:T(8,128)(2,1)S(1)} %get-tuple-element.13.up_ref, ...), custom_call_target="tpu_custom_call" | custom-call | tf_op jit(solution)/shard_map/pallas_call | solution.py:373
  131.6 0.2 collective-permute-start.10
  131.8 3.7 %shard_map.127.keep_ref = f32[32,4,16,512]{3,2,1,0:T(8,128)S(1)} custom-call(bf16[512,768]{1,0:T(8,128)(2,1)S(1)} %get-tuple-element.17.hidden_ref, bf16[768,4096]{1,0:T(8,128)(2,1)} %bitcast.22), custom_call_target="tpu_custom_call" | custom-call | flops 1610612736 | bytes 5242880 | tf_op jit(solution)/shard_map/pallas_call | solution.py:397
  135.5 0.3 collective-permute-done.10.partner_ref
  135.8 0.3 shard_map.128
  136.2 34.2 %all_to_all.17 = bf16[128,16,512]{2,1,0:T(8,128)(2,1)S(1)} all-to-all(bf16[128,16,512]{2,1,0:T(8,128)(2,1)S(1)} %bitcast.14), channel_id=1, replica_groups=mesh['seq'=32,'tp'=4] {'seq','tp'}, dimensions={0} | all-to-all | bytes 4194304 | tf_op jit(solution)/shard_map/all_to_all | solution.py:490
  170.4 1.1 shard_map.129
  (6 shorter events, 0.0 us)
Async XLA Ops:
  0.6 16.3 %collective-permute-start.6 = (bf16[4096,128]{1,0:T(8,128)(2,1)}, bf16[4096,128]{1,0:T(8,128)(2,1)S(1)}, u32[]{:S(2)}, u32[]{:S(2)}) collective-permute-start(bf16[4096,128]{1,0:T(8,128)(2,1)} %refs_4_.1), channel_id=1, source_target_pairs={{0,4},{4,0},{8,12},{12,8},{16,20},{20,16},{24,28},{28,24},{32,36},... | collective-permute-start | bytes 3145736 | tf_op jit(solution)/shard_map/ppermute | solution.py:454
  2.1 14.8 %collective-permute-start.7 = (bf16[4096,128]{1,0:T(8,128)(2,1)}, bf16[4096,128]{1,0:T(8,128)(2,1)S(1)}, u32[]{:S(2)}, u32[]{:S(2)}) collective-permute-start(bf16[4096,128]{1,0:T(8,128)(2,1)} %refs_5_.1), channel_id=1, source_target_pairs={{0,4},{4,0},{8,12},{12,8},{16,20},{20,16},{24,28},{28,24},{32,36},... | collective-permute-start | bytes 3145736 | tf_op jit(solution)/shard_map/ppermute | solution.py:454
  2.2 8.9 %collective-permute-start.1 = (bf16[32,1024]{1,0:T(8,128)(2,1)}, bf16[32,1024]{1,0:T(8,128)(2,1)S(1)}, u32[]{:S(2)}, u32[]{:S(2)}) collective-permute-start(bf16[32,1024]{1,0:T(8,128)(2,1)} %param.11), channel_id=1, source_target_pairs={{0,16},{4,20},{8,24},{12,28},{16,0},{20,4},{24,8},{28,12},{32,48},... | collective-permute-start | bytes 196616 | tf_op jit(solution)/shard_map/ppermute | solution.py:461
  5.2 4.7 %collective-permute-start = (bf16[32,1024]{1,0:T(8,128)(2,1)}, bf16[32,1024]{1,0:T(8,128)(2,1)S(1)}, u32[]{:S(2)}, u32[]{:S(2)}) collective-permute-start(bf16[32,1024]{1,0:T(8,128)(2,1)} %param.11), channel_id=1, source_target_pairs={{0,24},{4,28},{8,0},{12,4},{16,8},{20,12},{24,16},{28,20},{32,56},... | collective-permute-start | bytes 196616 | tf_op jit(solution)/shard_map/ppermute | solution.py:461
  6.0 5.2 %collective-permute-start.2 = (bf16[32,1024]{1,0:T(8,128)(2,1)}, bf16[32,1024]{1,0:T(8,128)(2,1)S(1)}, u32[]{:S(2)}, u32[]{:S(2)}) collective-permute-start(bf16[32,1024]{1,0:T(8,128)(2,1)} %param.11), channel_id=1, source_target_pairs={{0,8},{4,12},{8,16},{12,20},{16,24},{20,28},{24,0},{28,4},{32,40},... | collective-permute-start | bytes 196616 | tf_op jit(solution)/shard_map/ppermute | solution.py:461
  9.9 6.3 %collective-permute-start.8 = (bf16[64,128]{1,0:T(8,128)(2,1)S(1)}, bf16[64,128]{1,0:T(8,128)(2,1)S(1)}, u32[]{:S(2)}, u32[]{:S(2)}) collective-permute-start(bf16[64,128]{1,0:T(8,128)(2,1)S(1)} %constant_dynamic-update-slice_fusion.4.refs_6_.refs_8_), channel_id=1, source_target_pairs={{0,4},{4,0},{8,12},{12,8},{16,20},{20,16},{24,28},{28,24},{32,36},... | collective-permute-start | bytes 49160 | tf_op jit(solution)/shard_map/ppermute | solution.py:454
  11.2 18.3 %collective-permute-start.5 = (bf16[128,1024]{1,0:T(8,128)(2,1)S(1)}, bf16[128,1024]{1,0:T(8,128)(2,1)S(1)}, u32[]{:S(2)}, u32[]{:S(2)}) collective-permute-start(bf16[128,1024]{1,0:T(8,128)(2,1)S(1)} %constant_dynamic-update-slice_fusion.refs_1_), channel_id=1, source_target_pairs={{0,32},{4,36},{8,40},{12,44},{16,48},{20,52},{24,56},{28,60},{32,6... | collective-permute-start | bytes 786440 | tf_op jit(solution)/shard_map/ppermute | solution.py:461
  12.9 16.6 %collective-permute-start.4 = (bf16[128,1024]{1,0:T(8,128)(2,1)S(1)}, bf16[128,1024]{1,0:T(8,128)(2,1)S(1)}, u32[]{:S(2)}, u32[]{:S(2)}) collective-permute-start(bf16[128,1024]{1,0:T(8,128)(2,1)S(1)} %constant_dynamic-update-slice_fusion.refs_1_), channel_id=1, source_target_pairs={{0,64},{4,68},{8,72},{12,76},{16,80},{20,84},{24,88},{28,92},{32,9... | collective-permute-start | bytes 786440 | tf_op jit(solution)/shard_map/ppermute | solution.py:461
  16.2 13.3 %collective-permute-start.3 = (bf16[128,1024]{1,0:T(8,128)(2,1)S(1)}, bf16[128,1024]{1,0:T(8,128)(2,1)S(1)}, u32[]{:S(2)}, u32[]{:S(2)}) collective-permute-start(bf16[128,1024]{1,0:T(8,128)(2,1)S(1)} %constant_dynamic-update-slice_fusion.refs_1_), channel_id=1, source_target_pairs={{0,96},{4,100},{8,104},{12,108},{16,112},{20,116},{24,120},{28,124... | collective-permute-start | bytes 786440 | tf_op jit(solution)/shard_map/ppermute | solution.py:461
  61.0 21.2 %copy-start.1 = (s32[32,2]{0,1:T(2,128)S(1)}, s32[32,2]{0,1:T(2,128)}, u32[]{:S(2)}) copy-start(s32[32,2]{0,1:T(2,128)} %param.19) | copy-start | bytes 772
  61.0 21.2 %copy-start.2 = (f32[32,2]{0,1:T(2,128)S(1)}, f32[32,2]{0,1:T(2,128)}, u32[]{:S(2)}) copy-start(f32[32,2]{0,1:T(2,128)} %param.18) | copy-start | bytes 772
  83.8 38.4 %copy-start = (f32[4096]{0:T(1024)S(1)}, f32[4096]{0:T(1024)}, u32[]{:S(2)}) copy-start(f32[4096]{0:T(1024)} %param.17) | copy-start | bytes 49156
  121.8 5.8 %collective-permute-start.9 = (bf16[32,4,16,512]{3,2,1,0:T(8,128)(2,1)S(1)}, bf16[32,4,16,512]{3,2,1,0:T(8,128)(2,1)S(1)}, u32[]{:S(2)}, u32[]{:S(2)}) collective-permute-start(bf16[32,4,16,512]{3,2,1,0:T(8,128)(2,1)S(1)} %bitcast.12), channel_id=1, source_target_pairs={{0,4},{4,0},{8,12},{12,8},{16,20},{20,16},{24,28},{28,24},{32,36},... | collective-permute-start | bytes 6291464 | tf_op jit(solution)/shard_map/ppermute | solution.py:454
  131.6 4.2 %collective-permute-start.10 = (bf16[32,4,16,512]{3,2,1,0:T(8,128)(2,1)S(1)}, bf16[32,4,16,512]{3,2,1,0:T(8,128)(2,1)S(1)}, u32[]{:S(2)}, u32[]{:S(2)}) collective-permute-start(bf16[32,4,16,512]{3,2,1,0:T(8,128)(2,1)S(1)} %get-tuple-element.18), channel_id=1, source_target_pairs={{0,4},{4,0},{8,12},{12,8},{16,20},{20,16},{24,28},{28,24},{32,36},... | collective-permute-start | bytes 6291464 | tf_op jit(solution)/shard_map/ppermute | solution.py:454

commit v6 on v5

--- a/solution.py
+++ b/solution.py
@@ -201,7 +201,7 @@
     )(reach, *qs, *tables, *more)
 
 
-def home_kernel(recv_ref, ids_ref, gate_ref, att_ref, msg_ref, mat_ref):
+def home_kernel(recv_ref, ids_ref, att_ref, msg_ref):
     blocks, tok, _ = recv_ref.shape
     heads = att_ref.shape[1] // HD
     logs = []
@@ -235,7 +235,6 @@
             for y in range(msg_ref.shape[1]):
                 for x in range(msg_ref.shape[3]):
                     msg_ref[e, y, c, x] = part
-    gate_matrix(ids_ref, gate_ref, mat_ref, msg_ref.shape[1] * msg_ref.shape[3])
 
 
 def gate_matrix(ids_ref, gate_ref, mat_ref, copies):
@@ -261,19 +260,18 @@
     mat_ref[pl.ds(tok, tok), :] = (gate - high.astype(F32)).astype(BF)
 
 
-def home(recv, ids, gates, tp):
+def home(recv, ids, tp):
     tok, width = recv.shape[1], recv.shape[2] - 128
     return pl.pallas_call(
         home_kernel,
         out_shape=(
             jax.ShapeDtypeStruct((tok, width), BF),
             jax.ShapeDtypeStruct((E, 2, 2, tp, CAP, width // 2), BF),
-            jax.ShapeDtypeStruct((2 * tok, E * 2 * tp * CAP), BF),
         ),
-        in_specs=[VM] * 3,
-        out_specs=(VM, VM, VM),
+        in_specs=[VM] * 2,
+        out_specs=(VM, VM),
         compiler_params=pltpu.CompilerParams(vmem_limit_bytes=24 * MIB),
-    )(recv, ids.T, gates.T)
+    )(recv, ids.T)
 
 
 def columns(x, side, half):
@@ -382,9 +380,10 @@
     )(other, gain, up_rows, down_columns, total, square)
 
 
-def down_kernel(hidden_ref, down_ref, out_ref, d_buf, sems):
+def down_kernel(hidden_ref, down_ref, ids_ref, gate_ref, out_ref, mat_ref, d_buf, sems):
     seqs, tp, cap, half = out_ref.shape
     copies = start_columns(down_ref, d_buf, this_core(), sems)
+    gate_matrix(ids_ref, gate_ref, mat_ref, 2 * tp)
     hidden = hidden_ref[...]
     for copy in copies:
         copy.wait()
@@ -392,17 +391,20 @@
         out_ref[:, x] = jnp.dot(hidden, d_buf[x], preferred_element_type=F32).reshape(seqs, cap, half)
 
 
-def down_project(hidden, w_down, shape):
+def down_project(hidden, w_down, ids, gates, shape):
     tp, half, hid = shape[1], shape[3], hidden.shape[1]
     return pl.pallas_call(
         down_kernel,
-        out_shape=jax.ShapeDtypeStruct(shape, F32),
-        in_specs=[VM, HBM],
-        out_specs=VM,
+        out_shape=(
+            jax.ShapeDtypeStruct(shape, F32),
+            jax.ShapeDtypeStruct((2 * ids.shape[0], E * 2 * tp * CAP), BF),
+        ),
+        in_specs=[VM, HBM, VM, VM],
+        out_specs=(VM, VM),
         scratch_shapes=[pltpu.VMEM((tp, hid, half), BF), pltpu.SemaphoreType.DMA((tp,))],
         compiler_params=pltpu.CompilerParams(vmem_limit_bytes=24 * MIB),
         cost_estimate=pl.CostEstimate(flops=2 * hidden.shape[0] * tp * half * hid, bytes_accessed=5 * MIB, transcendentals=0),
-    )(hidden, w_down)
+    )(hidden, w_down, ids.T, gates.T)
 
 
 def join_kernel(keep_ref, partner_ref, out_ref):
@@ -476,7 +478,7 @@
     arrived = lax.all_to_all(
         outs.reshape(chips, tok, outs.shape[1]), "seq", 0, 0, axis_index_groups=same_core, tiled=True
     )
-    attended, message, matrix = home(arrived, expert_ids, gate_weights, tp)
+    attended, message = home(arrived, expert_ids, tp)
     half = width // 2
     rows = lax.all_to_all(
         message.reshape(seqs * tp, CAP, half), ("seq", "tp"), 0, 0, tiled=True
@@ -486,7 +488,8 @@
     down_rows = pltpu.with_memory_space_constraint(w_down[0], pltpu.HBM)
     total, square, next_up, next_down = up_first(rows, gain, up_rows, down_rows)
     hidden, send = up_second(swapped(rows), gain, next_up, next_down, total, square)
-    result = join(down_project(hidden, down_rows, send.shape), swapped(send))
+    kept, matrix = down_project(hidden, down_rows, expert_ids, gate_weights, send.shape)
+    result = join(kept, swapped(send))
     returned = lax.all_to_all(
         result.reshape(seqs * tp, CAP, half), ("seq", "tp"), 0, 0, tiled=True
     ).reshape(E, 2, 2, tp, CAP, half)

time: 172 us -> 172 us (level)
  no operation moved by 1% of the time
where the time goes in v6:
time: 172 us; the launch traced here: 171 us
  blocking collectives  93.4 us (54%)
  Pallas kernels  60 us (35%)
  starting transfers between devices  13.6 us (8%)
  local copies, waits for them, and re-layouts  3.15 us (2%)
    pallas_call x2, Pallas kernels, attention(): pl.pallas_call(functools.partial(attn_kernel, parts=len(qs), earlier=prev...  44 us
    all_to_all x1, blocking collectives, per_device(): lax.all_to_all(message.reshape(seqs * tp, CAP, half), ('seq', 'tp'), 0, 0...  38 us
    all_to_all x1, blocking collectives, per_device(): lax.all_to_all(result.reshape(seqs * tp, CAP, half), ('seq', 'tp'), 0, 0,...  34.2 us
    all_to_all x1, blocking collectives, per_device(): lax.all_to_all(outs.reshape(chips, tok, outs.shape[1]), 'seq', 0, 0, axis...  21.2 us
    ppermute x6, starting transfers between devices, moved(): return lax.ppermute(value, 'seq', pairs)  10.2 us
    pallas_call x1, Pallas kernels, up_first(): pl.pallas_call(up_first_kernel, out_shape=(jax.ShapeDtypeStruct((rows, hi...  5.35 us
    pallas_call x1, Pallas kernels, up_second(): pl.pallas_call(up_second_kernel, out_shape=(jax.ShapeDtypeStruct(total.sh...  4.04 us
    pallas_call x1, Pallas kernels, down_project(): pl.pallas_call(down_kernel, out_shape=(jax.ShapeDtypeStruct(shape, F32),...  3.71 us
  transfers between devices with their start and end apart: 11, of which 1 were waited for; matrix products, arithmetic and copies ran while one was open for 2% of the time, Pallas kernels for 13%

profile of v6, /device:TPU:1, one launch (start us, length us, event | category | flops | bytes accessed | tf_op | source)
XLA Modules:
  0.0 171.4 jit_solution(13976046486302239954)
XLA Ops:
  0.6 1.5 collective-permute-start.6
  2.1 0.1 collective-permute-start.7
  2.2 3.0 %collective-permute-start.1 = (bf16[32,1024]{1,0:T(8,128)(2,1)}, bf16[32,1024]{1,0:T(8,128)(2,1)S(1)}, u32[]{:S(2)}, u32[]{:S(2)}) collective-permute-start(bf16[32,1024]{1,0:T(8,128)(2,1)} %param.11), channel_id=1, source_target_pairs={{0,16},{4,20},{8,24},{12,28},{16,0},{20,4},{24,8},{28,12},{32,48},... | collective-permute-start | bytes 196616 | tf_op jit(solution)/shard_map/ppermute | solution.py:463
  5.2 0.8 collective-permute-start
  6.0 0.7 collective-permute-start.2
  6.7 0.8 reshape.28
  7.5 0.1 fusion.1
  7.6 0.1 reshape.29
  7.6 0.7 constant_dynamic-update-slice_fusion.5
  8.3 0.8 constant_dynamic-update-slice_fusion.3
  9.2 0.7 constant_dynamic-update-slice_fusion.4.refs_6_.refs_8_
  9.9 0.0 collective-permute-done
  9.9 1.3 collective-permute-start.8
  11.2 0.0 collective-permute-done.1
  11.2 0.0 collective-permute-done.2
  11.2 1.7 collective-permute-start.5
  12.9 3.3 %collective-permute-start.4 = (bf16[128,1024]{1,0:T(8,128)(2,1)S(1)}, bf16[128,1024]{1,0:T(8,128)(2,1)S(1)}, u32[]{:S(2)}, u32[]{:S(2)}) collective-permute-start(bf16[128,1024]{1,0:T(8,128)(2,1)S(1)} %constant_dynamic-update-slice_fusion.refs_1_), channel_id=1, source_target_pairs={{0,64},{4,68},{8,72},{12,76},{16,80},{20,84},{24,88},{28,92},{32,9... | collective-permute-start | bytes 786440 | tf_op jit(solution)/shard_map/ppermute | solution.py:463
  16.2 0.0 collective-permute-done.8.refs_7_.refs_9_
  16.2 0.7 collective-permute-start.3
  16.9 0.0 collective-permute-done.6.refs_4_.refs_6_
  17.0 0.0 collective-permute-done.7.refs_5_.refs_7_
  17.0 12.5 %shard_map.122.refs_10_ = bf16[128,1152]{1,0:T(8,128)(2,1)S(1)} custom-call(s32[1,128]{1,0:T(1,128)S(1)} %slice.9.refs_0_, bf16[128,1024]{1,0:T(8,128)(2,1)S(1)} %constant_dynamic-update-slice_fusion.refs_1_, bf16[4096,128]{1,0:T(8,128)(2,1)} %refs_4_.1, bf16[4096,128]{1,0:T(8,128)(2,1)} %refs_5_.1, ...), custom_call_target="tpu_custom_call" | custom-call | flops 4362076160 | bytes 8388608 | tf_op jit(solution)/shard_map/pallas_call | solution.py:181
  29.5 0.0 collective-permute-done.5.refs_3_
  29.5 0.0 collective-permute-done.4.refs_2_
  29.5 0.0 collective-permute-done.3.refs_1_
  29.5 31.4 %shard_map.123 = bf16[512,1152]{1,0:T(8,128)(2,1)S(1)} custom-call(s32[1,384]{1,0:T(1,128)S(1)} %slice.8.refs_0_, bf16[128,1024]{1,0:T(8,128)(2,1)S(1)} %collective-permute-done.3.refs_1_, bf16[128,1024]{1,0:T(8,128)(2,1)S(1)} %collective-permute-done.4.refs_2_, bf16[128,1024]{1,0:T(8,128)(2,1)S(1)} %collective-permute-done.5.refs_3_, ...), custom_call_target="tpu_custom_call" | custom-call | flops 13086228480 | bytes 8388608 | tf_op jit(solution)/shard_map/pallas_call | solution.py:181
  61.0 0.0 copy-start.1
  61.0 21.2 %all_to_all.15.recv_ref = bf16[16,32,1152]{2,1,0:T(8,128)(2,1)S(1)} all-to-all(bf16[16,32,1152]{2,1,0:T(8,128)(2,1)S(1)} %bitcast.16), channel_id=1, replica_groups={{0,8,16,24,32,40,48,56,64,72,80,88,96,104,112,120},{4,12,20,28,36,44,52..., dimensions={0} | all-to-all | bytes 2359296 | tf_op jit(solution)/shard_map/all_to_all | solution.py:478
  82.2 0.0 copy-done.1
  82.2 1.5 shard_map.124
  83.7 0.0 copy-start
  83.7 38.0 %all_to_all.16 = bf16[128,16,512]{2,1,0:T(8,128)(2,1)S(1)} all-to-all(bf16[128,16,512]{2,1,0:T(8,128)(2,1)S(1)} %bitcast.15), channel_id=1, replica_groups=mesh['seq'=32,'tp'=4] {'seq','tp'}, dimensions={0} | all-to-all | bytes 4194304 | tf_op jit(solution)/shard_map/all_to_all | solution.py:483
  121.7 0.4 collective-permute-start.9
  122.1 0.0 copy-done
  122.1 5.4 %shard_map.125 = (f32[512,768]{1,0:T(8,128)S(1)}, f32[512,128]{1,0:T(8,128)S(1)}, bf16[4,512,768]{2,1,0:T(8,128)(2,1)S(1)}, bf16[4,768,512]{2,1,0:T(8,128)(2,1)S(1)}) custom-call(bf16[32,4,16,512]{3,2,1,0:T(8,128)(2,1)S(1)} %bitcast.13, f32[1,4096]{1,0:T(1,128)S(1)} %bitcast.17, bf16[4096,768]{1,0:T(8,128)(2,1)} %bitcast.24, bf16[768,4096]{1,0:T(8,128)(2,1)} %bitcast.22), custom_call_target="tpu_custom_call" | custom-call | flops 1610612736 | bytes 5242880 | tf_op jit(solution)/shard_map/pallas_call | solution.py:329
  127.4 0.0 collective-permute-done.9.other_ref
  127.5 0.0 copy-start.2
  127.5 4.0 %shard_map.126 = (bf16[512,768]{1,0:T(8,128)(2,1)S(1)}, bf16[32,4,16,512]{3,2,1,0:T(8,128)(2,1)S(1)}) custom-call(bf16[32,4,16,512]{3,2,1,0:T(8,128)(2,1)S(1)} %collective-permute-done.9.other_ref, f32[1,4096]{1,0:T(1,128)S(1)} %bitcast.18, bf16[4,512,768]{2,1,0:T(8,128)(2,1)S(1)} %get-tuple-element.14.up_ref, ...), custom_call_target="tpu_custom_call" | custom-call | tf_op jit(solution)/shard_map/pallas_call | solution.py:371
  131.5 0.2 collective-permute-start.10
  131.7 0.0 copy-done.2
  131.7 3.7 %shard_map.127 = (f32[32,4,16,512]{3,2,1,0:T(8,128)S(1)}, bf16[64,1024]{1,0:T(8,128)(2,1)S(1)}) custom-call(bf16[512,768]{1,0:T(8,128)(2,1)S(1)} %get-tuple-element.18.hidden_ref, bf16[768,4096]{1,0:T(8,128)(2,1)} %bitcast.23, s32[2,32]{1,0:T(2,128)S(1)} %bitcast.20, f32[2,32]{1,0:T(2,128)S(1)} %bitcast.21), custom_call_target="tpu_custom_call" | custom-call | flops 1610612736 | bytes 5242880 | tf_op jit(solution)/shard_map/pallas_call | solution.py:396
  135.4 0.3 collective-permute-done.10.partner_ref
  135.7 0.3 shard_map.128
  136.1 34.2 %all_to_all.17 = bf16[128,16,512]{2,1,0:T(8,128)(2,1)S(1)} all-to-all(bf16[128,16,512]{2,1,0:T(8,128)(2,1)S(1)} %bitcast.14), channel_id=1, replica_groups=mesh['seq'=32,'tp'=4] {'seq','tp'}, dimensions={0} | all-to-all | bytes 4194304 | tf_op jit(solution)/shard_map/all_to_all | solution.py:493
  170.3 1.1 shard_map.129
  (6 shorter events, 0.0 us)
Async XLA Ops:
  0.6 16.3 %collective-permute-start.6 = (bf16[4096,128]{1,0:T(8,128)(2,1)}, bf16[4096,128]{1,0:T(8,128)(2,1)S(1)}, u32[]{:S(2)}, u32[]{:S(2)}) collective-permute-start(bf16[4096,128]{1,0:T(8,128)(2,1)} %refs_4_.1), channel_id=1, source_target_pairs={{0,4},{4,0},{8,12},{12,8},{16,20},{20,16},{24,28},{28,24},{32,36},... | collective-permute-start | bytes 3145736 | tf_op jit(solution)/shard_map/ppermute | solution.py:456
  2.1 14.8 %collective-permute-start.7 = (bf16[4096,128]{1,0:T(8,128)(2,1)}, bf16[4096,128]{1,0:T(8,128)(2,1)S(1)}, u32[]{:S(2)}, u32[]{:S(2)}) collective-permute-start(bf16[4096,128]{1,0:T(8,128)(2,1)} %refs_5_.1), channel_id=1, source_target_pairs={{0,4},{4,0},{8,12},{12,8},{16,20},{20,16},{24,28},{28,24},{32,36},... | collective-permute-start | bytes 3145736 | tf_op jit(solution)/shard_map/ppermute | solution.py:456
  2.2 8.9 %collective-permute-start.1 = (bf16[32,1024]{1,0:T(8,128)(2,1)}, bf16[32,1024]{1,0:T(8,128)(2,1)S(1)}, u32[]{:S(2)}, u32[]{:S(2)}) collective-permute-start(bf16[32,1024]{1,0:T(8,128)(2,1)} %param.11), channel_id=1, source_target_pairs={{0,16},{4,20},{8,24},{12,28},{16,0},{20,4},{24,8},{28,12},{32,48},... | collective-permute-start | bytes 196616 | tf_op jit(solution)/shard_map/ppermute | solution.py:463
  5.2 4.7 %collective-permute-start = (bf16[32,1024]{1,0:T(8,128)(2,1)}, bf16[32,1024]{1,0:T(8,128)(2,1)S(1)}, u32[]{:S(2)}, u32[]{:S(2)}) collective-permute-start(bf16[32,1024]{1,0:T(8,128)(2,1)} %param.11), channel_id=1, source_target_pairs={{0,24},{4,28},{8,0},{12,4},{16,8},{20,12},{24,16},{28,20},{32,56},... | collective-permute-start | bytes 196616 | tf_op jit(solution)/shard_map/ppermute | solution.py:463
  6.0 5.2 %collective-permute-start.2 = (bf16[32,1024]{1,0:T(8,128)(2,1)}, bf16[32,1024]{1,0:T(8,128)(2,1)S(1)}, u32[]{:S(2)}, u32[]{:S(2)}) collective-permute-start(bf16[32,1024]{1,0:T(8,128)(2,1)} %param.11), channel_id=1, source_target_pairs={{0,8},{4,12},{8,16},{12,20},{16,24},{20,28},{24,0},{28,4},{32,40},... | collective-permute-start | bytes 196616 | tf_op jit(solution)/shard_map/ppermute | solution.py:463
  9.9 6.3 %collective-permute-start.8 = (bf16[64,128]{1,0:T(8,128)(2,1)S(1)}, bf16[64,128]{1,0:T(8,128)(2,1)S(1)}, u32[]{:S(2)}, u32[]{:S(2)}) collective-permute-start(bf16[64,128]{1,0:T(8,128)(2,1)S(1)} %constant_dynamic-update-slice_fusion.4.refs_6_.refs_8_), channel_id=1, source_target_pairs={{0,4},{4,0},{8,12},{12,8},{16,20},{20,16},{24,28},{28,24},{32,36},... | collective-permute-start | bytes 49160 | tf_op jit(solution)/shard_map/ppermute | solution.py:456
  11.2 18.3 %collective-permute-start.5 = (bf16[128,1024]{1,0:T(8,128)(2,1)S(1)}, bf16[128,1024]{1,0:T(8,128)(2,1)S(1)}, u32[]{:S(2)}, u32[]{:S(2)}) collective-permute-start(bf16[128,1024]{1,0:T(8,128)(2,1)S(1)} %constant_dynamic-update-slice_fusion.refs_1_), channel_id=1, source_target_pairs={{0,32},{4,36},{8,40},{12,44},{16,48},{20,52},{24,56},{28,60},{32,6... | collective-permute-start | bytes 786440 | tf_op jit(solution)/shard_map/ppermute | solution.py:463
  12.9 16.6 %collective-permute-start.4 = (bf16[128,1024]{1,0:T(8,128)(2,1)S(1)}, bf16[128,1024]{1,0:T(8,128)(2,1)S(1)}, u32[]{:S(2)}, u32[]{:S(2)}) collective-permute-start(bf16[128,1024]{1,0:T(8,128)(2,1)S(1)} %constant_dynamic-update-slice_fusion.refs_1_), channel_id=1, source_target_pairs={{0,64},{4,68},{8,72},{12,76},{16,80},{20,84},{24,88},{28,92},{32,9... | collective-permute-start | bytes 786440 | tf_op jit(solution)/shard_map/ppermute | solution.py:463
  16.2 13.3 %collective-permute-start.3 = (bf16[128,1024]{1,0:T(8,128)(2,1)S(1)}, bf16[128,1024]{1,0:T(8,128)(2,1)S(1)}, u32[]{:S(2)}, u32[]{:S(2)}) collective-permute-start(bf16[128,1024]{1,0:T(8,128)(2,1)S(1)} %constant_dynamic-update-slice_fusion.refs_1_), channel_id=1, source_target_pairs={{0,96},{4,100},{8,104},{12,108},{16,112},{20,116},{24,120},{28,124... | collective-permute-start | bytes 786440 | tf_op jit(solution)/shard_map/ppermute | solution.py:463
  61.0 21.2 %copy-start.1 = (s32[32,2]{0,1:T(2,128)S(1)}, s32[32,2]{0,1:T(2,128)}, u32[]{:S(2)}) copy-start(s32[32,2]{0,1:T(2,128)} %param.19) | copy-start | bytes 772
  83.7 38.4 %copy-start = (f32[4096]{0:T(1024)S(1)}, f32[4096]{0:T(1024)}, u32[]{:S(2)}) copy-start(f32[4096]{0:T(1024)} %param.17) | copy-start | bytes 49156
  121.7 5.8 %collective-permute-start.9 = (bf16[32,4,16,512]{3,2,1,0:T(8,128)(2,1)S(1)}, bf16[32,4,16,512]{3,2,1,0:T(8,128)(2,1)S(1)}, u32[]{:S(2)}, u32[]{:S(2)}) collective-permute-start(bf16[32,4,16,512]{3,2,1,0:T(8,128)(2,1)S(1)} %bitcast.12), channel_id=1, source_target_pairs={{0,4},{4,0},{8,12},{12,8},{16,20},{20,16},{24,28},{28,24},{32,36},... | collective-permute-start | bytes 6291464 | tf_op jit(solution)/shard_map/ppermute | solution.py:456
  127.5 4.3 %copy-start.2 = (f32[32,2]{0,1:T(2,128)S(1)}, f32[32,2]{0,1:T(2,128)}, u32[]{:S(2)}) copy-start(f32[32,2]{0,1:T(2,128)} %param.18) | copy-start | bytes 772
  131.5 4.2 %collective-permute-start.10 = (bf16[32,4,16,512]{3,2,1,0:T(8,128)(2,1)S(1)}, bf16[32,4,16,512]{3,2,1,0:T(8,128)(2,1)S(1)}, u32[]{:S(2)}, u32[]{:S(2)}) collective-permute-start(bf16[32,4,16,512]{3,2,1,0:T(8,128)(2,1)S(1)} %get-tuple-element.20), channel_id=1, source_target_pairs={{0,4},{4,0},{8,12},{12,8},{16,20},{20,16},{24,28},{28,24},{32,36},... | collective-permute-start | bytes 6291464 | tf_op jit(solution)/shard_map/ppermute | solution.py:456
